TPU v7x, 256 devices: a whole 4x4x8 slice. The times are simulated.
256 devices in a mesh: dp: 4 (over z_lo), fsdp: 64 (over y, x, z_hi, core).
Axes of the slice: x: 4, y: 4, z: 8 (z_hi: 2, z_lo: 4; z = z_hi * 4 + z_lo), core: 2. Of those that a mesh axis runs over, the one named last changes fastest.
Arguments:
- normed: bfloat16 [65536, 4608], P(('dp', 'fsdp')), may hold values from -6 to 6
- key_weight: bfloat16 [4608, 1024], P('fsdp'), may hold values from -0.09375 to 0.09375
- key_grad: bfloat16 [65536, 1024], P(('dp', 'fsdp')), may hold values from -6 to 6
Outputs:
- keys: bfloat16 [65536, 1024], P(('dp', 'fsdp'))
- input_grad: bfloat16 [65536, 4608], P(('dp', 'fsdp'))
- weight_grad: float32 [4608, 1024], P('fsdp')
All inputs are finite; a program needn't handle non-finite values.
Results may differ from a plain program's by a relative error of at most 0.004.
Values may be sent and summed in bfloat16 or wider, within the bound.
No kernel may reach another device: no remote copies, remote signals or barrier semaphores. Data moves between devices by JAX's collectives and lax.ppermute only.
A program may use at most 128 MiB of HBM per device.

v0:
```python
import jax
import jax.numpy as jnp
from jax import lax
from jax.sharding import PartitionSpec as P

GROUP = 128
TAIL = 32


def restore(normed, block):
    rows, width = normed.shape
    values = normed.astype(jnp.float32).reshape(rows, width // GROUP, GROUP)
    scale = jnp.max(jnp.abs(values), axis=-1, keepdims=True)
    code = (
        (2.0 * values >= -scale).astype(jnp.float32)
        + (values >= 0.0).astype(jnp.float32)
        + (2.0 * values >= scale).astype(jnp.float32)
    )
    approx = ((code - 1.5) * 0.5 * scale).reshape(rows, width).astype(jnp.bfloat16)
    position = jnp.arange(rows, dtype=jnp.int32) % block
    exact = (position >= block - TAIL)[:, None]
    return jnp.where(exact, normed, approx)


def local(normed, key_weight, key_grad):
    whole_weight = lax.all_gather(key_weight, "fsdp", axis=0, tiled=True)
    keys = jnp.dot(normed, whole_weight, preferred_element_type=jnp.float32).astype(jnp.bfloat16)
    input_grad = lax.dot_general(
        key_grad, whole_weight, (((1,), (1,)), ((), ())), preferred_element_type=jnp.float32
    ).astype(jnp.bfloat16)
    restored = restore(normed, normed.shape[0])
    shard_rows = lax.psum_scatter(
        lax.dot_general(
            restored, key_grad, (((0,), (0,)), ((), ())), preferred_element_type=jnp.float32
        ),
        "fsdp",
        scatter_dimension=0,
        tiled=True,
    )
    weight_grad = lax.psum(shard_rows, "dp")
    return (keys, input_grad, weight_grad)


def solution(mesh):
    placed = (P(("dp", "fsdp"), None), P("fsdp", None), P(("dp", "fsdp"), None))
    return jax.shard_map(
        local,
        mesh=mesh,
        in_specs=placed,
        out_specs=(P(("dp", "fsdp"), None), P(("dp", "fsdp"), None), P("fsdp", None)),
        check_vma=False,
    )
```

profile of v0, /device:TPU:31, one launch (start us, length us, event | category | flops | bytes accessed | tf_op | source)
XLA Modules:
  0.0 461.0 jit_solution(8297228253402386917)
XLA Ops:
  7.2 0.0 copy-start
  7.2 0.0 all-gather.2.cloned.1.call-start
  7.2 0.7 all-gather.2.cloned.1.call-update
  7.9 0.0 reduce-scatter.2.cloned.1.call-start
  8.0 2.8 copy.7
  10.8 2.5 convert_abs_fusion
  13.3 2.8 reduce_max.9
  16.2 2.1 fusion.3
  18.3 0.0 copy-done
  18.3 7.9 %fusion.6 = f32[4608,1024]{1,0:T(8,128)} fusion(bf16[256,4608]{0,1:T(8,128)(2,1)S(1)} %fusion.3, bf16[256,1024]{1,0:T(8,128)(2,1)S(1)} %copy-done), kind=kOutput, calls=%fused_computation.14 | convolution fusion | flops 2415919104 | bytes 21757952 | tf_op jit(solution)/shard_map/dot_general | solution.py:33
  26.2 0.0 copy-start.1
  26.2 0.0 reduce-scatter.2.cloned.1.call-update
  26.2 0.0 all-reduce.2.cloned.1.call-start
  26.3 104.2 %all-gather.2.cloned.1.call-done = bf16[4608,1024]{1,0:T(8,128)(2,1)} async-done(((bf16[72,1024]{1,0:T(8,128)(2,1)}), bf16[4608,1024]{1,0:T(8,128)(2,1)}) %all-gather.2.cloned.1.call-update) | async-done | bytes 9437200 | tf_op jit(solution)/shard_map/all_gather | solution.py:26
  130.5 0.0 copy-done.1
  130.5 7.1 %convolution_convert_fusion.1 = bf16[256,1024]{1,0:T(8,128)(2,1)} fusion(bf16[256,4608]{1,0:T(8,128)(2,1)S(1)} %copy-done.1, bf16[4608,1024]{1,0:T(8,128)(2,1)} %all-gather.2.cloned.1.call-done), kind=kOutput, calls=%fused_computation.9 | convolution fusion | flops 2416181248 | bytes 12320768 | tf_op jit(solution)/shard_map/dot_general | solution.py:27
  137.6 266.5 %reduce-scatter.2.cloned.1.call-done = f32[72,1024]{1,0:T(8,128)} async-done(((f32[4608,1024]{1,0:T(8,128)}), f32[72,1024]{1,0:T(8,128)}) %reduce-scatter.2.cloned.1.call-update) | async-done | bytes 294928 | tf_op jit(solution)/shard_map/reduce_scatter | solution.py:32
  404.1 0.0 all-reduce.2.cloned.1.call-update
  404.1 11.2 %convolution_convert_fusion = bf16[256,4608]{1,0:T(8,128)(2,1)} fusion(bf16[256,1024]{1,0:T(8,128)(2,1)S(1)} %copy-done, bf16[4608,1024]{1,0:T(8,128)(2,1)} %all-gather.2.cloned.1.call-done), kind=kOutput, calls=%fused_computation.3 | convolution fusion | flops 2417098752 | bytes 12320768 | tf_op jit(solution)/shard_map/dot_general | solution.py:28
  415.3 37.4 %all-reduce.2.cloned.1.call-done = f32[72,1024]{1,0:T(8,128)} async-done(((f32[72,1024]{1,0:T(8,128)}), f32[72,1024]{1,0:T(8,128)}) %all-reduce.2.cloned.1.call-update) | async-done | bytes 294928 | tf_op jit(solution)/shard_map/psum | solution.py:40
  452.8 1.7 copy.9
  (2 shorter events, 0.0 us)
Async XLA Ops:
  7.2 11.1 %copy-start = (bf16[256,1024]{1,0:T(8,128)(2,1)S(1)}, bf16[256,1024]{1,0:T(8,128)(2,1)}, u32[]{:S(2)}) copy-start(bf16[256,1024]{1,0:T(8,128)(2,1)} %param.5) | copy-start | bytes 1572868
  7.2 123.3 %all-gather.2.cloned.1.call-start = ((), (), s32[]{:S(2)}) async-start(), calls=%async_computation.1 | async-start | bytes 9584640 | tf_op jit(solution)/shard_map/all_gather | solution.py:26
  7.9 396.2 %reduce-scatter.2.cloned.1.call-start = ((), (), s32[]{:S(2)}) async-start(), calls=%async_computation.2 | async-start | bytes 19169280 | tf_op jit(solution)/shard_map/reduce_scatter | solution.py:32
  26.2 104.3 %copy-start.1 = (bf16[256,4608]{1,0:T(8,128)(2,1)S(1)}, bf16[256,4608]{1,0:T(8,128)(2,1)}, u32[]{:S(2)}) copy-start(bf16[256,4608]{1,0:T(8,128)(2,1)} %param.3) | copy-start | bytes 7077892
  26.2 426.5 %all-reduce.2.cloned.1.call-start = ((), (), s32[]{:S(2)}) async-start(), calls=%async_computation.3 | async-start | bytes 589824 | tf_op jit(solution)/shard_map/psum | solution.py:40
Sparse Core Ops, SparseCore 0:
  11.5 118.9 all-gather.1
  136.9 267.1 reduce-scatter.1
  406.9 45.7 all-reduce.1
where the time goes:
time: 464 us; the launch traced here: 461 us
  waiting for transfers between devices  409 us (88%)
  matrix products  26.2 us (6%)
  between operations  13.8 us (3%)
  other arithmetic  7.48 us (2%)
    reduce_scatter x1, waiting for transfers between devices, local(): lax.psum_scatter(lax.dot_general(restored, key_grad, (((0,), (0,)), ((),...  266 us
    all_gather x1, waiting for transfers between devices, local(): whole_weight = lax.all_gather(key_weight, 'fsdp', axis=0, tiled=True)  104 us
    psum x1, waiting for transfers between devices, local(): weight_grad = lax.psum(shard_rows, 'dp')  37.4 us
    dot_general x1, matrix products, local(): lax.dot_general(key_grad, whole_weight, (((1,), (1,)), ((), ())), preferr...  11.2 us
  transfers between devices with their start and end apart: 3, of which 3 were waited for; matrix products, arithmetic and copies ran while one was open for 8% of the time, Pallas kernels for 0%

commit v1 on v0

v1 whole, which is shorter than its diff:
```python
import jax
import jax.numpy as jnp
from jax import lax
from jax.experimental import pallas as pl
from jax.experimental.pallas import tpu as pltpu
from jax.sharding import Mesh, PartitionSpec as P

GROUP = 128
TAIL = 32
AXES = ("zl", "y", "x", "zh", "c")
SIZES = (4, 4, 4, 2, 2)
TOK = 256
D = 4608
KD = 1024
HALF = KD // 2
BLK = D // 16
VMEM_LIMIT = 48 * 1024 * 1024


def pairs(move):
    out = []
    for i in range(256):
        rest, at = i, {}
        for name, size in zip(reversed(AXES), reversed(SIZES)):
            at[name] = rest % size
            rest //= size
        to = move(dict(at))
        j = 0
        for name, size in zip(AXES, SIZES):
            j = j * size + to[name] % size
        out.append((i, j))
    return out


def send(value, move):
    return lax.ppermute(value, AXES, pairs(move))


def other_core(at):
    at["c"] ^= 1
    return at


def mirror(at):
    at["zh"] ^= 1
    at["zl"] = 3 - at["zl"]
    return at


def first_by(step):
    def move(at):
        at["x" if at["c"] == 0 else "y"] += step
        return at

    return move


def second_by(step):
    def move(at):
        at["y" if at["c"] == 0 else "x"] += step
        return at

    return move


def zl_by(step):
    def move(at):
        at["zl"] += step
        return at

    return move


def quantize_kernel(x_ref, out_ref):
    for g in range(x_ref.shape[1] // GROUP):
        v = x_ref[:, g * GROUP : (g + 1) * GROUP].astype(jnp.float32).T
        scale = jnp.max(jnp.abs(v), axis=0, keepdims=True)
        low = (0.25 * scale).astype(jnp.bfloat16).astype(jnp.float32)
        high = (0.75 * scale).astype(jnp.bfloat16).astype(jnp.float32)
        twice = v + v
        mag = jnp.where((twice >= scale) | (twice < -scale), high, low)
        r = jnp.where(v >= 0.0, mag, -mag)
        token = lax.broadcasted_iota(jnp.int32, r.shape, 1)
        r = jnp.where(token >= TOK - TAIL, v, r)
        out_ref[g * GROUP : (g + 1) * GROUP, :] = r.astype(jnp.bfloat16)


def quantize(normed):
    width = 4 * GROUP
    return pl.pallas_call(
        quantize_kernel,
        grid=(D // width,),
        in_specs=[pl.BlockSpec((TOK, width), lambda i: (0, i))],
        out_specs=pl.BlockSpec((width, TOK), lambda i: (i, 0)),
        out_shape=jax.ShapeDtypeStruct((D, TOK), jnp.bfloat16),
        compiler_params=pltpu.CompilerParams(vmem_limit_bytes=VMEM_LIMIT),
        cost_estimate=pl.CostEstimate(flops=0, bytes_accessed=4 * D * TOK, transcendentals=0),
    )(normed)


def partial_kernel(at_ref, mine_ref, theirs_ref, gmine_ref, gtheirs_ref, o0, o1, o2, o3, acc, sem):
    step = pl.program_id(0)
    rows = mine_ref.shape[0]
    total = jnp.dot(mine_ref[...], gmine_ref[...], preferred_element_type=jnp.float32)
    total += jnp.dot(theirs_ref[...], gtheirs_ref[...], preferred_element_type=jnp.float32)
    acc[pl.ds(pl.multiple_of(step * rows, rows), rows), :] = total.astype(jnp.bfloat16)

    @pl.when(step == pl.num_programs(0) - 1)
    def _():
        first, core = at_ref[0], at_ref[2]
        copies = []
        for j, out in enumerate((o0, o1, o2, o3)):
            to = lax.rem(first + j, 4)
            for i in range(4):
                block = jnp.where(core == 0, 4 * i + to, 4 * to + i)
                copy = pltpu.make_async_copy(
                    acc.at[pl.ds(pl.multiple_of(block * BLK, BLK), BLK), :], out.at[i], sem.at[j, i]
                )
                copy.start()
                copies.append(copy)
        for copy in copies:
            copy.wait()


def partial_blocks(at, mine, theirs, gmine, gtheirs):
    rows = 1152
    return pl.pallas_call(
        partial_kernel,
        grid_spec=pltpu.PrefetchScalarGridSpec(
            num_scalar_prefetch=1,
            grid=(D // rows,),
            in_specs=[
                pl.BlockSpec((rows, TOK), lambda i, at: (i, 0)),
                pl.BlockSpec((rows, TOK), lambda i, at: (i, 0)),
                pl.BlockSpec((TOK, HALF), lambda i, at: (0, 0)),
                pl.BlockSpec((TOK, HALF), lambda i, at: (0, 0)),
            ],
            out_specs=[pl.BlockSpec(memory_space=pl.ANY)] * 4,
            scratch_shapes=[pltpu.VMEM((D, HALF), jnp.bfloat16), pltpu.SemaphoreType.DMA((4, 4))],
        ),
        out_shape=[jax.ShapeDtypeStruct((4, BLK, HALF), jnp.bfloat16)] * 4,
        compiler_params=pltpu.CompilerParams(vmem_limit_bytes=VMEM_LIMIT),
        cost_estimate=pl.CostEstimate(flops=4 * D * HALF * TOK, bytes_accessed=10 * 2**20, transcendentals=0),
    )(at, mine, theirs, gmine, gtheirs)


def sum_kernel(at_ref, a, b, c, d, r0, r1, r2, r3):
    total = a[0].astype(jnp.float32) + b[0].astype(jnp.float32) + c[0].astype(jnp.float32) + d[0].astype(jnp.float32)
    total = total.astype(jnp.bfloat16)
    for j, r in enumerate((r0, r1, r2, r3)):

        @pl.when(pl.program_id(0) == j)
        def _():
            r[...] = total


def sum_blocks(at, blocks):
    spec = pl.BlockSpec((1, BLK, HALF), lambda j, at: (lax.rem(at[1] + j, 4), 0, 0))
    return pl.pallas_call(
        sum_kernel,
        grid_spec=pltpu.PrefetchScalarGridSpec(
            num_scalar_prefetch=1,
            grid=(4,),
            in_specs=[spec] * 4,
            out_specs=[pl.BlockSpec((BLK, HALF), lambda j, at: (0, 0))] * 4,
        ),
        out_shape=[jax.ShapeDtypeStruct((BLK, HALF), jnp.bfloat16)] * 4,
        compiler_params=pltpu.CompilerParams(vmem_limit_bytes=VMEM_LIMIT),
        cost_estimate=pl.CostEstimate(flops=0, bytes_accessed=6 * 2**20, transcendentals=0),
    )(at, *blocks)


def product_kernel(at_ref, x_ref, g_ref, *rest):
    parts, (keys_ref, grad_ref, w, sem) = rest[:8], rest[8:]
    first, second, core = at_ref[0], at_ref[1], at_ref[2]
    copies = []
    for own in range(2):
        side = core if own == 0 else 1 - core
        ahead, behind = (first, second) if own == 0 else (second, first)
        for k in range(4):
            for j in range(4):
                f, s = lax.rem(ahead + j, 4), lax.rem(behind + k, 4)
                block = jnp.where(side == 0, 4 * s + f, 4 * f + s)
                copy = pltpu.make_async_copy(
                    parts[4 * own + k].at[j],
                    w.at[pl.ds(pl.multiple_of(block * BLK, BLK), BLK), pl.ds(pl.multiple_of(side * HALF, HALF), HALF)],
                    sem.at[own, k, j],
                )
                copy.start()
                copies.append(copy)
    for copy in copies:
        copy.wait()
    rows = 1152
    total = jnp.zeros((TOK, KD), jnp.float32)
    for i in range(D // rows):
        chunk = slice(i * rows, (i + 1) * rows)
        total += jnp.dot(x_ref[:, chunk], w[chunk, :], preferred_element_type=jnp.float32)
        grad_ref[:, chunk] = lax.dot_general(
            g_ref[...], w[chunk, :], (((1,), (1,)), ((), ())), preferred_element_type=jnp.float32
        ).astype(jnp.bfloat16)
    keys_ref[...] = total.astype(jnp.bfloat16)


def products(at, normed, key_grad, parts):
    vmem = pl.BlockSpec(memory_space=pltpu.VMEM)
    return pl.pallas_call(
        product_kernel,
        in_specs=[pl.BlockSpec(memory_space=pltpu.SMEM), vmem, vmem] + [pl.BlockSpec(memory_space=pl.ANY)] * 8,
        out_specs=[vmem, vmem],
        out_shape=[
            jax.ShapeDtypeStruct((TOK, KD), jnp.bfloat16),
            jax.ShapeDtypeStruct((TOK, D), jnp.bfloat16),
        ],
        scratch_shapes=[pltpu.VMEM((D, KD), jnp.bfloat16), pltpu.SemaphoreType.DMA((2, 4, 4))],
        compiler_params=pltpu.CompilerParams(vmem_limit_bytes=VMEM_LIMIT),
        cost_estimate=pl.CostEstimate(flops=4 * D * KD * TOK, bytes_accessed=16 * 2**20, transcendentals=0),
    )(at, normed, key_grad, *parts)


def local(normed, key_weight, key_grad):
    zl, y, x, zh, c = (lax.axis_index(name) for name in AXES)
    first, second = jnp.where(c == 0, x, y), jnp.where(c == 0, y, x)
    at = jnp.stack([first, second, c]).astype(jnp.int32)

    def half(a, which):
        return lax.dynamic_slice_in_dim(a, which * HALF, HALF, axis=1)

    w_mine, w_theirs = half(key_weight, c), half(key_weight, 1 - c)
    w_core = send(w_theirs, other_core)
    w_mirror = send(w_mine, mirror)
    w_both = send(w_theirs, lambda at: other_core(mirror(at)))
    quads = jnp.stack([w_mine, w_core, w_mirror, w_both]).reshape(2, 2, 72, HALF)
    quads = jnp.where(c == 0, quads, quads[:, ::-1])
    quads = jnp.where(zh == 0, quads, quads[::-1])
    block = quads.reshape(BLK, HALF)

    mine = quantize(normed)
    theirs = send(mine, other_core)
    g_theirs = send(half(key_grad, 1 - c), other_core)
    out = partial_blocks(at, mine, theirs, half(key_grad, c), g_theirs)

    line = jnp.stack([block] + [send(block, first_by(-j)) for j in (1, 2, 3)])
    first_sums = [out[0]] + [send(out[j], first_by(j)) for j in (1, 2, 3)]
    planes = [line] + [send(line, second_by(-j)) for j in (1, 2, 3)]
    sums = sum_blocks(at, first_sums)
    column = [sums[0]] + [send(sums[j], second_by(j)) for j in (1, 2, 3)]
    total = sum(a.astype(jnp.float32) for a in column).astype(jnp.bfloat16)

    swapped = [send(p, other_core) for p in planes]
    keys, input_grad = products(at, normed, key_grad, planes + swapped)

    units = total.reshape(2, 2, 72, 4, 128).transpose(0, 3, 1, 2, 4).reshape(16, 72, 128)
    units = lax.all_to_all(units, ("zh", "zl", "c"), 0, 0, tiled=True)
    piece = jnp.sum(units.reshape(8, 2, 72, 128).astype(jnp.float32), axis=0)
    ring = jnp.stack([piece] + [send(piece, zl_by(-j)) for j in (1, 2, 3)])
    ring = lax.dynamic_slice_in_dim(jnp.concatenate([ring, ring]), (4 - zl) % 4, 4, axis=0)
    weight_grad = ring.transpose(2, 1, 0, 3).reshape(72, KD)
    return keys, input_grad, weight_grad


def solution(mesh):
    fine = Mesh(mesh.devices.reshape(SIZES), AXES)
    fsdp = ("y", "x", "zh", "c")
    tokens, rows = P(AXES, None), P(fsdp, None)
    return jax.shard_map(
        local,
        mesh=fine,
        in_specs=(tokens, rows, tokens),
        out_specs=(tokens, tokens, rows),
        check_vma=False,
    )
```

time: 464 us -> 160 us (0.34)
  waiting for transfers between devices: 409 us -> 68.5 us
  starting transfers between devices: 0.12 us -> 54.5 us
  matrix products: 26.2 us -> 0 us
  Pallas kernels: 0 us -> 24 us
  between operations: 13.8 us -> 0.9 us
  other arithmetic: 7.48 us -> 1.61 us
  local copies, waits for them, and re-layouts: 4.54 us -> 9.98 us
    reduce_scatter x1 -> x0, waiting for transfers between devices: 266 us -> none  [local(): lax.psum_scatter(lax.dot_general(restored, key_grad, (((0,), (0,)), ((),...]
    all_gather x1 -> x0, waiting for transfers between devices: 104 us -> none  [local(): whole_weight = lax.all_gather(key_weight, 'fsdp', axis=0, tiled=True)]
    ppermute x0 -> x24, waiting for transfers between devices: none -> 68.4 us  [send(): return lax.ppermute(value, AXES, pairs(move))]
    ppermute x0 -> x24, starting transfers between devices: none -> 39.7 us  [send(): return lax.ppermute(value, AXES, pairs(move))]
    psum x1 -> x0, waiting for transfers between devices: 37.4 us -> none  [local(): weight_grad = lax.psum(shard_rows, 'dp')]
    dot_general x3 -> x0, matrix products: 26.2 us -> none  [the longest x1 11.2 us: local(): lax.dot_general(key_grad, whole_weight, (((1,), (1,)), ((), ())), preferr...]
    pallas_call x0 -> x4, Pallas kernels: none -> 24 us  [the longest x1 12.7 us: products(): pl.pallas_call(product_kernel, in_specs=[pl.BlockSpec(memory_space=pltpu....]
    all_to_all x0 -> x1, starting transfers between devices: none -> 14.7 us  [local(): units = lax.all_to_all(units, ('zh', 'zl', 'c'), 0, 0, tiled=True)]
  transfers between devices with their start and end apart: 3 -> 25, of which waited for: 3 -> 9; matrix products, arithmetic and copies ran while one was open for 8% -> 2% of each run, Pallas kernels for 0% -> 9%
where the time goes in v1:
time: 160 us; the launch traced here: 159 us
  waiting for transfers between devices  68.5 us (43%)
  starting transfers between devices  54.5 us (34%)
  Pallas kernels  24 us (15%)
  local copies, waits for them, and re-layouts  9.98 us (6%)
  other arithmetic  1.61 us (1%)
    ppermute x24, waiting for transfers between devices, send(): return lax.ppermute(value, AXES, pairs(move))  68.4 us
    ppermute x24, starting transfers between devices, send(): return lax.ppermute(value, AXES, pairs(move))  39.7 us
    all_to_all x1, starting transfers between devices, local(): units = lax.all_to_all(units, ('zh', 'zl', 'c'), 0, 0, tiled=True)  14.7 us
    pallas_call x1, Pallas kernels, products(): pl.pallas_call(product_kernel, in_specs=[pl.BlockSpec(memory_space=pltpu....  12.7 us
    unnamed x31, local copies, waits for them, and re-layouts  7.42 us
    pallas_call x1, Pallas kernels, partial_blocks(): pl.pallas_call(partial_kernel, grid_spec=pltpu.PrefetchScalarGridSpec(num...  6.89 us
  transfers between devices with their start and end apart: 25, of which 9 were waited for; matrix products, arithmetic and copies ran while one was open for 2% of the time, Pallas kernels for 9%

profile of v1, /device:TPU:31, one launch (start us, length us, event | category | flops | bytes accessed | tf_op | source)
XLA Modules:
  0.0 159.4 jit_solution(13701666837907919799)
XLA Ops:
  0.6 1.7 %copy-done = bf16[256,4608]{1,0:T(8,128)(2,1)S(1)} copy-done((bf16[256,4608]{1,0:T(8,128)(2,1)S(1)}, bf16[256,4608]{1,0:T(8,128)(2,1)}, u32[]{:S(2)}) %copy-start) | copy-done | bytes 2359320
  2.3 2.7 %shard_map.59.mine_ref = bf16[4608,256]{1,0:T(8,128)(2,1)S(1)} custom-call(bf16[256,4608]{1,0:T(8,128)(2,1)S(1)} %copy-done), custom_call_target="tpu_custom_call" | custom-call | bytes 4718592 | tf_op jit(solution)/shard_map/pallas_call | solution.py:90
  6.9 3.5 %collective-permute-done.14.gtheirs_ref = bf16[256,512]{1,0:T(8,128)(2,1)S(1)} collective-permute-done((bf16[256,512]{1,0:T(8,128)(2,1)S(1)}, bf16[256,512]{1,0:T(8,128)(2,1)S(1)}, u32[]{:S(2)}, u32[]{:S(2)}) %collective-permute-start.14) | collective-permute-done | bytes 262176 | tf_op jit(solution)/shard_map/ppermute | solution.py:36
  11.1 0.9 copy-done.4
  12.0 0.9 copy-done.9
  13.0 6.9 %shard_map.60 = (bf16[4,288,512]{2,1,0:T(8,128)(2,1)S(1)}, bf16[4,288,512]{2,1,0:T(8,128)(2,1)}, bf16[4,288,512]{2,1,0:T(8,128)(2,1)S(1)}, bf16[4,288,512]{2,1,0:T(8,128)(2,1)S(1)}) custom-call(s32[3]{0:T(128)S(1)} %pad_add_fusion.at_ref, bf16[4608,256]{1,0:T(8,128)(2,1)} %copy-done.1, bf16[4608,256]{1,0:T(8,128)(2,1)} %collective-permute-done.13.theirs_ref, ...), custom_call_target="tpu_custom_call" | custom-call | flops 2415919104 | bytes 10485760 | tf_op jit(solution)/shard_map/pallas_call | solution.py:127
  19.9 1.0 copy-done.5
  20.9 1.0 copy-done.7
  21.9 0.9 collective-permute-start
  22.9 5.6 %collective-permute-start.1 = (bf16[72,512]{1,0:T(8,128)(2,1)S(1)}, bf16[72,512]{1,0:T(8,128)(2,1)S(1)}, u32[]{:S(2)}, u32[]{:S(2)}) collective-permute-start(bf16[72,512]{1,0:T(8,128)(2,1)S(1)} %get-tuple-element.25), channel_id=1, source_target_pairs={{0,194},{1,195},{2,192},{3,193},{4,198},{5,199},{6,196},{7,197},{8... | collective-permute-start | bytes 221192 | tf_op jit(solution)/shard_map/ppermute | solution.py:36
  28.5 4.0 %collective-permute-done.1 = bf16[72,512]{1,0:T(8,128)(2,1)S(1)} collective-permute-done((bf16[72,512]{1,0:T(8,128)(2,1)S(1)}, bf16[72,512]{1,0:T(8,128)(2,1)S(1)}, u32[]{:S(2)}, u32[]{:S(2)}) %collective-permute-start.1) | collective-permute-done | bytes 73760 | tf_op jit(solution)/shard_map/ppermute | solution.py:36
  32.6 2.1 %collective-permute-done.2 = bf16[72,512]{1,0:T(8,128)(2,1)S(1)} collective-permute-done((bf16[72,512]{1,0:T(8,128)(2,1)S(1)}, bf16[72,512]{1,0:T(8,128)(2,1)S(1)}, u32[]{:S(2)}, u32[]{:S(2)}) %collective-permute-start.2) | collective-permute-done | bytes 73760 | tf_op jit(solution)/shard_map/ppermute | solution.py:36
  35.5 1.0 collective-permute-start.4
  36.4 1.9 %collective-permute-start.5 = (bf16[288,512]{1,0:T(8,128)(2,1)S(1)}, bf16[288,512]{1,0:T(8,128)(2,1)S(1)}, u32[]{:S(2)}, u32[]{:S(2)}) collective-permute-start(bf16[288,512]{1,0:T(8,128)(2,1)S(1)} %bitcast.34), channel_id=1, source_target_pairs={{0,4},{1,17},{2,6},{3,19},{4,8},{5,21},{6,10},{7,23},{8,12},{9,25}... | collective-permute-start | bytes 884744 | tf_op jit(solution)/shard_map/ppermute | solution.py:36
  38.3 1.6 %collective-permute-start.16 = (bf16[4,288,512]{2,1,0:T(8,128)(2,1)}, bf16[4,288,512]{2,1,0:T(8,128)(2,1)S(1)}, u32[]{:S(2)}, u32[]{:S(2)}) collective-permute-start(bf16[4,288,512]{2,1,0:T(8,128)(2,1)} %copy-done.7), channel_id=1, source_target_pairs={{0,8},{1,33},{2,10},{3,35},{4,12},{5,37},{6,14},{7,39},{8,0},{9,41... | collective-permute-start | bytes 3538952 | tf_op jit(solution)/shard_map/ppermute | solution.py:36
  40.0 17.8 %collective-permute-done.3 = bf16[288,512]{1,0:T(8,128)(2,1)S(1)} collective-permute-done((bf16[288,512]{1,0:T(8,128)(2,1)S(1)}, bf16[288,512]{1,0:T(8,128)(2,1)S(1)}, u32[]{:S(2)}, u32[]{:S(2)}) %collective-permute-start.3) | collective-permute-done | bytes 294944 | tf_op jit(solution)/shard_map/ppermute | solution.py:36
  57.8 1.2 pad_maximum_fusion.rest_0_
  59.0 1.2 collective-permute-start.6
  60.2 1.2 collective-permute-start.7
  61.4 1.7 %collective-permute-start.8 = (bf16[4,288,512]{2,1,0:T(8,128)(2,1)}, bf16[4,288,512]{2,1,0:T(8,128)(2,1)}, u32[]{:S(2)}, u32[]{:S(2)}) collective-permute-start(bf16[4,288,512]{2,1,0:T(8,128)(2,1)} %pad_maximum_fusion.rest_0_), channel_id=1, source_target_pairs={{0,16},{1,5},{2,18},{3,7},{4,20},{5,9},{6,22},{7,11},{8,24},{9,13}... | collective-permute-start | bytes 3538952 | tf_op jit(solution)/shard_map/ppermute | solution.py:36
  63.1 20.2 %collective-permute-done.17.d = bf16[4,288,512]{2,1,0:T(8,128)(2,1)S(1)} collective-permute-done((bf16[4,288,512]{2,1,0:T(8,128)(2,1)S(1)}, bf16[4,288,512]{2,1,0:T(8,128)(2,1)S(1)}, u32[]{:S(2)}, u32[]{:S(2)}) %collective-permute-start.17) | collective-permute-done | bytes 1179680 | tf_op jit(solution)/shard_map/ppermute | solution.py:36
  83.3 1.7 %shard_map.61 = (bf16[288,512]{1,0:T(8,128)(2,1)S(1)}, bf16[288,512]{1,0:T(8,128)(2,1)S(1)}, bf16[288,512]{1,0:T(8,128)(2,1)S(1)}, bf16[288,512]{1,0:T(8,128)(2,1)S(1)}) custom-call(s32[3]{0:T(128)S(1)} %pad_add_fusion.at_ref, bf16[4,288,512]{2,1,0:T(8,128)(2,1)S(1)} %get-tuple-element.15.a, bf16[4,288,512]{2,1,0:T(8,128)(2,1)S(1)} %collective-permute-done.15.b, ...), custom_call_target="tpu_custom_call" | custom-call | bytes 6291456 | tf_op jit(solution)/shard_map/pallas_call | solution.py:159
  85.1 18.5 %collective-permute-start.9 = (bf16[4,288,512]{2,1,0:T(8,128)(2,1)}, bf16[4,288,512]{2,1,0:T(8,128)(2,1)S(1)}, u32[]{:S(2)}, u32[]{:S(2)}) collective-permute-start(bf16[4,288,512]{2,1,0:T(8,128)(2,1)} %pad_maximum_fusion.rest_0_), channel_id=1, source_target_pairs={{0,1},{1,0},{2,3},{3,2},{4,5},{5,4},{6,7},{7,6},{8,9},{9,8},{10,11... | collective-permute-start | bytes 3538952 | tf_op jit(solution)/shard_map/ppermute | solution.py:36
  104.2 7.1 %collective-permute-done.19 = bf16[288,512]{1,0:T(8,128)(2,1)S(1)} collective-permute-done((bf16[288,512]{1,0:T(8,128)(2,1)S(1)}, bf16[288,512]{1,0:T(8,128)(2,1)S(1)}, u32[]{:S(2)}, u32[]{:S(2)}) %collective-permute-start.19) | collective-permute-done | bytes 294944 | tf_op jit(solution)/shard_map/ppermute | solution.py:36
  111.3 6.8 %collective-permute-done.20 = bf16[288,512]{1,0:T(8,128)(2,1)S(1)} collective-permute-done((bf16[288,512]{1,0:T(8,128)(2,1)S(1)}, bf16[288,512]{1,0:T(8,128)(2,1)S(1)}, u32[]{:S(2)}, u32[]{:S(2)}) %collective-permute-start.20) | collective-permute-done | bytes 294944 | tf_op jit(solution)/shard_map/ppermute | solution.py:36
  119.1 14.7 %all-to-all-start = ((bf16[16,72,128]{2,1,0:T(8,128)(2,1)}), bf16[16,72,128]{2,1,0:T(8,128)(2,1)S(1)}, u32[]{:S(2)}, u32[]{:S(2)}) async-start(bf16[16,72,128]{2,1,0:T(8,128)(2,1)} %bitcast.14), calls=%async_computation | async-start | bytes 589824 | tf_op jit(solution)/shard_map/all_to_all | solution.py:253
  133.8 1.0 copy-done.11
  134.9 12.7 %shard_map.58 = (bf16[256,1024]{1,0:T(8,128)(2,1)}, bf16[256,4608]{1,0:T(8,128)(2,1)}) custom-call(s32[3]{0:T(128)S(1)} %pad_add_fusion.at_ref, bf16[256,4608]{1,0:T(8,128)(2,1)} %x_ref.3, bf16[256,1024]{1,0:T(8,128)(2,1)S(1)} %copy-done.3, bf16[4,288,512]{2,1,0:T(8,128)(2,1)} %pad_maximum_fusion.rest_0_, ...), custom_call_target="tpu_custom_call" | custom-call | flops 4831838208 | bytes 16777216 | tf_op jit(solution)/shard_map/pallas_call | solution.py:206
  147.6 3.3 %collective-permute-start.21 = (f32[2,72,128]{2,1,0:T(8,128)S(1)}, f32[2,72,128]{2,1,0:T(8,128)S(1)}, u32[]{:S(2)}, u32[]{:S(2)}) collective-permute-start(f32[2,72,128]{2,1,0:T(8,128)S(1)} %convert_reduce_fusion), channel_id=1, source_target_pairs={{0,192},{1,193},{2,194},{3,195},{4,196},{5,197},{6,198},{7,199},{8... | collective-permute-start | bytes 221192 | tf_op jit(solution)/shard_map/ppermute | solution.py:36
  151.4 0.8 collective-permute-done.21
  152.3 6.0 %collective-permute-done.22 = f32[2,72,128]{2,1,0:T(8,128)S(1)} collective-permute-done((f32[2,72,128]{2,1,0:T(8,128)S(1)}, f32[2,72,128]{2,1,0:T(8,128)S(1)}, u32[]{:S(2)}, u32[]{:S(2)}) %collective-permute-start.22) | collective-permute-done | bytes 73760 | tf_op jit(solution)/shard_map/ppermute | solution.py:36
  158.6 0.8 reshape.28
  (68 shorter events, 5.9 us)
Async XLA Ops:
  0.6 1.7 %copy-start = (bf16[256,4608]{1,0:T(8,128)(2,1)S(1)}, bf16[256,4608]{1,0:T(8,128)(2,1)}, u32[]{:S(2)}) copy-start(bf16[256,4608]{1,0:T(8,128)(2,1)} %x_ref.3) | copy-start | bytes 7077892
  2.3 3.5 %copy-start.2 = (bf16[256,1024]{1,0:T(8,128)(2,1)S(1)}, bf16[256,1024]{1,0:T(8,128)(2,1)}, u32[]{:S(2)}) copy-start(bf16[256,1024]{1,0:T(8,128)(2,1)} %g_ref.1) | copy-start | bytes 1572868
  5.1 6.0 %copy-start.1 = (bf16[4608,256]{1,0:T(8,128)(2,1)}, bf16[4608,256]{1,0:T(8,128)(2,1)S(1)}, u32[]{:S(2)}) copy-start(bf16[4608,256]{1,0:T(8,128)(2,1)S(1)} %shard_map.59.mine_ref) | copy-start | bytes 7077892
  5.1 6.0 %collective-permute-start.13 = (bf16[4608,256]{1,0:T(8,128)(2,1)S(1)}, bf16[4608,256]{1,0:T(8,128)(2,1)}, u32[]{:S(2)}, u32[]{:S(2)}) collective-permute-start(bf16[4608,256]{1,0:T(8,128)(2,1)S(1)} %shard_map.59.mine_ref), channel_id=1, source_target_pairs={{0,1},{1,0},{2,3},{3,2},{4,5},{5,4},{6,7},{7,6},{8,9},{9,8},{10,11... | collective-permute-start | bytes 7077896 | tf_op jit(solution)/shard_map/ppermute | solution.py:36
  6.6 3.8 %collective-permute-start.14 = (bf16[256,512]{1,0:T(8,128)(2,1)S(1)}, bf16[256,512]{1,0:T(8,128)(2,1)S(1)}, u32[]{:S(2)}, u32[]{:S(2)}) collective-permute-start(bf16[256,512]{1,0:T(8,128)(2,1)S(1)} %get-tuple-element.23), channel_id=1, source_target_pairs={{0,1},{1,0},{2,3},{3,2},{4,5},{5,4},{6,7},{7,6},{8,9},{9,8},{10,11... | collective-permute-start | bytes 786440 | tf_op jit(solution)/shard_map/ppermute | solution.py:36
  13.0 9.0 %copy-start.10 = (bf16[72,1024]{1,0:T(8,128)(2,1)S(1)}, bf16[72,1024]{1,0:T(8,128)(2,1)}, u32[]{:S(2)}) copy-start(bf16[72,1024]{1,0:T(8,128)(2,1)} %param.4) | copy-start | bytes 442372
  21.9 39.5 %collective-permute-start.15 = (bf16[4,288,512]{2,1,0:T(8,128)(2,1)}, bf16[4,288,512]{2,1,0:T(8,128)(2,1)S(1)}, u32[]{:S(2)}, u32[]{:S(2)}) collective-permute-start(bf16[4,288,512]{2,1,0:T(8,128)(2,1)} %get-tuple-element.16), channel_id=1, source_target_pairs={{0,4},{1,17},{2,6},{3,19},{4,8},{5,21},{6,10},{7,23},{8,12},{9,25}... | collective-permute-start | bytes 3538952 | tf_op jit(solution)/shard_map/ppermute | solution.py:36
  21.9 6.6 %collective-permute-start = (bf16[72,512]{1,0:T(8,128)(2,1)S(1)}, bf16[72,512]{1,0:T(8,128)(2,1)S(1)}, u32[]{:S(2)}, u32[]{:S(2)}) collective-permute-start(bf16[72,512]{1,0:T(8,128)(2,1)S(1)} %get-tuple-element.26), channel_id=1, source_target_pairs={{0,1},{1,0},{2,3},{3,2},{4,5},{5,4},{6,7},{7,6},{8,9},{9,8},{10,11... | collective-permute-start | bytes 221192 | tf_op jit(solution)/shard_map/ppermute | solution.py:36
  22.9 9.7 %collective-permute-start.1 = (bf16[72,512]{1,0:T(8,128)(2,1)S(1)}, bf16[72,512]{1,0:T(8,128)(2,1)S(1)}, u32[]{:S(2)}, u32[]{:S(2)}) collective-permute-start(bf16[72,512]{1,0:T(8,128)(2,1)S(1)} %get-tuple-element.25), channel_id=1, source_target_pairs={{0,194},{1,195},{2,192},{3,193},{4,198},{5,199},{6,196},{7,197},{8... | collective-permute-start | bytes 221192 | tf_op jit(solution)/shard_map/ppermute | solution.py:36
  28.5 6.2 %collective-permute-start.2 = (bf16[72,512]{1,0:T(8,128)(2,1)S(1)}, bf16[72,512]{1,0:T(8,128)(2,1)S(1)}, u32[]{:S(2)}, u32[]{:S(2)}) collective-permute-start(bf16[72,512]{1,0:T(8,128)(2,1)S(1)} %get-tuple-element.26), channel_id=1, source_target_pairs={{0,195},{1,194},{2,193},{3,192},{4,199},{5,198},{6,197},{7,196},{8... | collective-permute-start | bytes 221192 | tf_op jit(solution)/shard_map/ppermute | solution.py:36
  28.5 29.3 %copy-start.6 = (bf16[4,288,512]{2,1,0:T(8,128)(2,1)S(1)}, bf16[4,288,512]{2,1,0:T(8,128)(2,1)}, u32[]{:S(2)}) copy-start(bf16[4,288,512]{2,1,0:T(8,128)(2,1)} %copy-done.5) | copy-start | bytes 3538948
  34.8 23.0 %collective-permute-start.3 = (bf16[288,512]{1,0:T(8,128)(2,1)S(1)}, bf16[288,512]{1,0:T(8,128)(2,1)S(1)}, u32[]{:S(2)}, u32[]{:S(2)}) collective-permute-start(bf16[288,512]{1,0:T(8,128)(2,1)S(1)} %bitcast.32), channel_id=1, source_target_pairs={{0,12},{1,49},{2,14},{3,51},{4,0},{5,53},{6,2},{7,55},{8,4},{9,57}... | collective-permute-start | bytes 884744 | tf_op jit(solution)/shard_map/ppermute | solution.py:36
  35.5 22.3 %collective-permute-start.4 = (bf16[288,512]{1,0:T(8,128)(2,1)S(1)}, bf16[288,512]{1,0:T(8,128)(2,1)S(1)}, u32[]{:S(2)}, u32[]{:S(2)}) collective-permute-start(bf16[288,512]{1,0:T(8,128)(2,1)S(1)} %bitcast.33), channel_id=1, source_target_pairs={{0,8},{1,33},{2,10},{3,35},{4,12},{5,37},{6,14},{7,39},{8,0},{9,41... | collective-permute-start | bytes 884744 | tf_op jit(solution)/shard_map/ppermute | solution.py:36
  36.4 21.4 %collective-permute-start.5 = (bf16[288,512]{1,0:T(8,128)(2,1)S(1)}, bf16[288,512]{1,0:T(8,128)(2,1)S(1)}, u32[]{:S(2)}, u32[]{:S(2)}) collective-permute-start(bf16[288,512]{1,0:T(8,128)(2,1)S(1)} %bitcast.34), channel_id=1, source_target_pairs={{0,4},{1,17},{2,6},{3,19},{4,8},{5,21},{6,10},{7,23},{8,12},{9,25}... | collective-permute-start | bytes 884744 | tf_op jit(solution)/shard_map/ppermute | solution.py:36
  38.3 24.7 %collective-permute-start.16 = (bf16[4,288,512]{2,1,0:T(8,128)(2,1)}, bf16[4,288,512]{2,1,0:T(8,128)(2,1)S(1)}, u32[]{:S(2)}, u32[]{:S(2)}) collective-permute-start(bf16[4,288,512]{2,1,0:T(8,128)(2,1)} %copy-done.7), channel_id=1, source_target_pairs={{0,8},{1,33},{2,10},{3,35},{4,12},{5,37},{6,14},{7,39},{8,0},{9,41... | collective-permute-start | bytes 3538952 | tf_op jit(solution)/shard_map/ppermute | solution.py:36
  57.8 25.5 %collective-permute-start.17 = (bf16[4,288,512]{2,1,0:T(8,128)(2,1)S(1)}, bf16[4,288,512]{2,1,0:T(8,128)(2,1)S(1)}, u32[]{:S(2)}, u32[]{:S(2)}) collective-permute-start(bf16[4,288,512]{2,1,0:T(8,128)(2,1)S(1)} %copy-done.6), channel_id=1, source_target_pairs={{0,12},{1,49},{2,14},{3,51},{4,0},{5,53},{6,2},{7,55},{8,4},{9,57}... | collective-permute-start | bytes 3538952 | tf_op jit(solution)/shard_map/ppermute | solution.py:36
  59.0 44.6 %collective-permute-start.6 = (bf16[4,288,512]{2,1,0:T(8,128)(2,1)}, bf16[4,288,512]{2,1,0:T(8,128)(2,1)}, u32[]{:S(2)}, u32[]{:S(2)}) collective-permute-start(bf16[4,288,512]{2,1,0:T(8,128)(2,1)} %pad_maximum_fusion.rest_0_), channel_id=1, source_target_pairs={{0,48},{1,13},{2,50},{3,15},{4,52},{5,1},{6,54},{7,3},{8,56},{9,5}... | collective-permute-start | bytes 3538952 | tf_op jit(solution)/shard_map/ppermute | solution.py:36
  60.2 43.4 %collective-permute-start.7 = (bf16[4,288,512]{2,1,0:T(8,128)(2,1)}, bf16[4,288,512]{2,1,0:T(8,128)(2,1)}, u32[]{:S(2)}, u32[]{:S(2)}) collective-permute-start(bf16[4,288,512]{2,1,0:T(8,128)(2,1)} %pad_maximum_fusion.rest_0_), channel_id=1, source_target_pairs={{0,32},{1,9},{2,34},{3,11},{4,36},{5,13},{6,38},{7,15},{8,40},{9,1... | collective-permute-start | bytes 3538952 | tf_op jit(solution)/shard_map/ppermute | solution.py:36
  61.4 42.7 %collective-permute-start.8 = (bf16[4,288,512]{2,1,0:T(8,128)(2,1)}, bf16[4,288,512]{2,1,0:T(8,128)(2,1)}, u32[]{:S(2)}, u32[]{:S(2)}) collective-permute-start(bf16[4,288,512]{2,1,0:T(8,128)(2,1)} %pad_maximum_fusion.rest_0_), channel_id=1, source_target_pairs={{0,16},{1,5},{2,18},{3,7},{4,20},{5,9},{6,22},{7,11},{8,24},{9,13}... | collective-permute-start | bytes 3538952 | tf_op jit(solution)/shard_map/ppermute | solution.py:36
  85.0 19.2 %collective-permute-start.18 = (bf16[288,512]{1,0:T(8,128)(2,1)S(1)}, bf16[288,512]{1,0:T(8,128)(2,1)S(1)}, u32[]{:S(2)}, u32[]{:S(2)}) collective-permute-start(bf16[288,512]{1,0:T(8,128)(2,1)S(1)} %get-tuple-element.20), channel_id=1, source_target_pairs={{0,16},{1,5},{2,18},{3,7},{4,20},{5,9},{6,22},{7,11},{8,24},{9,13}... | collective-permute-start | bytes 884744 | tf_op jit(solution)/shard_map/ppermute | solution.py:36
  85.1 48.7 %collective-permute-start.9 = (bf16[4,288,512]{2,1,0:T(8,128)(2,1)}, bf16[4,288,512]{2,1,0:T(8,128)(2,1)S(1)}, u32[]{:S(2)}, u32[]{:S(2)}) collective-permute-start(bf16[4,288,512]{2,1,0:T(8,128)(2,1)} %pad_maximum_fusion.rest_0_), channel_id=1, source_target_pairs={{0,1},{1,0},{2,3},{3,2},{4,5},{5,4},{6,7},{7,6},{8,9},{9,8},{10,11... | collective-permute-start | bytes 3538952 | tf_op jit(solution)/shard_map/ppermute | solution.py:36
  103.6 30.2 %collective-permute-start.10 = (bf16[4,288,512]{2,1,0:T(8,128)(2,1)}, bf16[4,288,512]{2,1,0:T(8,128)(2,1)}, u32[]{:S(2)}, u32[]{:S(2)}) collective-permute-start(bf16[4,288,512]{2,1,0:T(8,128)(2,1)} %collective-permute-done.6.rest_1_), channel_id=1, source_target_pairs={{0,1},{1,0},{2,3},{3,2},{4,5},{5,4},{6,7},{7,6},{8,9},{9,8},{10,11... | collective-permute-start | bytes 3538952 | tf_op jit(solution)/shard_map/ppermute | solution.py:36
  103.7 30.2 %collective-permute-start.11 = (bf16[4,288,512]{2,1,0:T(8,128)(2,1)}, bf16[4,288,512]{2,1,0:T(8,128)(2,1)}, u32[]{:S(2)}, u32[]{:S(2)}) collective-permute-start(bf16[4,288,512]{2,1,0:T(8,128)(2,1)} %collective-permute-done.7.rest_2_), channel_id=1, source_target_pairs={{0,1},{1,0},{2,3},{3,2},{4,5},{5,4},{6,7},{7,6},{8,9},{9,8},{10,11... | collective-permute-start | bytes 3538952 | tf_op jit(solution)/shard_map/ppermute | solution.py:36
  104.1 29.7 %collective-permute-start.12 = (bf16[4,288,512]{2,1,0:T(8,128)(2,1)}, bf16[4,288,512]{2,1,0:T(8,128)(2,1)}, u32[]{:S(2)}, u32[]{:S(2)}) collective-permute-start(bf16[4,288,512]{2,1,0:T(8,128)(2,1)} %collective-permute-done.8.rest_3_), channel_id=1, source_target_pairs={{0,1},{1,0},{2,3},{3,2},{4,5},{5,4},{6,7},{7,6},{8,9},{9,8},{10,11... | collective-permute-start | bytes 3538952 | tf_op jit(solution)/shard_map/ppermute | solution.py:36
  104.2 7.1 %collective-permute-start.19 = (bf16[288,512]{1,0:T(8,128)(2,1)S(1)}, bf16[288,512]{1,0:T(8,128)(2,1)S(1)}, u32[]{:S(2)}, u32[]{:S(2)}) collective-permute-start(bf16[288,512]{1,0:T(8,128)(2,1)S(1)} %get-tuple-element.21), channel_id=1, source_target_pairs={{0,32},{1,9},{2,34},{3,11},{4,36},{5,13},{6,38},{7,15},{8,40},{9,1... | collective-permute-start | bytes 884744 | tf_op jit(solution)/shard_map/ppermute | solution.py:36
  111.3 6.8 %collective-permute-start.20 = (bf16[288,512]{1,0:T(8,128)(2,1)S(1)}, bf16[288,512]{1,0:T(8,128)(2,1)S(1)}, u32[]{:S(2)}, u32[]{:S(2)}) collective-permute-start(bf16[288,512]{1,0:T(8,128)(2,1)S(1)} %get-tuple-element.22), channel_id=1, source_target_pairs={{0,48},{1,13},{2,50},{3,15},{4,52},{5,1},{6,54},{7,3},{8,56},{9,5}... | collective-permute-start | bytes 884744 | tf_op jit(solution)/shard_map/ppermute | solution.py:36
  118.2 16.6 %copy-start.3 = (bf16[256,1024]{1,0:T(8,128)(2,1)S(1)}, bf16[256,1024]{1,0:T(8,128)(2,1)}, u32[]{:S(2)}) copy-start(bf16[256,1024]{1,0:T(8,128)(2,1)} %g_ref.1) | copy-start | bytes 1572868
  119.1 28.5 %all-to-all-start = ((bf16[16,72,128]{2,1,0:T(8,128)(2,1)}), bf16[16,72,128]{2,1,0:T(8,128)(2,1)S(1)}, u32[]{:S(2)}, u32[]{:S(2)}) async-start(bf16[16,72,128]{2,1,0:T(8,128)(2,1)} %bitcast.14), calls=%async_computation | async-start | bytes 589824 | tf_op jit(solution)/shard_map/all_to_all | solution.py:253
  133.8 1.1 copy-start.11
  147.6 4.7 %collective-permute-start.21 = (f32[2,72,128]{2,1,0:T(8,128)S(1)}, f32[2,72,128]{2,1,0:T(8,128)S(1)}, u32[]{:S(2)}, u32[]{:S(2)}) collective-permute-start(f32[2,72,128]{2,1,0:T(8,128)S(1)} %convert_reduce_fusion), channel_id=1, source_target_pairs={{0,192},{1,193},{2,194},{3,195},{4,196},{5,197},{6,198},{7,199},{8... | collective-permute-start | bytes 221192 | tf_op jit(solution)/shard_map/ppermute | solution.py:36
  150.9 7.5 %collective-permute-start.22 = (f32[2,72,128]{2,1,0:T(8,128)S(1)}, f32[2,72,128]{2,1,0:T(8,128)S(1)}, u32[]{:S(2)}, u32[]{:S(2)}) collective-permute-start(f32[2,72,128]{2,1,0:T(8,128)S(1)} %convert_reduce_fusion), channel_id=1, source_target_pairs={{0,128},{1,129},{2,130},{3,131},{4,132},{5,133},{6,134},{7,135},{8... | collective-permute-start | bytes 221192 | tf_op jit(solution)/shard_map/ppermute | solution.py:36
  150.9 7.5 %collective-permute-start.23 = (f32[2,72,128]{2,1,0:T(8,128)S(1)}, f32[2,72,128]{2,1,0:T(8,128)S(1)}, u32[]{:S(2)}, u32[]{:S(2)}) collective-permute-start(f32[2,72,128]{2,1,0:T(8,128)S(1)} %convert_reduce_fusion), channel_id=1, source_target_pairs={{0,64},{1,65},{2,66},{3,67},{4,68},{5,69},{6,70},{7,71},{8,72},{9,... | collective-permute-start | bytes 221192 | tf_op jit(solution)/shard_map/ppermute | solution.py:36
  (5 other events, 4.7 us)

commit v2 on v1

v2 whole, which is shorter than its diff:
```python
import functools

import jax
import jax.numpy as jnp
from jax import lax
from jax.experimental import pallas as pl
from jax.experimental.pallas import tpu as pltpu
from jax.sharding import Mesh, PartitionSpec as P

GROUP = 128
TAIL = 32
AXES = ("zl", "y", "x", "zh", "c")
SIZES = (4, 4, 4, 2, 2)
TOK = 256
D = 4608
KD = 1024
HALF = KD // 2
BLK = D // 16
VMEM_LIMIT = 48 * 1024 * 1024


barrier = lax.optimization_barrier


def pairs(move):
    out = []
    for i in range(256):
        rest, at = i, {}
        for name, size in zip(reversed(AXES), reversed(SIZES)):
            at[name] = rest % size
            rest //= size
        to = move(dict(at))
        j = 0
        for name, size in zip(AXES, SIZES):
            j = j * size + to[name] % size
        out.append((i, j))
    return out


def send(value, move):
    return lax.ppermute(value, AXES, pairs(move))


def other_core(at):
    at["c"] ^= 1
    return at


def mirror(at):
    at["zh"] ^= 1
    at["zl"] = 3 - at["zl"]
    return at


def first_by(step):
    def move(at):
        at["x" if at["c"] == 0 else "y"] += step
        return at

    return move


def second_by(step):
    def move(at):
        at["y" if at["c"] == 0 else "x"] += step
        return at

    return move


def z_by(step):
    def move(at):
        z = (4 * at["zh"] + at["zl"] + step) % 8
        at["zh"], at["zl"] = z // 4, z % 4
        return at

    return move


def zl_by(step):
    def move(at):
        at["zl"] += step
        return at

    return move


def restored(x):
    v = x.astype(jnp.float32).T
    scale = jnp.max(jnp.abs(v), axis=0, keepdims=True)
    low = (0.25 * scale).astype(jnp.bfloat16).astype(jnp.float32)
    high = (0.75 * scale).astype(jnp.bfloat16).astype(jnp.float32)
    twice = v + v
    mag = jnp.where((twice >= scale) | (twice < -scale), high, low)
    r = jnp.where(v >= 0.0, mag, -mag)
    token = lax.broadcasted_iota(jnp.int32, r.shape, 1)
    return jnp.where(token >= TOK - TAIL, v, r).astype(jnp.bfloat16)


def quantize_kernel(x_ref, out_ref):
    for g in range(x_ref.shape[1] // GROUP):
        span = slice(g * GROUP, (g + 1) * GROUP)
        out_ref[span, :] = restored(x_ref[:, span])


def quantize(normed):
    width = 6 * GROUP
    return pl.pallas_call(
        quantize_kernel,
        grid=(D // width,),
        in_specs=[pl.BlockSpec((TOK, width), lambda i: (0, i))],
        out_specs=pl.BlockSpec((width, TOK), lambda i: (i, 0)),
        out_shape=jax.ShapeDtypeStruct((D, TOK), jnp.bfloat16),
        compiler_params=pltpu.CompilerParams(vmem_limit_bytes=VMEM_LIMIT),
        cost_estimate=pl.CostEstimate(flops=2 * D * HALF * TOK, bytes_accessed=4 * D * TOK, transcendentals=0),
    )(normed)


ROWS = D // 4


def partial_kernel(at_ref, mine_ref, theirs_ref, gmine_ref, gtheirs_ref, o0, o1, o2, o3, acc, r, sem):
    first, core = at_ref[0], at_ref[2]
    outs = (o0, o1, o2, o3)

    def rows(block):
        return acc.at[block * BLK : (block + 1) * BLK, :]

    def make(step):
        span = slice(step * ROWS, (step + 1) * ROWS)
        total = jnp.dot(mine_ref[...], gmine_ref[...], preferred_element_type=jnp.float32)
        quantize_kernel(theirs_ref, r)
        total += jnp.dot(r[...], gtheirs_ref[...], preferred_element_type=jnp.float32)
        acc[span, :] = total.astype(jnp.bfloat16)
        for b in range(4 * step, 4 * step + 4):
            to = jnp.where(core == 0, b % 4, b // 4)
            place = jnp.where(core == 0, b // 4, b % 4)
            ahead = lax.rem(to + 4 - first, 4)
            for j, out in enumerate(outs):

                @pl.when(ahead == j)
                def _():
                    pltpu.make_async_copy(rows(b), out.at[place], sem.at[b]).start()

    for step in range(4):

        @pl.when(pl.program_id(0) == step)
        def _():
            make(step)

    @pl.when(pl.program_id(0) == 3)
    def _():
        for b in range(16):
            pltpu.make_async_copy(rows(b), o0.at[0], sem.at[b]).wait()


def partial_blocks(at, mine, theirs, gmine, gtheirs):
    acts = pl.BlockSpec((ROWS, TOK), lambda i, at: (i, 0))
    grads = pl.BlockSpec((TOK, HALF), lambda i, at: (0, 0))
    return pl.pallas_call(
        partial_kernel,
        grid_spec=pltpu.PrefetchScalarGridSpec(
            num_scalar_prefetch=1,
            grid=(4,),
            in_specs=[acts, pl.BlockSpec((TOK, ROWS), lambda i, at: (0, i)), grads, grads],
            out_specs=[pl.BlockSpec(memory_space=pl.ANY)] * 4,
            scratch_shapes=[
                pltpu.VMEM((D, HALF), jnp.bfloat16),
                pltpu.VMEM((ROWS, TOK), jnp.bfloat16),
                pltpu.SemaphoreType.DMA((16,)),
            ],
        ),
        out_shape=[jax.ShapeDtypeStruct((4, BLK, HALF), jnp.bfloat16)] * 4,
        compiler_params=pltpu.CompilerParams(vmem_limit_bytes=VMEM_LIMIT),
        cost_estimate=pl.CostEstimate(flops=3 * 4 * D * HALF * TOK, bytes_accessed=10 * 2**20, transcendentals=0),
    )(at, mine, theirs, gmine, gtheirs)


def sum_kernel(at_ref, a, b, c, d, r0, r1, r2, r3):
    total = a[0].astype(jnp.float32) + b[0].astype(jnp.float32) + c[0].astype(jnp.float32) + d[0].astype(jnp.float32)
    for j, r in enumerate((r0, r1, r2, r3)):

        @pl.when(pl.program_id(0) == j)
        def _():
            r[...] = total.astype(r.dtype)


def sum_blocks(at, blocks):
    spec = pl.BlockSpec((1, BLK, HALF), lambda j, at: (lax.rem(at[1] + j, 4), 0, 0))
    return pl.pallas_call(
        sum_kernel,
        grid_spec=pltpu.PrefetchScalarGridSpec(
            num_scalar_prefetch=1,
            grid=(4,),
            in_specs=[spec] * 4,
            out_specs=[pl.BlockSpec((BLK, HALF), lambda j, at: (0, 0))] * 4,
        ),
        out_shape=[jax.ShapeDtypeStruct((BLK, HALF), jnp.bfloat16 if j else jnp.float32) for j in range(4)],
        compiler_params=pltpu.CompilerParams(vmem_limit_bytes=VMEM_LIMIT),
        cost_estimate=pl.CostEstimate(flops=0, bytes_accessed=6 * 2**20, transcendentals=0),
    )(at, *blocks)


def units_kernel(a, b, c, d, out_ref, total):
    total[...] = a[...] + b[...].astype(jnp.float32) + c[...].astype(jnp.float32) + d[...].astype(jnp.float32)
    for zh in range(2):
        for core in range(2):
            for zl in range(4):
                s = 72 * (2 * zh + core)
                out_ref[8 * zh + 2 * zl + core] = total[s : s + 72, 128 * zl : 128 * (zl + 1)].astype(jnp.bfloat16)


def unit_sums(column):
    vmem = pl.BlockSpec(memory_space=pltpu.VMEM)
    return pl.pallas_call(
        units_kernel,
        in_specs=[vmem] * 4,
        out_specs=vmem,
        out_shape=jax.ShapeDtypeStruct((16, 72, 128), jnp.bfloat16),
        scratch_shapes=[pltpu.VMEM((BLK, HALF), jnp.float32)],
        compiler_params=pltpu.CompilerParams(vmem_limit_bytes=VMEM_LIMIT),
        cost_estimate=pl.CostEstimate(flops=0, bytes_accessed=2 * 2**20, transcendentals=0),
    )(*column)


def product_kernel(own, at_ref, x_ref, g_ref, *rest):
    line, parts, rest = rest[0], rest[1:5], rest[5:]
    if own:
        keys_ref, grad_ref, w, total, sem = rest
    else:
        half_ref, before_ref, keys_ref, grad_ref, w, total, sem = rest
    step, core = pl.program_id(0), at_ref[2]
    first, second = (at_ref[0], at_ref[1]) if own else (at_ref[1], at_ref[0])
    side = core if own else 1 - core
    turn = 2 * lax.rem(at_ref[3], 2)
    now = lax.rem(jnp.where(side == 0, second, first + turn) + step, 4)

    def copy(source, f, s, i, m):
        f, s = lax.rem(first + f, 4), lax.rem(second + s, 4)
        block = jnp.where(side == 0, 4 * s + f, 4 * f + s)
        return pltpu.make_async_copy(
            source, w.at[pl.ds(pl.multiple_of(block * BLK, BLK), BLK), :], sem.at[i, m]
        )

    @pl.when(step == 0)
    def _():
        total[...] = jnp.zeros_like(total)

        @pl.when(side == 0)
        def _():
            for m in range(4):
                copy(line.at[m], m, 0, 0, m).start()
            for i in range(1, 4):
                for m in range(4):
                    copy(parts[m].at[i - 1], turn + m, i, i, m).start()

        @pl.when(side != 0)
        def _():
            for i in range(4):
                copy(line.at[lax.rem(turn + i, 4)], turn + i, 0, i, 0).start()
                for m in range(1, 4):
                    copy(parts[i].at[m - 1], turn + i, m, i, m).start()

    for m in range(4):
        copy(line.at[0], 0, 0, step, m).wait()

    part = w[pl.ds(pl.multiple_of(now * ROWS, ROWS), ROWS), :]
    total[...] += jnp.dot(x_ref[...], part, preferred_element_type=jnp.float32)
    grad = lax.dot_general(part, g_ref[...], (((1,), (1,)), ((), ())), preferred_element_type=jnp.float32)
    if own:
        grad_ref[...] = grad
    else:
        grad_ref[...] = (grad + before_ref[...]).T.astype(grad_ref.dtype)

    @pl.when(step == 3)
    def _():
        keys = total[...].astype(jnp.bfloat16)
        if own:
            keys_ref[...] = keys
        else:

            @pl.when(core == 0)
            def _():
                keys_ref[:, :HALF] = half_ref[...]
                keys_ref[:, HALF:] = keys

            @pl.when(core != 0)
            def _():
                keys_ref[:, HALF:] = half_ref[...]
                keys_ref[:, :HALF] = keys


def products(at, normed, key_grad, parts, before=()):
    own = not before
    width = HALF if own else KD

    def now(i, at):
        side = at[2] if own else 1 - at[2]
        first, second = (at[0], at[1]) if own else (at[1], at[0])
        start = jnp.where(side == 0, second, first + 2 * lax.rem(at[3], 2))
        return lax.rem(start + i, 4)

    whole = lambda i, at: (0, 0)
    across, down = (lambda i, at: (0, now(i, at))), (lambda i, at: (now(i, at), 0))
    return pl.pallas_call(
        functools.partial(product_kernel, own),
        grid_spec=pltpu.PrefetchScalarGridSpec(
            num_scalar_prefetch=1,
            grid=(4,),
            in_specs=[pl.BlockSpec((TOK, ROWS), across), pl.BlockSpec((TOK, HALF), whole)]
            + [pl.BlockSpec(memory_space=pl.ANY)] * 5
            + ([] if own else [pl.BlockSpec((TOK, HALF), whole), pl.BlockSpec((ROWS, TOK), down)]),
            out_specs=[
                pl.BlockSpec((TOK, width), whole),
                pl.BlockSpec((ROWS, TOK), down) if own else pl.BlockSpec((TOK, ROWS), across),
            ],
            scratch_shapes=[
                pltpu.VMEM((D, HALF), jnp.bfloat16),
                pltpu.VMEM((TOK, HALF), jnp.float32),
                pltpu.SemaphoreType.DMA((4, 4)),
            ],
        ),
        out_shape=[
            jax.ShapeDtypeStruct((TOK, width), jnp.bfloat16),
            jax.ShapeDtypeStruct((D, TOK) if own else (TOK, D), jnp.float32 if own else jnp.bfloat16),
        ],
        compiler_params=pltpu.CompilerParams(vmem_limit_bytes=VMEM_LIMIT),
        cost_estimate=pl.CostEstimate(flops=2 * D * KD * TOK, bytes_accessed=12 * 2**20, transcendentals=0),
    )(at, normed, key_grad, *parts, *before)


def local(normed, key_weight, key_grad):
    zl, y, x, zh, c = (lax.axis_index(name) for name in AXES)
    first, second = jnp.where(c == 0, x, y), jnp.where(c == 0, y, x)
    at = jnp.stack([first, second, c, zl]).astype(jnp.int32)

    def half(a, which):
        return lax.dynamic_slice_in_dim(a, which * HALF, HALF, axis=1)

    w_mine, w_theirs = half(key_weight, c), half(key_weight, 1 - c)
    g_mine, g_other = half(key_grad, c), half(key_grad, 1 - c)
    x_theirs = send(normed, other_core)
    g_theirs = send(g_other, other_core)
    w_core = send(w_theirs, other_core)
    w_mirror = send(w_mine, mirror)
    w_both = send(w_theirs, lambda at: other_core(mirror(at)))
    mine = quantize(normed)
    w_core, w_mirror, w_both, mine = barrier((w_core, w_mirror, w_both, mine))
    quads = jnp.stack([w_mine, w_core, w_mirror, w_both]).reshape(2, 2, 72, HALF)
    quads = jnp.where(c == 0, quads, quads[:, ::-1])
    quads = jnp.where(zh == 0, quads, quads[::-1])
    block = quads.reshape(BLK, HALF)
    x_theirs, block, mine = barrier((x_theirs, block, mine))
    near = [send(block, first_by(-j)) for j in (1, 2, 3)]

    out = partial_blocks(at, mine, x_theirs, g_mine, g_theirs)
    out, near = barrier((out, near))

    line = jnp.stack([block] + near)
    some = lax.dynamic_slice_in_dim(line, 2 * (zl % 2), 2, axis=0)
    far = [send(some, second_by(-j)) for j in (1, 2, 3)]
    out = list(out)
    out[2], far[1] = barrier((out[2], far[1]))
    got2, got1, got3 = (send(out[j], first_by(j)) for j in (2, 1, 3))
    far_a, far_b = jnp.stack([f[0] for f in far]), jnp.stack([f[1] for f in far])
    parts = [far_a, far_b, send(far_a, z_by(-1)), send(far_b, z_by(1))]

    sums = sum_blocks(at, [out[0], got1, got2, got3])
    column = [sums[0]] + [send(sums[j], second_by(j)) for j in (1, 2, 3)]
    units = unit_sums(column)
    units, line, parts = barrier((units, line, parts))
    swapped = [send(p, other_core) for p in [line] + parts]
    keys_mine, grad = products(at, normed, g_mine, [line] + parts)
    units = lax.all_to_all(units, ("zh", "zl", "c"), 0, 0, tiled=True)
    units, keys_mine, grad, swapped = barrier((units, keys_mine, grad, swapped))
    piece = jnp.sum(units.reshape(8, 2, 72, 128).astype(jnp.float32), axis=0)
    piece, swapped = barrier((piece, swapped))
    ring = jnp.stack([piece] + [send(piece, zl_by(-j)) for j in (1, 2, 3)])
    ring = lax.dynamic_slice_in_dim(jnp.concatenate([ring, ring]), (4 - zl) % 4, 4, axis=0)
    weight_grad = ring.transpose(2, 1, 0, 3).reshape(72, KD)
    keys, input_grad = products(at, normed, g_other, swapped, (keys_mine, grad))
    return keys, input_grad, weight_grad


def solution(mesh):
    fine = Mesh(mesh.devices.reshape(SIZES), AXES)
    fsdp = ("y", "x", "zh", "c")
    tokens, rows = P(AXES, None), P(fsdp, None)
    return jax.shard_map(
        local,
        mesh=fine,
        in_specs=(tokens, rows, tokens),
        out_specs=(tokens, tokens, rows),
        check_vma=False,
    )
```

time: 160 us -> 122 us (0.76)
  starting transfers between devices: 54.5 us -> 32.1 us
  waiting for transfers between devices: 68.5 us -> 46.4 us
  Pallas kernels: 24 us -> 29.1 us
  other arithmetic: 1.61 us -> 3.4 us
    ppermute x24 -> x27, waiting for transfers between devices: 68.4 us -> 43.8 us  [send(): return lax.ppermute(value, AXES, pairs(move))]
    ppermute x24 -> x27, starting transfers between devices: 39.7 us -> 25.1 us  [send(): return lax.ppermute(value, AXES, pairs(move))]
    all_to_all x1, starting transfers between devices: 14.7 us -> 6.97 us  [local(): units = lax.all_to_all(units, ('zh', 'zl', 'c'), 0, 0, tiled=True)]
    pallas_call x1 -> x3, Pallas kernels: 12.7 us -> 17.4 us  [the longest x2 16.5 us: products(): pl.pallas_call(functools.partial(product_kernel, own), grid_spec=pltpu.Pr...]
    all_to_all x1, waiting for transfers between devices: 0.01 us -> 2.67 us  [local(): units = lax.all_to_all(units, ('zh', 'zl', 'c'), 0, 0, tiled=True)]
    unnamed x31 -> x19, local copies, waits for them, and re-layouts: 7.42 us -> 5.72 us
  transfers between devices with their start and end apart: 25 -> 28, of which waited for: 9 -> 10; matrix products, arithmetic and copies ran while one was open for 2% -> 4% of each run, Pallas kernels for 9% -> 24%
where the time goes in v2:
time: 122 us; the launch traced here: 121 us
  waiting for transfers between devices  46.4 us (38%)
  starting transfers between devices  32.1 us (26%)
  Pallas kernels  29.1 us (24%)
  local copies, waits for them, and re-layouts  8.86 us (7%)
  other arithmetic  3.4 us (3%)
    ppermute x27, waiting for transfers between devices, send(): return lax.ppermute(value, AXES, pairs(move))  43.8 us
    ppermute x27, starting transfers between devices, send(): return lax.ppermute(value, AXES, pairs(move))  25.1 us
    pallas_call x2, Pallas kernels, products(): pl.pallas_call(functools.partial(product_kernel, own), grid_spec=pltpu.Pr...  16.5 us
    pallas_call x1, Pallas kernels, partial_blocks(): pl.pallas_call(partial_kernel, grid_spec=pltpu.PrefetchScalarGridSpec(num...  7.48 us
    all_to_all x1, starting transfers between devices, local(): units = lax.all_to_all(units, ('zh', 'zl', 'c'), 0, 0, tiled=True)  6.97 us
    unnamed x19, local copies, waits for them, and re-layouts  5.72 us
    all_to_all x1, waiting for transfers between devices, local(): units = lax.all_to_all(units, ('zh', 'zl', 'c'), 0, 0, tiled=True)  2.67 us
    pallas_call x1, Pallas kernels, quantize(): pl.pallas_call(quantize_kernel, grid=(D // width,), in_specs=[pl.BlockSpe...  2.46 us
  transfers between devices with their start and end apart: 28, of which 10 were waited for; matrix products, arithmetic and copies ran while one was open for 4% of the time, Pallas kernels for 24%

profile of v2, /device:TPU:31, one launch (start us, length us, event | category | flops | bytes accessed | tf_op | source)
XLA Modules:
  0.0 120.7 jit_solution(6516822494669515261)
XLA Ops:
  1.4 0.9 constant_dynamic-slice_fusion.3
  2.4 5.9 %collective-permute-start.3 = (bf16[72,512]{1,0:T(8,128)(2,1)S(1)}, bf16[72,512]{1,0:T(8,128)(2,1)S(1)}, u32[]{:S(2)}, u32[]{:S(2)}) collective-permute-start(bf16[72,512]{1,0:T(8,128)(2,1)S(1)} %get-tuple-element.108), channel_id=1, source_target_pairs={{0,195},{1,194},{2,193},{3,192},{4,199},{5,198},{6,197},{7,196},{8... | collective-permute-start | bytes 221192 | tf_op jit(solution)/shard_map/ppermute | solution.py:41
  8.4 1.1 constant_dynamic-slice_fusion.1
  10.0 1.7 %copy-done = bf16[256,4608]{1,0:T(8,128)(2,1)S(1)} copy-done((bf16[256,4608]{1,0:T(8,128)(2,1)S(1)}, bf16[256,4608]{1,0:T(8,128)(2,1)}, u32[]{:S(2)}) %copy-start) | copy-done | bytes 2359320
  11.6 2.5 %shard_map.58.mine_ref = bf16[4608,256]{1,0:T(8,128)(2,1)S(1)} custom-call(bf16[256,4608]{1,0:T(8,128)(2,1)S(1)} %copy-done), custom_call_target="tpu_custom_call" | custom-call | flops 1207959552 | bytes 4718592 | tf_op jit(solution)/shard_map/pallas_call | solution.py:108
  14.1 1.4 %copy-done.1 = bf16[4608,256]{1,0:T(8,128)(2,1)} copy-done((bf16[4608,256]{1,0:T(8,128)(2,1)}, bf16[4608,256]{1,0:T(8,128)(2,1)S(1)}, u32[]{:S(2)}) %copy-start.1) | copy-done | bytes 2359320
  17.0 1.9 %collective-permute-start.7 = (bf16[288,512]{1,0:T(8,128)(2,1)S(1)}, bf16[288,512]{1,0:T(8,128)(2,1)S(1)}, u32[]{:S(2)}, u32[]{:S(2)}) collective-permute-start(bf16[288,512]{1,0:T(8,128)(2,1)S(1)} %bitcast.32), channel_id=1, source_target_pairs={{0,4},{1,17},{2,6},{3,19},{4,8},{5,21},{6,10},{7,23},{8,12},{9,25}... | collective-permute-start | bytes 884744 | tf_op jit(solution)/shard_map/ppermute | solution.py:41
  18.9 7.5 %shard_map.59 = (bf16[4,288,512]{2,1,0:T(8,128)(2,1)S(1)}, bf16[4,288,512]{2,1,0:T(8,128)(2,1)S(1)}, bf16[4,288,512]{2,1,0:T(8,128)(2,1)S(1)}, bf16[4,288,512]{2,1,0:T(8,128)(2,1)S(1)}) custom-call(s32[4]{0:T(128)S(1)} %pad_add_fusion.at_ref, bf16[4608,256]{1,0:T(8,128)(2,1)} %copy-done.1, bf16[256,4608]{1,0:T(8,128)(2,1)} %collective-permute-done.theirs_ref, ...), custom_call_target="tpu_custom_call" | custom-call | flops 7247757312 | bytes 10485760 | tf_op jit(solution)/shard_map/pallas_call | solution.py:160
  26.9 1.2 %collective-permute-start.9 = (bf16[2,288,512]{2,1,0:T(8,128)(2,1)S(1)}, bf16[2,288,512]{2,1,0:T(8,128)(2,1)S(1)}, u32[]{:S(2)}, u32[]{:S(2)}) collective-permute-start(bf16[2,288,512]{2,1,0:T(8,128)(2,1)S(1)} %constant_dynamic-slice_fusion), channel_id=1, source_target_pairs={{0,32},{1,9},{2,34},{3,11},{4,36},{5,13},{6,38},{7,15},{8,40},{9,1... | collective-permute-start | bytes 1769480 | tf_op jit(solution)/shard_map/ppermute | solution.py:41
  28.1 1.8 %collective-permute-start.16 = (bf16[2,288,512]{2,1,0:T(8,128)(2,1)S(1)}, bf16[2,288,512]{2,1,0:T(8,128)(2,1)S(1)}, u32[]{:S(2)}, u32[]{:S(2)}) collective-permute-start(bf16[2,288,512]{2,1,0:T(8,128)(2,1)S(1)} %constant_dynamic-slice_fusion), channel_id=1, source_target_pairs={{0,16},{1,5},{2,18},{3,7},{4,20},{5,9},{6,22},{7,11},{8,24},{9,13}... | collective-permute-start | bytes 1769480 | tf_op jit(solution)/shard_map/ppermute | solution.py:41
  30.0 2.1 %collective-permute-start.8 = (bf16[4,288,512]{2,1,0:T(8,128)(2,1)S(1)}, bf16[4,288,512]{2,1,0:T(8,128)(2,1)S(1)}, u32[]{:S(2)}, u32[]{:S(2)}) collective-permute-start(bf16[4,288,512]{2,1,0:T(8,128)(2,1)S(1)} %get-tuple-element.63), channel_id=1, source_target_pairs={{0,4},{1,17},{2,6},{3,19},{4,8},{5,21},{6,10},{7,23},{8,12},{9,25}... | collective-permute-start | bytes 3538952 | tf_op jit(solution)/shard_map/ppermute | solution.py:41
  32.0 6.2 %collective-permute-done.9 = bf16[2,288,512]{2,1,0:T(8,128)(2,1)S(1)} collective-permute-done((bf16[2,288,512]{2,1,0:T(8,128)(2,1)S(1)}, bf16[2,288,512]{2,1,0:T(8,128)(2,1)S(1)}, u32[]{:S(2)}, u32[]{:S(2)}) %collective-permute-start.9) | collective-permute-done | bytes 589856 | tf_op jit(solution)/shard_map/ppermute | solution.py:41
  38.2 1.3 %collective-permute-start.10 = (bf16[4,288,512]{2,1,0:T(8,128)(2,1)S(1)}, bf16[4,288,512]{2,1,0:T(8,128)(2,1)S(1)}, u32[]{:S(2)}, u32[]{:S(2)}) collective-permute-start(bf16[4,288,512]{2,1,0:T(8,128)(2,1)S(1)} %get-tuple-element.68), channel_id=1, source_target_pairs={{0,8},{1,33},{2,10},{3,35},{4,12},{5,37},{6,14},{7,39},{8,0},{9,41... | collective-permute-start | bytes 3538952 | tf_op jit(solution)/shard_map/ppermute | solution.py:41
  39.5 9.0 %collective-permute-done.16 = bf16[2,288,512]{2,1,0:T(8,128)(2,1)S(1)} collective-permute-done((bf16[2,288,512]{2,1,0:T(8,128)(2,1)S(1)}, bf16[2,288,512]{2,1,0:T(8,128)(2,1)S(1)}, u32[]{:S(2)}, u32[]{:S(2)}) %collective-permute-start.16) | collective-permute-done | bytes 589856 | tf_op jit(solution)/shard_map/ppermute | solution.py:41
  49.1 1.0 pad_maximum_fusion.1.rest_1_
  50.1 2.1 %collective-permute-start.17 = (bf16[3,288,512]{2,1,0:T(8,128)(2,1)}, bf16[3,288,512]{2,1,0:T(8,128)(2,1)}, u32[]{:S(2)}, u32[]{:S(2)}) collective-permute-start(bf16[3,288,512]{2,1,0:T(8,128)(2,1)} %pad_maximum_fusion.1.rest_1_), channel_id=1, source_target_pairs={{0,194},{1,195},{2,192},{3,193},{4,198},{5,199},{6,196},{7,197},{8... | collective-permute-start | bytes 2654216 | tf_op jit(solution)/shard_map/ppermute | solution.py:41
  52.2 1.0 pad_maximum_fusion.2.rest_2_
  53.2 2.5 %collective-permute-done.8.b = bf16[4,288,512]{2,1,0:T(8,128)(2,1)S(1)} collective-permute-done((bf16[4,288,512]{2,1,0:T(8,128)(2,1)S(1)}, bf16[4,288,512]{2,1,0:T(8,128)(2,1)S(1)}, u32[]{:S(2)}, u32[]{:S(2)}) %collective-permute-start.8) | collective-permute-done | bytes 1179680 | tf_op jit(solution)/shard_map/ppermute | solution.py:41
  55.7 15.9 %collective-permute-done.11.d = bf16[4,288,512]{2,1,0:T(8,128)(2,1)S(1)} collective-permute-done((bf16[4,288,512]{2,1,0:T(8,128)(2,1)S(1)}, bf16[4,288,512]{2,1,0:T(8,128)(2,1)S(1)}, u32[]{:S(2)}, u32[]{:S(2)}) %collective-permute-start.11) | collective-permute-done | bytes 1179680 | tf_op jit(solution)/shard_map/ppermute | solution.py:41
  71.7 1.7 %shard_map.60 = (f32[288,512]{1,0:T(8,128)S(1)}, bf16[288,512]{1,0:T(8,128)(2,1)S(1)}, bf16[288,512]{1,0:T(8,128)(2,1)S(1)}, bf16[288,512]{1,0:T(8,128)(2,1)S(1)}) custom-call(s32[4]{0:T(128)S(1)} %pad_add_fusion.at_ref, bf16[4,288,512]{2,1,0:T(8,128)(2,1)S(1)} %get-tuple-element.62.a, bf16[4,288,512]{2,1,0:T(8,128)(2,1)S(1)} %collective-permute-done.8.b, ...), custom_call_target="tpu_custom_call" | custom-call | bytes 6291456 | tf_op jit(solution)/shard_map/pallas_call | solution.py:190
  73.4 2.3 %collective-permute-start.12 = (bf16[288,512]{1,0:T(8,128)(2,1)S(1)}, bf16[288,512]{1,0:T(8,128)(2,1)S(1)}, u32[]{:S(2)}, u32[]{:S(2)}) collective-permute-start(bf16[288,512]{1,0:T(8,128)(2,1)S(1)} %get-tuple-element.71), channel_id=1, source_target_pairs={{0,16},{1,5},{2,18},{3,7},{4,20},{5,9},{6,22},{7,11},{8,24},{9,13}... | collective-permute-start | bytes 884744 | tf_op jit(solution)/shard_map/ppermute | solution.py:41
  76.4 6.2 %collective-permute-done.12.b = bf16[288,512]{1,0:T(8,128)(2,1)S(1)} collective-permute-done((bf16[288,512]{1,0:T(8,128)(2,1)S(1)}, bf16[288,512]{1,0:T(8,128)(2,1)S(1)}, u32[]{:S(2)}, u32[]{:S(2)}) %collective-permute-start.12) | collective-permute-done | bytes 294944 | tf_op jit(solution)/shard_map/ppermute | solution.py:41
  82.9 2.8 %collective-permute-done.14.d = bf16[288,512]{1,0:T(8,128)(2,1)S(1)} collective-permute-done((bf16[288,512]{1,0:T(8,128)(2,1)S(1)}, bf16[288,512]{1,0:T(8,128)(2,1)S(1)}, u32[]{:S(2)}, u32[]{:S(2)}) %collective-permute-start.14) | collective-permute-done | bytes 294944 | tf_op jit(solution)/shard_map/ppermute | solution.py:41
  87.7 7.0 %all-to-all-start = ((bf16[16,72,128]{2,1,0:T(8,128)(2,1)}), bf16[16,72,128]{2,1,0:T(8,128)(2,1)}, u32[]{:S(2)}, u32[]{:S(2)}) async-start(bf16[16,72,128]{2,1,0:T(8,128)(2,1)} %shard_map.61), calls=%async_computation | async-start | bytes 589824 | tf_op jit(solution)/shard_map/all_to_all | solution.py:374
  94.7 0.9 copy-done.3
  95.6 8.1 %shard_map.62 = (bf16[256,512]{1,0:T(8,128)(2,1)S(1)}, f32[4608,256]{1,0:T(8,128)}) custom-call(s32[4]{0:T(128)S(1)} %pad_add_fusion.at_ref, bf16[256,4608]{1,0:T(8,128)(2,1)} %x_ref.5, bf16[256,512]{1,0:T(8,128)(2,1)S(1)} %copy-done.3, bf16[4,288,512]{2,1,0:T(8,128)(2,1)S(1)} %pad_maximum_fusion.rest_0_, bf16[3,288,512]{2,1,0:T(8,128)(2,1)} %pad_maximum_fusion.1.rest_1_, ...), custom_call_target="tpu_custom_call" | custom-call | flops 2415919104 | bytes 12582912 | tf_op jit(solution)/shard_map/pallas_call | solution.py:305
  104.5 2.7 %all-to-all-done = bf16[16,72,128]{2,1,0:T(8,128)(2,1)} async-done(((bf16[16,72,128]{2,1,0:T(8,128)(2,1)}), bf16[16,72,128]{2,1,0:T(8,128)(2,1)}, u32[]{:S(2)}, u32[]{:S(2)}) %all-to-all-start) | async-done | bytes 294944 | tf_op jit(solution)/shard_map/all_to_all | solution.py:374
  107.2 1.0 convert_reduce_fusion
  108.2 1.2 collective-permute-start.24
  109.4 0.9 collective-permute-start.26
  110.3 0.9 copy-done.5
  111.2 8.4 %shard_map.63 = (bf16[256,1024]{1,0:T(8,128)(2,1)}, bf16[256,4608]{1,0:T(8,128)(2,1)}) custom-call(s32[4]{0:T(128)S(1)} %pad_add_fusion.at_ref, bf16[256,4608]{1,0:T(8,128)(2,1)} %x_ref.5, bf16[256,512]{1,0:T(8,128)(2,1)S(1)} %get-tuple-element.106.g_ref, bf16[4,288,512]{2,1,0:T(8,128)(2,1)S(1)} %collective-permute-done.19.rest_0_, ...), custom_call_target="tpu_custom_call" | custom-call | flops 2415919104 | bytes 12582912 | tf_op jit(solution)/shard_map/pallas_call | solution.py:305
  (67 shorter events, 8.7 us)
Async XLA Ops:
  0.6 15.2 %collective-permute-start = (bf16[256,4608]{1,0:T(8,128)(2,1)}, bf16[256,4608]{1,0:T(8,128)(2,1)}, u32[]{:S(2)}, u32[]{:S(2)}) collective-permute-start(bf16[256,4608]{1,0:T(8,128)(2,1)} %x_ref.5), channel_id=1, source_target_pairs={{0,1},{1,0},{2,3},{3,2},{4,5},{5,4},{6,7},{7,6},{8,9},{9,8},{10,11... | collective-permute-start | bytes 7077896 | tf_op jit(solution)/shard_map/ppermute | solution.py:41
  2.3 13.3 %collective-permute-start.1 = (bf16[72,512]{1,0:T(8,128)(2,1)S(1)}, bf16[72,512]{1,0:T(8,128)(2,1)S(1)}, u32[]{:S(2)}, u32[]{:S(2)}) collective-permute-start(bf16[72,512]{1,0:T(8,128)(2,1)S(1)} %get-tuple-element.108), channel_id=1, source_target_pairs={{0,1},{1,0},{2,3},{3,2},{4,5},{5,4},{6,7},{7,6},{8,9},{9,8},{10,11... | collective-permute-start | bytes 221192 | tf_op jit(solution)/shard_map/ppermute | solution.py:41
  2.4 13.2 %collective-permute-start.3 = (bf16[72,512]{1,0:T(8,128)(2,1)S(1)}, bf16[72,512]{1,0:T(8,128)(2,1)S(1)}, u32[]{:S(2)}, u32[]{:S(2)}) collective-permute-start(bf16[72,512]{1,0:T(8,128)(2,1)S(1)} %get-tuple-element.108), channel_id=1, source_target_pairs={{0,195},{1,194},{2,193},{3,192},{4,199},{5,198},{6,197},{7,196},{8... | collective-permute-start | bytes 221192 | tf_op jit(solution)/shard_map/ppermute | solution.py:41
  8.4 7.2 %collective-permute-start.2 = (bf16[72,512]{1,0:T(8,128)(2,1)S(1)}, bf16[72,512]{1,0:T(8,128)(2,1)S(1)}, u32[]{:S(2)}, u32[]{:S(2)}) collective-permute-start(bf16[72,512]{1,0:T(8,128)(2,1)S(1)} %get-tuple-element.107), channel_id=1, source_target_pairs={{0,194},{1,195},{2,192},{3,193},{4,198},{5,199},{6,196},{7,197},{8... | collective-permute-start | bytes 221192 | tf_op jit(solution)/shard_map/ppermute | solution.py:41
  9.5 9.4 %copy-start.2 = (bf16[256,512]{1,0:T(8,128)(2,1)}, bf16[256,512]{1,0:T(8,128)(2,1)S(1)}, u32[]{:S(2)}) copy-start(bf16[256,512]{1,0:T(8,128)(2,1)S(1)} %get-tuple-element.105.gmine_ref.g_ref) | copy-start | bytes 786436
  9.5 9.4 %collective-permute-start.4 = (bf16[256,512]{1,0:T(8,128)(2,1)S(1)}, bf16[256,512]{1,0:T(8,128)(2,1)S(1)}, u32[]{:S(2)}, u32[]{:S(2)}) collective-permute-start(bf16[256,512]{1,0:T(8,128)(2,1)S(1)} %get-tuple-element.106.g_ref), channel_id=1, source_target_pairs={{0,1},{1,0},{2,3},{3,2},{4,5},{5,4},{6,7},{7,6},{8,9},{9,8},{10,11... | collective-permute-start | bytes 786440 | tf_op jit(solution)/shard_map/ppermute | solution.py:41
  10.0 1.7 %copy-start = (bf16[256,4608]{1,0:T(8,128)(2,1)S(1)}, bf16[256,4608]{1,0:T(8,128)(2,1)}, u32[]{:S(2)}) copy-start(bf16[256,4608]{1,0:T(8,128)(2,1)} %x_ref.5) | copy-start | bytes 7077892
  14.1 1.4 %copy-start.1 = (bf16[4608,256]{1,0:T(8,128)(2,1)}, bf16[4608,256]{1,0:T(8,128)(2,1)S(1)}, u32[]{:S(2)}) copy-start(bf16[4608,256]{1,0:T(8,128)(2,1)S(1)} %shard_map.58.mine_ref) | copy-start | bytes 7077892
  15.8 10.6 %collective-permute-start.5 = (bf16[288,512]{1,0:T(8,128)(2,1)S(1)}, bf16[288,512]{1,0:T(8,128)(2,1)S(1)}, u32[]{:S(2)}, u32[]{:S(2)}) collective-permute-start(bf16[288,512]{1,0:T(8,128)(2,1)S(1)} %bitcast.30), channel_id=1, source_target_pairs={{0,12},{1,49},{2,14},{3,51},{4,0},{5,53},{6,2},{7,55},{8,4},{9,57}... | collective-permute-start | bytes 884744 | tf_op jit(solution)/shard_map/ppermute | solution.py:41
  16.3 10.1 %collective-permute-start.6 = (bf16[288,512]{1,0:T(8,128)(2,1)S(1)}, bf16[288,512]{1,0:T(8,128)(2,1)S(1)}, u32[]{:S(2)}, u32[]{:S(2)}) collective-permute-start(bf16[288,512]{1,0:T(8,128)(2,1)S(1)} %bitcast.31), channel_id=1, source_target_pairs={{0,8},{1,33},{2,10},{3,35},{4,12},{5,37},{6,14},{7,39},{8,0},{9,41... | collective-permute-start | bytes 884744 | tf_op jit(solution)/shard_map/ppermute | solution.py:41
  17.0 9.7 %collective-permute-start.7 = (bf16[288,512]{1,0:T(8,128)(2,1)S(1)}, bf16[288,512]{1,0:T(8,128)(2,1)S(1)}, u32[]{:S(2)}, u32[]{:S(2)}) collective-permute-start(bf16[288,512]{1,0:T(8,128)(2,1)S(1)} %bitcast.32), channel_id=1, source_target_pairs={{0,4},{1,17},{2,6},{3,19},{4,8},{5,21},{6,10},{7,23},{8,12},{9,25}... | collective-permute-start | bytes 884744 | tf_op jit(solution)/shard_map/ppermute | solution.py:41
  26.9 11.3 %collective-permute-start.9 = (bf16[2,288,512]{2,1,0:T(8,128)(2,1)S(1)}, bf16[2,288,512]{2,1,0:T(8,128)(2,1)S(1)}, u32[]{:S(2)}, u32[]{:S(2)}) collective-permute-start(bf16[2,288,512]{2,1,0:T(8,128)(2,1)S(1)} %constant_dynamic-slice_fusion), channel_id=1, source_target_pairs={{0,32},{1,9},{2,34},{3,11},{4,36},{5,13},{6,38},{7,15},{8,40},{9,1... | collective-permute-start | bytes 1769480 | tf_op jit(solution)/shard_map/ppermute | solution.py:41
  28.1 20.4 %collective-permute-start.16 = (bf16[2,288,512]{2,1,0:T(8,128)(2,1)S(1)}, bf16[2,288,512]{2,1,0:T(8,128)(2,1)S(1)}, u32[]{:S(2)}, u32[]{:S(2)}) collective-permute-start(bf16[2,288,512]{2,1,0:T(8,128)(2,1)S(1)} %constant_dynamic-slice_fusion), channel_id=1, source_target_pairs={{0,16},{1,5},{2,18},{3,7},{4,20},{5,9},{6,22},{7,11},{8,24},{9,13}... | collective-permute-start | bytes 1769480 | tf_op jit(solution)/shard_map/ppermute | solution.py:41
  30.0 19.0 %collective-permute-start.15 = (bf16[2,288,512]{2,1,0:T(8,128)(2,1)S(1)}, bf16[2,288,512]{2,1,0:T(8,128)(2,1)S(1)}, u32[]{:S(2)}, u32[]{:S(2)}) collective-permute-start(bf16[2,288,512]{2,1,0:T(8,128)(2,1)S(1)} %constant_dynamic-slice_fusion), channel_id=1, source_target_pairs={{0,48},{1,13},{2,50},{3,15},{4,52},{5,1},{6,54},{7,3},{8,56},{9,5}... | collective-permute-start | bytes 1769480 | tf_op jit(solution)/shard_map/ppermute | solution.py:41
  30.0 25.8 %collective-permute-start.8 = (bf16[4,288,512]{2,1,0:T(8,128)(2,1)S(1)}, bf16[4,288,512]{2,1,0:T(8,128)(2,1)S(1)}, u32[]{:S(2)}, u32[]{:S(2)}) collective-permute-start(bf16[4,288,512]{2,1,0:T(8,128)(2,1)S(1)} %get-tuple-element.63), channel_id=1, source_target_pairs={{0,4},{1,17},{2,6},{3,19},{4,8},{5,21},{6,10},{7,23},{8,12},{9,25}... | collective-permute-start | bytes 3538952 | tf_op jit(solution)/shard_map/ppermute | solution.py:41
  32.0 39.6 %collective-permute-start.11 = (bf16[4,288,512]{2,1,0:T(8,128)(2,1)S(1)}, bf16[4,288,512]{2,1,0:T(8,128)(2,1)S(1)}, u32[]{:S(2)}, u32[]{:S(2)}) collective-permute-start(bf16[4,288,512]{2,1,0:T(8,128)(2,1)S(1)} %get-tuple-element.69), channel_id=1, source_target_pairs={{0,12},{1,49},{2,14},{3,51},{4,0},{5,53},{6,2},{7,55},{8,4},{9,57}... | collective-permute-start | bytes 3538952 | tf_op jit(solution)/shard_map/ppermute | solution.py:41
  38.2 33.4 %collective-permute-start.10 = (bf16[4,288,512]{2,1,0:T(8,128)(2,1)S(1)}, bf16[4,288,512]{2,1,0:T(8,128)(2,1)S(1)}, u32[]{:S(2)}, u32[]{:S(2)}) collective-permute-start(bf16[4,288,512]{2,1,0:T(8,128)(2,1)S(1)} %get-tuple-element.68), channel_id=1, source_target_pairs={{0,8},{1,33},{2,10},{3,35},{4,12},{5,37},{6,14},{7,39},{8,0},{9,41... | collective-permute-start | bytes 3538952 | tf_op jit(solution)/shard_map/ppermute | solution.py:41
  50.1 36.5 %collective-permute-start.17 = (bf16[3,288,512]{2,1,0:T(8,128)(2,1)}, bf16[3,288,512]{2,1,0:T(8,128)(2,1)}, u32[]{:S(2)}, u32[]{:S(2)}) collective-permute-start(bf16[3,288,512]{2,1,0:T(8,128)(2,1)} %pad_maximum_fusion.1.rest_1_), channel_id=1, source_target_pairs={{0,194},{1,195},{2,192},{3,193},{4,198},{5,199},{6,196},{7,197},{8... | collective-permute-start | bytes 2654216 | tf_op jit(solution)/shard_map/ppermute | solution.py:41
  53.2 33.4 %collective-permute-start.18 = (bf16[3,288,512]{2,1,0:T(8,128)(2,1)}, bf16[3,288,512]{2,1,0:T(8,128)(2,1)}, u32[]{:S(2)}, u32[]{:S(2)}) collective-permute-start(bf16[3,288,512]{2,1,0:T(8,128)(2,1)} %pad_maximum_fusion.2.rest_2_), channel_id=1, source_target_pairs={{0,64},{1,65},{2,66},{3,67},{4,68},{5,69},{6,70},{7,71},{8,72},{9,... | collective-permute-start | bytes 2654216 | tf_op jit(solution)/shard_map/ppermute | solution.py:41
  73.4 9.1 %collective-permute-start.12 = (bf16[288,512]{1,0:T(8,128)(2,1)S(1)}, bf16[288,512]{1,0:T(8,128)(2,1)S(1)}, u32[]{:S(2)}, u32[]{:S(2)}) collective-permute-start(bf16[288,512]{1,0:T(8,128)(2,1)S(1)} %get-tuple-element.71), channel_id=1, source_target_pairs={{0,16},{1,5},{2,18},{3,7},{4,20},{5,9},{6,22},{7,11},{8,24},{9,13}... | collective-permute-start | bytes 884744 | tf_op jit(solution)/shard_map/ppermute | solution.py:41
  75.7 7.2 %collective-permute-start.13 = (bf16[288,512]{1,0:T(8,128)(2,1)S(1)}, bf16[288,512]{1,0:T(8,128)(2,1)S(1)}, u32[]{:S(2)}, u32[]{:S(2)}) collective-permute-start(bf16[288,512]{1,0:T(8,128)(2,1)S(1)} %get-tuple-element.72), channel_id=1, source_target_pairs={{0,32},{1,9},{2,34},{3,11},{4,36},{5,13},{6,38},{7,15},{8,40},{9,1... | collective-permute-start | bytes 884744 | tf_op jit(solution)/shard_map/ppermute | solution.py:41
  75.8 9.9 %collective-permute-start.14 = (bf16[288,512]{1,0:T(8,128)(2,1)S(1)}, bf16[288,512]{1,0:T(8,128)(2,1)S(1)}, u32[]{:S(2)}, u32[]{:S(2)}) collective-permute-start(bf16[288,512]{1,0:T(8,128)(2,1)S(1)} %get-tuple-element.73), channel_id=1, source_target_pairs={{0,48},{1,13},{2,50},{3,15},{4,52},{5,1},{6,54},{7,3},{8,56},{9,5}... | collective-permute-start | bytes 884744 | tf_op jit(solution)/shard_map/ppermute | solution.py:41
  86.6 20.6 %collective-permute-start.19 = (bf16[4,288,512]{2,1,0:T(8,128)(2,1)S(1)}, bf16[4,288,512]{2,1,0:T(8,128)(2,1)S(1)}, u32[]{:S(2)}, u32[]{:S(2)}) collective-permute-start(bf16[4,288,512]{2,1,0:T(8,128)(2,1)S(1)} %pad_maximum_fusion.rest_0_), channel_id=1, source_target_pairs={{0,1},{1,0},{2,3},{3,2},{4,5},{5,4},{6,7},{7,6},{8,9},{9,8},{10,11... | collective-permute-start | bytes 3538952 | tf_op jit(solution)/shard_map/ppermute | solution.py:41
  86.6 20.6 %collective-permute-start.20 = (bf16[3,288,512]{2,1,0:T(8,128)(2,1)}, bf16[3,288,512]{2,1,0:T(8,128)(2,1)S(1)}, u32[]{:S(2)}, u32[]{:S(2)}) collective-permute-start(bf16[3,288,512]{2,1,0:T(8,128)(2,1)} %pad_maximum_fusion.1.rest_1_), channel_id=1, source_target_pairs={{0,1},{1,0},{2,3},{3,2},{4,5},{5,4},{6,7},{7,6},{8,9},{9,8},{10,11... | collective-permute-start | bytes 2654216 | tf_op jit(solution)/shard_map/ppermute | solution.py:41
  87.1 20.1 %collective-permute-start.21 = (bf16[3,288,512]{2,1,0:T(8,128)(2,1)}, bf16[3,288,512]{2,1,0:T(8,128)(2,1)}, u32[]{:S(2)}, u32[]{:S(2)}) collective-permute-start(bf16[3,288,512]{2,1,0:T(8,128)(2,1)} %pad_maximum_fusion.2.rest_2_), channel_id=1, source_target_pairs={{0,1},{1,0},{2,3},{3,2},{4,5},{5,4},{6,7},{7,6},{8,9},{9,8},{10,11... | collective-permute-start | bytes 2654216 | tf_op jit(solution)/shard_map/ppermute | solution.py:41
  87.2 20.0 %collective-permute-start.22 = (bf16[3,288,512]{2,1,0:T(8,128)(2,1)}, bf16[3,288,512]{2,1,0:T(8,128)(2,1)}, u32[]{:S(2)}, u32[]{:S(2)}) collective-permute-start(bf16[3,288,512]{2,1,0:T(8,128)(2,1)} %collective-permute-done.17.rest_3_), channel_id=1, source_target_pairs={{0,1},{1,0},{2,3},{3,2},{4,5},{5,4},{6,7},{7,6},{8,9},{9,8},{10,11... | collective-permute-start | bytes 2654216 | tf_op jit(solution)/shard_map/ppermute | solution.py:41
  87.6 19.5 %collective-permute-start.23 = (bf16[3,288,512]{2,1,0:T(8,128)(2,1)}, bf16[3,288,512]{2,1,0:T(8,128)(2,1)}, u32[]{:S(2)}, u32[]{:S(2)}) collective-permute-start(bf16[3,288,512]{2,1,0:T(8,128)(2,1)} %collective-permute-done.18.rest_4_), channel_id=1, source_target_pairs={{0,1},{1,0},{2,3},{3,2},{4,5},{5,4},{6,7},{7,6},{8,9},{9,8},{10,11... | collective-permute-start | bytes 2654216 | tf_op jit(solution)/shard_map/ppermute | solution.py:41
  87.7 19.4 %all-to-all-start = ((bf16[16,72,128]{2,1,0:T(8,128)(2,1)}), bf16[16,72,128]{2,1,0:T(8,128)(2,1)}, u32[]{:S(2)}, u32[]{:S(2)}) async-start(bf16[16,72,128]{2,1,0:T(8,128)(2,1)} %shard_map.61), calls=%async_computation | async-start | bytes 589824 | tf_op jit(solution)/shard_map/all_to_all | solution.py:374
  94.7 0.9 copy-start.3
  108.2 11.4 %collective-permute-start.24 = (f32[2,72,128]{2,1,0:T(8,128)S(1)}, f32[2,72,128]{2,1,0:T(8,128)S(1)}, u32[]{:S(2)}, u32[]{:S(2)}) collective-permute-start(f32[2,72,128]{2,1,0:T(8,128)S(1)} %convert_reduce_fusion), channel_id=1, source_target_pairs={{0,192},{1,193},{2,194},{3,195},{4,196},{5,197},{6,198},{7,199},{8... | collective-permute-start | bytes 221192 | tf_op jit(solution)/shard_map/ppermute | solution.py:41
  109.4 10.2 %collective-permute-start.25 = (f32[2,72,128]{2,1,0:T(8,128)S(1)}, f32[2,72,128]{2,1,0:T(8,128)S(1)}, u32[]{:S(2)}, u32[]{:S(2)}) collective-permute-start(f32[2,72,128]{2,1,0:T(8,128)S(1)} %convert_reduce_fusion), channel_id=1, source_target_pairs={{0,128},{1,129},{2,130},{3,131},{4,132},{5,133},{6,134},{7,135},{8... | collective-permute-start | bytes 221192 | tf_op jit(solution)/shard_map/ppermute | solution.py:41
  109.4 10.3 %collective-permute-start.26 = (f32[2,72,128]{2,1,0:T(8,128)S(1)}, f32[2,72,128]{2,1,0:T(8,128)S(1)}, u32[]{:S(2)}, u32[]{:S(2)}) collective-permute-start(f32[2,72,128]{2,1,0:T(8,128)S(1)} %convert_reduce_fusion), channel_id=1, source_target_pairs={{0,64},{1,65},{2,66},{3,67},{4,68},{5,69},{6,70},{7,71},{8,72},{9,... | collective-permute-start | bytes 221192 | tf_op jit(solution)/shard_map/ppermute | solution.py:41
  (2 other events, 1.7 us)

commit v3 on v2

--- a/solution.py
+++ b/solution.py
@@ -1,5 +1,3 @@
-import functools
-
 import jax
 import jax.numpy as jnp
 from jax import lax
@@ -16,10 +14,15 @@
 KD = 1024
 HALF = KD // 2
 BLK = D // 16
-VMEM_LIMIT = 48 * 1024 * 1024
+VMEM_LIMIT = 28 * 1024 * 1024
+SMALL_LIMIT = 20 * 1024 * 1024
 
 
 barrier = lax.optimization_barrier
+
+
+def in_hbm(x):
+    return pltpu.with_memory_space_constraint(x, pltpu.HBM)
 
 
 def pairs(move):
@@ -111,7 +114,7 @@
         in_specs=[pl.BlockSpec((TOK, width), lambda i: (0, i))],
         out_specs=pl.BlockSpec((width, TOK), lambda i: (i, 0)),
         out_shape=jax.ShapeDtypeStruct((D, TOK), jnp.bfloat16),
-        compiler_params=pltpu.CompilerParams(vmem_limit_bytes=VMEM_LIMIT),
+        compiler_params=pltpu.CompilerParams(vmem_limit_bytes=SMALL_LIMIT),
         cost_estimate=pl.CostEstimate(flops=2 * D * HALF * TOK, bytes_accessed=4 * D * TOK, transcendentals=0),
     )(normed)
 
@@ -171,7 +174,7 @@
             ],
         ),
         out_shape=[jax.ShapeDtypeStruct((4, BLK, HALF), jnp.bfloat16)] * 4,
-        compiler_params=pltpu.CompilerParams(vmem_limit_bytes=VMEM_LIMIT),
+        compiler_params=pltpu.CompilerParams(vmem_limit_bytes=SMALL_LIMIT),
         cost_estimate=pl.CostEstimate(flops=3 * 4 * D * HALF * TOK, bytes_accessed=10 * 2**20, transcendentals=0),
     )(at, mine, theirs, gmine, gtheirs)
 
@@ -196,7 +199,7 @@
             out_specs=[pl.BlockSpec((BLK, HALF), lambda j, at: (0, 0))] * 4,
         ),
         out_shape=[jax.ShapeDtypeStruct((BLK, HALF), jnp.bfloat16 if j else jnp.float32) for j in range(4)],
-        compiler_params=pltpu.CompilerParams(vmem_limit_bytes=VMEM_LIMIT),
+        compiler_params=pltpu.CompilerParams(vmem_limit_bytes=SMALL_LIMIT),
         cost_estimate=pl.CostEstimate(flops=0, bytes_accessed=6 * 2**20, transcendentals=0),
     )(at, *blocks)
 
@@ -218,115 +221,93 @@
         out_specs=vmem,
         out_shape=jax.ShapeDtypeStruct((16, 72, 128), jnp.bfloat16),
         scratch_shapes=[pltpu.VMEM((BLK, HALF), jnp.float32)],
-        compiler_params=pltpu.CompilerParams(vmem_limit_bytes=VMEM_LIMIT),
+        compiler_params=pltpu.CompilerParams(vmem_limit_bytes=SMALL_LIMIT),
         cost_estimate=pl.CostEstimate(flops=0, bytes_accessed=2 * 2**20, transcendentals=0),
     )(*column)
 
 
-def product_kernel(own, at_ref, x_ref, g_ref, *rest):
-    line, parts, rest = rest[0], rest[1:5], rest[5:]
-    if own:
-        keys_ref, grad_ref, w, total, sem = rest
-    else:
-        half_ref, before_ref, keys_ref, grad_ref, w, total, sem = rest
+def product_kernel(at_ref, x_ref, g_ref, *rest):
+    sides, (keys_ref, grad_ref, w, total, sem) = (rest[:5], rest[5:10]), rest[10:]
     step, core = pl.program_id(0), at_ref[2]
-    first, second = (at_ref[0], at_ref[1]) if own else (at_ref[1], at_ref[0])
-    side = core if own else 1 - core
+    x_at, y_at = jnp.where(core == 0, at_ref[0], at_ref[1]), jnp.where(core == 0, at_ref[1], at_ref[0])
     turn = 2 * lax.rem(at_ref[3], 2)
-    now = lax.rem(jnp.where(side == 0, second, first + turn) + step, 4)
-
-    def copy(source, f, s, i, m):
-        f, s = lax.rem(first + f, 4), lax.rem(second + s, 4)
-        block = jnp.where(side == 0, 4 * s + f, 4 * f + s)
-        return pltpu.make_async_copy(
-            source, w.at[pl.ds(pl.multiple_of(block * BLK, BLK), BLK), :], sem.at[i, m]
-        )
+
+    def copy(source, y, x, side, i, m):
+        y, x = lax.rem(y_at + y, 4), lax.rem(x_at + x, 4)
+        rows = pl.ds(pl.multiple_of((4 * y + x) * BLK, BLK), BLK)
+        columns = slice(side * HALF, (side + 1) * HALF)
+        return pltpu.make_async_copy(source, w.at[rows, columns], sem.at[side, i, m])
+
+    def start(side, line, parts, i):
+        ahead = lax.rem(turn + i, 4)
+        if side == 1:
+            copy(line.at[ahead], ahead, 0, side, i, 0).start()
+            for m in range(1, 4):
+                copy(parts[i].at[m - 1], ahead, m, side, i, m).start()
+            return
+
+        @pl.when(ahead == 0)
+        def _():
+            for m in range(4):
+                copy(line.at[m], 0, m, side, i, m).start()
+
+        @pl.when(ahead != 0)
+        def _():
+            for m in range(4):
+                copy(parts[m].at[jnp.maximum(ahead - 1, 0)], ahead, turn + m, side, i, m).start()
+
+    for i in range(4):
+        for own in range(2):
+
+            @pl.when((step == max(i - 1, 0)) & (core == own))
+            def _():
+                for side in range(2):
+                    mine = sides[0 if side == own else 1]
+                    start(side, mine[0], mine[1:], i)
 
     @pl.when(step == 0)
     def _():
         total[...] = jnp.zeros_like(total)
 
-        @pl.when(side == 0)
-        def _():
-            for m in range(4):
-                copy(line.at[m], m, 0, 0, m).start()
-            for i in range(1, 4):
-                for m in range(4):
-                    copy(parts[m].at[i - 1], turn + m, i, i, m).start()
-
-        @pl.when(side != 0)
-        def _():
-            for i in range(4):
-                copy(line.at[lax.rem(turn + i, 4)], turn + i, 0, i, 0).start()
-                for m in range(1, 4):
-                    copy(parts[i].at[m - 1], turn + i, m, i, m).start()
-
-    for m in range(4):
-        copy(line.at[0], 0, 0, step, m).wait()
-
+    for side in range(2):
+        for m in range(4):
+            copy(sides[0][0].at[0], 0, 0, side, step, m).wait()
+
+    now = lax.rem(y_at + turn + step, 4)
     part = w[pl.ds(pl.multiple_of(now * ROWS, ROWS), ROWS), :]
     total[...] += jnp.dot(x_ref[...], part, preferred_element_type=jnp.float32)
-    grad = lax.dot_general(part, g_ref[...], (((1,), (1,)), ((), ())), preferred_element_type=jnp.float32)
-    if own:
-        grad_ref[...] = grad
-    else:
-        grad_ref[...] = (grad + before_ref[...]).T.astype(grad_ref.dtype)
-
-    @pl.when(step == 3)
+    grad = lax.dot_general(g_ref[...], part, (((1,), (1,)), ((), ())), preferred_element_type=jnp.float32)
+    grad_ref[...] = grad.astype(grad_ref.dtype)
+
+    @pl.when(step == pl.num_programs(0) - 1)
     def _():
-        keys = total[...].astype(jnp.bfloat16)
-        if own:
-            keys_ref[...] = keys
-        else:
-
-            @pl.when(core == 0)
-            def _():
-                keys_ref[:, :HALF] = half_ref[...]
-                keys_ref[:, HALF:] = keys
-
-            @pl.when(core != 0)
-            def _():
-                keys_ref[:, HALF:] = half_ref[...]
-                keys_ref[:, :HALF] = keys
-
-
-def products(at, normed, key_grad, parts, before=()):
-    own = not before
-    width = HALF if own else KD
-
-    def now(i, at):
-        side = at[2] if own else 1 - at[2]
-        first, second = (at[0], at[1]) if own else (at[1], at[0])
-        start = jnp.where(side == 0, second, first + 2 * lax.rem(at[3], 2))
-        return lax.rem(start + i, 4)
+        keys_ref[...] = total[...].astype(jnp.bfloat16)
+
+
+def products(at, normed, key_grad, parts, swapped):
+    def across(i, at):
+        y = jnp.where(at[2] == 0, at[1], at[0])
+        return (0, lax.rem(y + 2 * lax.rem(at[3], 2) + i, 4))
 
     whole = lambda i, at: (0, 0)
-    across, down = (lambda i, at: (0, now(i, at))), (lambda i, at: (now(i, at), 0))
-    return pl.pallas_call(
-        functools.partial(product_kernel, own),
+    return pl.pallas_call(
+        product_kernel,
         grid_spec=pltpu.PrefetchScalarGridSpec(
             num_scalar_prefetch=1,
             grid=(4,),
-            in_specs=[pl.BlockSpec((TOK, ROWS), across), pl.BlockSpec((TOK, HALF), whole)]
-            + [pl.BlockSpec(memory_space=pl.ANY)] * 5
-            + ([] if own else [pl.BlockSpec((TOK, HALF), whole), pl.BlockSpec((ROWS, TOK), down)]),
-            out_specs=[
-                pl.BlockSpec((TOK, width), whole),
-                pl.BlockSpec((ROWS, TOK), down) if own else pl.BlockSpec((TOK, ROWS), across),
-            ],
+            in_specs=[pl.BlockSpec((TOK, ROWS), across), pl.BlockSpec((TOK, KD), whole)]
+            + [pl.BlockSpec(memory_space=pl.ANY)] * 10,
+            out_specs=[pl.BlockSpec((TOK, KD), whole), pl.BlockSpec((TOK, ROWS), across)],
             scratch_shapes=[
-                pltpu.VMEM((D, HALF), jnp.bfloat16),
-                pltpu.VMEM((TOK, HALF), jnp.float32),
-                pltpu.SemaphoreType.DMA((4, 4)),
+                pltpu.VMEM((D, KD), jnp.bfloat16),
+                pltpu.VMEM((TOK, KD), jnp.float32),
+                pltpu.SemaphoreType.DMA((2, 4, 4)),
             ],
         ),
-        out_shape=[
-            jax.ShapeDtypeStruct((TOK, width), jnp.bfloat16),
-            jax.ShapeDtypeStruct((D, TOK) if own else (TOK, D), jnp.float32 if own else jnp.bfloat16),
-        ],
+        out_shape=[jax.ShapeDtypeStruct((TOK, KD), jnp.bfloat16), jax.ShapeDtypeStruct((TOK, D), jnp.bfloat16)],
         compiler_params=pltpu.CompilerParams(vmem_limit_bytes=VMEM_LIMIT),
-        cost_estimate=pl.CostEstimate(flops=2 * D * KD * TOK, bytes_accessed=12 * 2**20, transcendentals=0),
-    )(at, normed, key_grad, *parts, *before)
+        cost_estimate=pl.CostEstimate(flops=4 * D * KD * TOK, bytes_accessed=14 * 2**20, transcendentals=0),
+    )(at, in_hbm(normed), in_hbm(key_grad), *parts, *swapped)
 
 
 def local(normed, key_weight, key_grad):
@@ -357,7 +338,7 @@
     out, near = barrier((out, near))
 
     line = jnp.stack([block] + near)
-    some = lax.dynamic_slice_in_dim(line, 2 * (zl % 2), 2, axis=0)
+    some = jnp.where(zl % 2 == 0, jnp.stack([block, near[0]]), jnp.stack(near[1:]))
     far = [send(some, second_by(-j)) for j in (1, 2, 3)]
     out = list(out)
     out[2], far[1] = barrier((out[2], far[1]))
@@ -370,15 +351,13 @@
     units = unit_sums(column)
     units, line, parts = barrier((units, line, parts))
     swapped = [send(p, other_core) for p in [line] + parts]
-    keys_mine, grad = products(at, normed, g_mine, [line] + parts)
+    keys, input_grad = products(at, normed, key_grad, [line] + parts, swapped)
     units = lax.all_to_all(units, ("zh", "zl", "c"), 0, 0, tiled=True)
-    units, keys_mine, grad, swapped = barrier((units, keys_mine, grad, swapped))
+    units, keys, input_grad = barrier((units, keys, input_grad))
     piece = jnp.sum(units.reshape(8, 2, 72, 128).astype(jnp.float32), axis=0)
-    piece, swapped = barrier((piece, swapped))
     ring = jnp.stack([piece] + [send(piece, zl_by(-j)) for j in (1, 2, 3)])
     ring = lax.dynamic_slice_in_dim(jnp.concatenate([ring, ring]), (4 - zl) % 4, 4, axis=0)
     weight_grad = ring.transpose(2, 1, 0, 3).reshape(72, KD)
-    keys, input_grad = products(at, normed, g_other, swapped, (keys_mine, grad))
     return keys, input_grad, weight_grad
 
 

time: 122 us -> 116 us (0.951)
  Pallas kernels: 29.1 us -> 22.6 us
  waiting for transfers between devices: 46.4 us -> 51.9 us
  local copies, waits for them, and re-layouts: 8.86 us -> 5.44 us
  other arithmetic: 3.4 us -> 0.72 us
  starting transfers between devices: 32.1 us -> 33.5 us
    ppermute x27, waiting for transfers between devices: 43.8 us -> 51.1 us  [send(): return lax.ppermute(value, AXES, pairs(move))]
    pallas_call x2 -> x1, Pallas kernels: 16.5 us -> 11.1 us  [products(): pl.pallas_call(product_kernel, grid_spec=pltpu.PrefetchScalarGridSpec(num...]
    unnamed x19 -> x9, local copies, waits for them, and re-layouts: 5.72 us -> 1.71 us
    all_to_all x1, waiting for transfers between devices: 2.67 us -> 0.81 us  [local(): units = lax.all_to_all(units, ('zh', 'zl', 'c'), 0, 0, tiled=True)]
    ppermute x27, starting transfers between devices: 25.1 us -> 26.8 us  [send(): return lax.ppermute(value, AXES, pairs(move))]
  transfers between devices with their start and end apart: 28 -> 28, of which waited for: 10 -> 14; matrix products, arithmetic and copies ran while one was open for 4% -> 3% of each run, Pallas kernels for 24% -> 20%
where the time goes in v3:
time: 116 us; the launch traced here: 115 us
  waiting for transfers between devices  51.9 us (45%)
  starting transfers between devices  33.5 us (29%)
  Pallas kernels  22.6 us (19%)
  local copies, waits for them, and re-layouts  5.44 us (5%)
    ppermute x27, waiting for transfers between devices, send(): return lax.ppermute(value, AXES, pairs(move))  51.1 us
    ppermute x27, starting transfers between devices, send(): return lax.ppermute(value, AXES, pairs(move))  26.8 us
    pallas_call x1, Pallas kernels, products(): pl.pallas_call(product_kernel, grid_spec=pltpu.PrefetchScalarGridSpec(num...  11.1 us
    all_to_all x1, starting transfers between devices, local(): units = lax.all_to_all(units, ('zh', 'zl', 'c'), 0, 0, tiled=True)  6.72 us
    pallas_call x1, Pallas kernels, partial_blocks(): pl.pallas_call(partial_kernel, grid_spec=pltpu.PrefetchScalarGridSpec(num...  6.44 us
    dynamic_slice x2, local copies, waits for them, and re-layouts, half(): return lax.dynamic_slice_in_dim(a, which * HALF, HALF, axis=1)  2.63 us
    pallas_call x1, Pallas kernels, quantize(): pl.pallas_call(quantize_kernel, grid=(D // width,), in_specs=[pl.BlockSpe...  2.46 us
  transfers between devices with their start and end apart: 28, of which 14 were waited for; matrix products, arithmetic and copies ran while one was open for 3% of the time, Pallas kernels for 20%

profile of v3, /device:TPU:31, one launch (start us, length us, event | category | flops | bytes accessed | tf_op | source)
XLA Modules:
  0.0 115.1 jit_solution(9995319915667028735)
XLA Ops:
  1.4 1.6 %constant_dynamic-slice_fusion.3 = (bf16[72,512]{1,0:T(8,128)(2,1)S(1)}, bf16[72,512]{1,0:T(8,128)(2,1)}) fusion(bf16[72,1024]{1,0:T(8,128)(2,1)} %param.4, s32[]{:T(128)S(6)} %select_n.54, s32[]{:T(128)S(6)} %select_n.55), kind=kLoop, calls=%fused_computation.20 | loop fusion | bytes 294920 | tf_op jit(solution)/shard_map/dynamic_slice | solution.py:319
  3.0 5.5 %collective-permute-start.3 = (bf16[72,512]{1,0:T(8,128)(2,1)}, bf16[72,512]{1,0:T(8,128)(2,1)S(1)}, u32[]{:S(2)}, u32[]{:S(2)}) collective-permute-start(bf16[72,512]{1,0:T(8,128)(2,1)} %get-tuple-element.82), channel_id=1, source_target_pairs={{0,195},{1,194},{2,193},{3,192},{4,199},{5,198},{6,197},{7,196},{8... | collective-permute-start | bytes 221192 | tf_op jit(solution)/shard_map/ppermute | solution.py:44
  8.9 1.1 constant_dynamic-slice_fusion
  10.5 1.7 %copy-done = bf16[256,4608]{1,0:T(8,128)(2,1)S(1)} copy-done((bf16[256,4608]{1,0:T(8,128)(2,1)S(1)}, bf16[256,4608]{1,0:T(8,128)(2,1)}, u32[]{:S(2)}) %copy-start) | copy-done | bytes 2359320
  12.1 2.5 %shard_map.58.mine_ref = bf16[4608,256]{1,0:T(8,128)(2,1)S(1)} custom-call(bf16[256,4608]{1,0:T(8,128)(2,1)S(1)} %copy-done), custom_call_target="tpu_custom_call" | custom-call | flops 1207959552 | bytes 4718592 | tf_op jit(solution)/shard_map/pallas_call | solution.py:111
  15.0 2.2 %collective-permute-start.6 = (bf16[288,512]{1,0:T(8,128)(2,1)S(1)}, bf16[288,512]{1,0:T(8,128)(2,1)S(1)}, u32[]{:S(2)}, u32[]{:S(2)}) collective-permute-start(bf16[288,512]{1,0:T(8,128)(2,1)S(1)} %bitcast.31), channel_id=1, source_target_pairs={{0,8},{1,33},{2,10},{3,35},{4,12},{5,37},{6,14},{7,39},{8,0},{9,41... | collective-permute-start | bytes 884744 | tf_op jit(solution)/shard_map/ppermute | solution.py:44
  17.2 6.4 %shard_map.59 = (bf16[4,288,512]{2,1,0:T(8,128)(2,1)S(1)}, bf16[4,288,512]{2,1,0:T(8,128)(2,1)S(1)}, bf16[4,288,512]{2,1,0:T(8,128)(2,1)S(1)}, bf16[4,288,512]{2,1,0:T(8,128)(2,1)S(1)}) custom-call(s32[4]{0:T(128)S(1)} %pad_add_fusion.at_ref, bf16[4608,256]{1,0:T(8,128)(2,1)S(1)} %shard_map.58.mine_ref, ...), custom_call_target="tpu_custom_call" | custom-call | flops 7247757312 | bytes 10485760 | tf_op jit(solution)/shard_map/pallas_call | solution.py:163
  23.7 1.9 %collective-permute-done.5 = bf16[288,512]{1,0:T(8,128)(2,1)S(1)} collective-permute-done((bf16[288,512]{1,0:T(8,128)(2,1)S(1)}, bf16[288,512]{1,0:T(8,128)(2,1)S(1)}, u32[]{:S(2)}, u32[]{:S(2)}) %collective-permute-start.5) | collective-permute-done | bytes 294944 | tf_op jit(solution)/shard_map/ppermute | solution.py:44
  25.7 1.1 collective-permute-start.9
  26.8 1.8 %collective-permute-start.16 = (bf16[2,288,512]{2,1,0:T(8,128)(2,1)S(1)}, bf16[2,288,512]{2,1,0:T(8,128)(2,1)S(1)}, u32[]{:S(2)}, u32[]{:S(2)}) collective-permute-start(bf16[2,288,512]{2,1,0:T(8,128)(2,1)S(1)} %maximum_select_fusion), channel_id=1, source_target_pairs={{0,16},{1,5},{2,18},{3,7},{4,20},{5,9},{6,22},{7,11},{8,24},{9,13}... | collective-permute-start | bytes 1769480 | tf_op jit(solution)/shard_map/ppermute | solution.py:44
  28.6 0.9 collective-permute-start.8
  30.1 6.3 %collective-permute-done.9 = bf16[2,288,512]{2,1,0:T(8,128)(2,1)S(1)} collective-permute-done((bf16[2,288,512]{2,1,0:T(8,128)(2,1)S(1)}, bf16[2,288,512]{2,1,0:T(8,128)(2,1)S(1)}, u32[]{:S(2)}, u32[]{:S(2)}) %collective-permute-start.9) | collective-permute-done | bytes 589856 | tf_op jit(solution)/shard_map/ppermute | solution.py:44
  36.4 1.2 %collective-permute-start.10 = (bf16[4,288,512]{2,1,0:T(8,128)(2,1)S(1)}, bf16[4,288,512]{2,1,0:T(8,128)(2,1)S(1)}, u32[]{:S(2)}, u32[]{:S(2)}) collective-permute-start(bf16[4,288,512]{2,1,0:T(8,128)(2,1)S(1)} %get-tuple-element.55), channel_id=1, source_target_pairs={{0,8},{1,33},{2,10},{3,35},{4,12},{5,37},{6,14},{7,39},{8,0},{9,41... | collective-permute-start | bytes 3538952 | tf_op jit(solution)/shard_map/ppermute | solution.py:44
  37.7 8.5 %collective-permute-done.16 = bf16[2,288,512]{2,1,0:T(8,128)(2,1)S(1)} collective-permute-done((bf16[2,288,512]{2,1,0:T(8,128)(2,1)S(1)}, bf16[2,288,512]{2,1,0:T(8,128)(2,1)S(1)}, u32[]{:S(2)}, u32[]{:S(2)}) %collective-permute-start.16) | collective-permute-done | bytes 589856 | tf_op jit(solution)/shard_map/ppermute | solution.py:44
  46.2 2.3 %collective-permute-done.15 = bf16[2,288,512]{2,1,0:T(8,128)(2,1)S(1)} collective-permute-done((bf16[2,288,512]{2,1,0:T(8,128)(2,1)S(1)}, bf16[2,288,512]{2,1,0:T(8,128)(2,1)S(1)}, u32[]{:S(2)}, u32[]{:S(2)}) %collective-permute-start.15) | collective-permute-done | bytes 589856 | tf_op jit(solution)/shard_map/ppermute | solution.py:44
  48.7 3.8 %collective-permute-start.17 = (bf16[3,288,512]{2,1,0:T(8,128)(2,1)S(1)}, bf16[3,288,512]{2,1,0:T(8,128)(2,1)}, u32[]{:S(2)}, u32[]{:S(2)}) collective-permute-start(bf16[3,288,512]{2,1,0:T(8,128)(2,1)S(1)} %pad_maximum_fusion.1.rest_1_), channel_id=1, source_target_pairs={{0,194},{1,195},{2,192},{3,193},{4,198},{5,199},{6,196},{7,197},{8... | collective-permute-start | bytes 2654216 | tf_op jit(solution)/shard_map/ppermute | solution.py:44
  52.7 3.0 %collective-permute-done.8.b = bf16[4,288,512]{2,1,0:T(8,128)(2,1)S(1)} collective-permute-done((bf16[4,288,512]{2,1,0:T(8,128)(2,1)S(1)}, bf16[4,288,512]{2,1,0:T(8,128)(2,1)S(1)}, u32[]{:S(2)}, u32[]{:S(2)}) %collective-permute-start.8) | collective-permute-done | bytes 1179680 | tf_op jit(solution)/shard_map/ppermute | solution.py:44
  55.7 15.5 %collective-permute-done.11.d = bf16[4,288,512]{2,1,0:T(8,128)(2,1)S(1)} collective-permute-done((bf16[4,288,512]{2,1,0:T(8,128)(2,1)S(1)}, bf16[4,288,512]{2,1,0:T(8,128)(2,1)S(1)}, u32[]{:S(2)}, u32[]{:S(2)}) %collective-permute-start.11) | collective-permute-done | bytes 1179680 | tf_op jit(solution)/shard_map/ppermute | solution.py:44
  71.2 1.7 %shard_map.60 = (f32[288,512]{1,0:T(8,128)S(1)}, bf16[288,512]{1,0:T(8,128)(2,1)S(1)}, bf16[288,512]{1,0:T(8,128)(2,1)S(1)}, bf16[288,512]{1,0:T(8,128)(2,1)S(1)}) custom-call(s32[4]{0:T(128)S(1)} %pad_add_fusion.at_ref, bf16[4,288,512]{2,1,0:T(8,128)(2,1)S(1)} %get-tuple-element.49.a, bf16[4,288,512]{2,1,0:T(8,128)(2,1)S(1)} %collective-permute-done.8.b, ...), custom_call_target="tpu_custom_call" | custom-call | bytes 6291456 | tf_op jit(solution)/shard_map/pallas_call | solution.py:193
  73.4 1.4 %collective-permute-start.13 = (bf16[288,512]{1,0:T(8,128)(2,1)S(1)}, bf16[288,512]{1,0:T(8,128)(2,1)S(1)}, u32[]{:S(2)}, u32[]{:S(2)}) collective-permute-start(bf16[288,512]{1,0:T(8,128)(2,1)S(1)} %get-tuple-element.59), channel_id=1, source_target_pairs={{0,32},{1,9},{2,34},{3,11},{4,36},{5,13},{6,38},{7,15},{8,40},{9,1... | collective-permute-start | bytes 884744 | tf_op jit(solution)/shard_map/ppermute | solution.py:44
  75.6 3.2 %collective-permute-done.12.b = bf16[288,512]{1,0:T(8,128)(2,1)S(1)} collective-permute-done((bf16[288,512]{1,0:T(8,128)(2,1)S(1)}, bf16[288,512]{1,0:T(8,128)(2,1)S(1)}, u32[]{:S(2)}, u32[]{:S(2)}) %collective-permute-start.12) | collective-permute-done | bytes 294944 | tf_op jit(solution)/shard_map/ppermute | solution.py:44
  78.8 1.8 %collective-permute-done.13.c = bf16[288,512]{1,0:T(8,128)(2,1)S(1)} collective-permute-done((bf16[288,512]{1,0:T(8,128)(2,1)S(1)}, bf16[288,512]{1,0:T(8,128)(2,1)S(1)}, u32[]{:S(2)}, u32[]{:S(2)}) %collective-permute-start.13) | collective-permute-done | bytes 294944 | tf_op jit(solution)/shard_map/ppermute | solution.py:44
  80.6 3.1 %collective-permute-done.14.d = bf16[288,512]{1,0:T(8,128)(2,1)S(1)} collective-permute-done((bf16[288,512]{1,0:T(8,128)(2,1)S(1)}, bf16[288,512]{1,0:T(8,128)(2,1)S(1)}, u32[]{:S(2)}, u32[]{:S(2)}) %collective-permute-start.14) | collective-permute-done | bytes 294944 | tf_op jit(solution)/shard_map/ppermute | solution.py:44
  83.7 0.9 shard_map.61
  85.7 6.7 %all-to-all-start = ((bf16[16,72,128]{2,1,0:T(8,128)(2,1)}), bf16[16,72,128]{2,1,0:T(8,128)(2,1)S(1)}, u32[]{:S(2)}, u32[]{:S(2)}) async-start(bf16[16,72,128]{2,1,0:T(8,128)(2,1)} %shard_map.61), calls=%async_computation | async-start | bytes 589824 | tf_op jit(solution)/shard_map/all_to_all | solution.py:355
  92.8 11.1 %shard_map.62 = (bf16[256,1024]{1,0:T(8,128)(2,1)}, bf16[256,4608]{1,0:T(8,128)(2,1)}) custom-call(s32[4]{0:T(128)S(1)} %pad_add_fusion.at_ref, bf16[256,4608]{1,0:T(8,128)(2,1)} %x_ref.3, bf16[256,1024]{1,0:T(8,128)(2,1)} %g_ref.1, bf16[4,288,512]{2,1,0:T(8,128)(2,1)S(1)} %pad_maximum_fusion.rest_0_, bf16[3,288,512]{2,1,0:T(8,128)(2,1)S(1)} %pad_maximum_fusion.1.rest_1_, ...), custom_call_target="tpu_custom_call" | custom-call | flops 4831838208 | bytes 14680064 | tf_op jit(solution)/shard_map/pallas_call | solution.py:293
  104.8 1.2 %collective-permute-start.26 = (f32[2,72,128]{2,1,0:T(8,128)S(1)}, f32[2,72,128]{2,1,0:T(8,128)S(1)}, u32[]{:S(2)}, u32[]{:S(2)}) collective-permute-start(f32[2,72,128]{2,1,0:T(8,128)S(1)} %convert_reduce_fusion), channel_id=1, source_target_pairs={{0,64},{1,65},{2,66},{3,67},{4,68},{5,69},{6,70},{7,71},{8,72},{9,... | collective-permute-start | bytes 221192 | tf_op jit(solution)/shard_map/ppermute | solution.py:44
  106.0 1.2 %collective-permute-start.25 = (f32[2,72,128]{2,1,0:T(8,128)S(1)}, f32[2,72,128]{2,1,0:T(8,128)S(1)}, u32[]{:S(2)}, u32[]{:S(2)}) collective-permute-start(f32[2,72,128]{2,1,0:T(8,128)S(1)} %convert_reduce_fusion), channel_id=1, source_target_pairs={{0,128},{1,129},{2,130},{3,131},{4,132},{5,133},{6,134},{7,135},{8... | collective-permute-start | bytes 221192 | tf_op jit(solution)/shard_map/ppermute | solution.py:44
  107.2 1.7 %collective-permute-start.24 = (f32[2,72,128]{2,1,0:T(8,128)S(1)}, f32[2,72,128]{2,1,0:T(8,128)S(1)}, u32[]{:S(2)}, u32[]{:S(2)}) collective-permute-start(f32[2,72,128]{2,1,0:T(8,128)S(1)} %convert_reduce_fusion), channel_id=1, source_target_pairs={{0,192},{1,193},{2,194},{3,195},{4,196},{5,197},{6,198},{7,199},{8... | collective-permute-start | bytes 221192 | tf_op jit(solution)/shard_map/ppermute | solution.py:44
  108.8 3.2 %collective-permute-done.24 = f32[2,72,128]{2,1,0:T(8,128)S(1)} collective-permute-done((f32[2,72,128]{2,1,0:T(8,128)S(1)}, f32[2,72,128]{2,1,0:T(8,128)S(1)}, u32[]{:S(2)}, u32[]{:S(2)}) %collective-permute-start.24) | collective-permute-done | bytes 73760 | tf_op jit(solution)/shard_map/ppermute | solution.py:44
  112.1 1.9 %collective-permute-done.25 = f32[2,72,128]{2,1,0:T(8,128)S(1)} collective-permute-done((f32[2,72,128]{2,1,0:T(8,128)S(1)}, f32[2,72,128]{2,1,0:T(8,128)S(1)}, u32[]{:S(2)}, u32[]{:S(2)}) %collective-permute-start.25) | collective-permute-done | bytes 73760 | tf_op jit(solution)/shard_map/ppermute | solution.py:44
  114.2 0.8 reshape.20
  (56 shorter events, 7.1 us)
Async XLA Ops:
  0.6 14.3 %collective-permute-start = (bf16[256,4608]{1,0:T(8,128)(2,1)}, bf16[256,4608]{1,0:T(8,128)(2,1)S(1)}, u32[]{:S(2)}, u32[]{:S(2)}) collective-permute-start(bf16[256,4608]{1,0:T(8,128)(2,1)} %x_ref.3), channel_id=1, source_target_pairs={{0,1},{1,0},{2,3},{3,2},{4,5},{5,4},{6,7},{7,6},{8,9},{9,8},{10,11... | collective-permute-start | bytes 7077896 | tf_op jit(solution)/shard_map/ppermute | solution.py:44
  3.0 11.8 %collective-permute-start.3 = (bf16[72,512]{1,0:T(8,128)(2,1)}, bf16[72,512]{1,0:T(8,128)(2,1)S(1)}, u32[]{:S(2)}, u32[]{:S(2)}) collective-permute-start(bf16[72,512]{1,0:T(8,128)(2,1)} %get-tuple-element.82), channel_id=1, source_target_pairs={{0,195},{1,194},{2,193},{3,192},{4,199},{5,198},{6,197},{7,196},{8... | collective-permute-start | bytes 221192 | tf_op jit(solution)/shard_map/ppermute | solution.py:44
  8.4 6.3 %collective-permute-start.1 = (bf16[72,512]{1,0:T(8,128)(2,1)}, bf16[72,512]{1,0:T(8,128)(2,1)S(1)}, u32[]{:S(2)}, u32[]{:S(2)}) collective-permute-start(bf16[72,512]{1,0:T(8,128)(2,1)} %get-tuple-element.82), channel_id=1, source_target_pairs={{0,1},{1,0},{2,3},{3,2},{4,5},{5,4},{6,7},{7,6},{8,9},{9,8},{10,11... | collective-permute-start | bytes 221192 | tf_op jit(solution)/shard_map/ppermute | solution.py:44
  8.9 5.8 %collective-permute-start.2 = (bf16[72,512]{1,0:T(8,128)(2,1)S(1)}, bf16[72,512]{1,0:T(8,128)(2,1)S(1)}, u32[]{:S(2)}, u32[]{:S(2)}) collective-permute-start(bf16[72,512]{1,0:T(8,128)(2,1)S(1)} %get-tuple-element.81), channel_id=1, source_target_pairs={{0,194},{1,195},{2,192},{3,193},{4,198},{5,199},{6,196},{7,197},{8... | collective-permute-start | bytes 221192 | tf_op jit(solution)/shard_map/ppermute | solution.py:44
  10.0 7.2 %collective-permute-start.4 = (bf16[256,512]{1,0:T(8,128)(2,1)S(1)}, bf16[256,512]{1,0:T(8,128)(2,1)S(1)}, u32[]{:S(2)}, u32[]{:S(2)}) collective-permute-start(bf16[256,512]{1,0:T(8,128)(2,1)S(1)} %get-tuple-element.79), channel_id=1, source_target_pairs={{0,1},{1,0},{2,3},{3,2},{4,5},{5,4},{6,7},{7,6},{8,9},{9,8},{10,11... | collective-permute-start | bytes 786440 | tf_op jit(solution)/shard_map/ppermute | solution.py:44
  10.5 1.7 %copy-start = (bf16[256,4608]{1,0:T(8,128)(2,1)S(1)}, bf16[256,4608]{1,0:T(8,128)(2,1)}, u32[]{:S(2)}) copy-start(bf16[256,4608]{1,0:T(8,128)(2,1)} %x_ref.3) | copy-start | bytes 7077892
  14.9 8.8 %collective-permute-start.7 = (bf16[288,512]{1,0:T(8,128)(2,1)S(1)}, bf16[288,512]{1,0:T(8,128)(2,1)S(1)}, u32[]{:S(2)}, u32[]{:S(2)}) collective-permute-start(bf16[288,512]{1,0:T(8,128)(2,1)S(1)} %bitcast.30), channel_id=1, source_target_pairs={{0,4},{1,17},{2,6},{3,19},{4,8},{5,21},{6,10},{7,23},{8,12},{9,25}... | collective-permute-start | bytes 884744 | tf_op jit(solution)/shard_map/ppermute | solution.py:44
  15.0 8.7 %collective-permute-start.6 = (bf16[288,512]{1,0:T(8,128)(2,1)S(1)}, bf16[288,512]{1,0:T(8,128)(2,1)S(1)}, u32[]{:S(2)}, u32[]{:S(2)}) collective-permute-start(bf16[288,512]{1,0:T(8,128)(2,1)S(1)} %bitcast.31), channel_id=1, source_target_pairs={{0,8},{1,33},{2,10},{3,35},{4,12},{5,37},{6,14},{7,39},{8,0},{9,41... | collective-permute-start | bytes 884744 | tf_op jit(solution)/shard_map/ppermute | solution.py:44
  17.2 8.4 %collective-permute-start.5 = (bf16[288,512]{1,0:T(8,128)(2,1)S(1)}, bf16[288,512]{1,0:T(8,128)(2,1)S(1)}, u32[]{:S(2)}, u32[]{:S(2)}) collective-permute-start(bf16[288,512]{1,0:T(8,128)(2,1)S(1)} %bitcast.32), channel_id=1, source_target_pairs={{0,12},{1,49},{2,14},{3,51},{4,0},{5,53},{6,2},{7,55},{8,4},{9,57}... | collective-permute-start | bytes 884744 | tf_op jit(solution)/shard_map/ppermute | solution.py:44
  25.7 10.7 %collective-permute-start.9 = (bf16[2,288,512]{2,1,0:T(8,128)(2,1)S(1)}, bf16[2,288,512]{2,1,0:T(8,128)(2,1)S(1)}, u32[]{:S(2)}, u32[]{:S(2)}) collective-permute-start(bf16[2,288,512]{2,1,0:T(8,128)(2,1)S(1)} %maximum_select_fusion), channel_id=1, source_target_pairs={{0,32},{1,9},{2,34},{3,11},{4,36},{5,13},{6,38},{7,15},{8,40},{9,1... | collective-permute-start | bytes 1769480 | tf_op jit(solution)/shard_map/ppermute | solution.py:44
  26.8 19.4 %collective-permute-start.16 = (bf16[2,288,512]{2,1,0:T(8,128)(2,1)S(1)}, bf16[2,288,512]{2,1,0:T(8,128)(2,1)S(1)}, u32[]{:S(2)}, u32[]{:S(2)}) collective-permute-start(bf16[2,288,512]{2,1,0:T(8,128)(2,1)S(1)} %maximum_select_fusion), channel_id=1, source_target_pairs={{0,16},{1,5},{2,18},{3,7},{4,20},{5,9},{6,22},{7,11},{8,24},{9,13}... | collective-permute-start | bytes 1769480 | tf_op jit(solution)/shard_map/ppermute | solution.py:44
  28.6 19.9 %collective-permute-start.15 = (bf16[2,288,512]{2,1,0:T(8,128)(2,1)S(1)}, bf16[2,288,512]{2,1,0:T(8,128)(2,1)S(1)}, u32[]{:S(2)}, u32[]{:S(2)}) collective-permute-start(bf16[2,288,512]{2,1,0:T(8,128)(2,1)S(1)} %maximum_select_fusion), channel_id=1, source_target_pairs={{0,48},{1,13},{2,50},{3,15},{4,52},{5,1},{6,54},{7,3},{8,56},{9,5}... | collective-permute-start | bytes 1769480 | tf_op jit(solution)/shard_map/ppermute | solution.py:44
  28.6 27.1 %collective-permute-start.8 = (bf16[4,288,512]{2,1,0:T(8,128)(2,1)S(1)}, bf16[4,288,512]{2,1,0:T(8,128)(2,1)S(1)}, u32[]{:S(2)}, u32[]{:S(2)}) collective-permute-start(bf16[4,288,512]{2,1,0:T(8,128)(2,1)S(1)} %get-tuple-element.50), channel_id=1, source_target_pairs={{0,4},{1,17},{2,6},{3,19},{4,8},{5,21},{6,10},{7,23},{8,12},{9,25}... | collective-permute-start | bytes 3538952 | tf_op jit(solution)/shard_map/ppermute | solution.py:44
  29.5 41.6 %collective-permute-start.11 = (bf16[4,288,512]{2,1,0:T(8,128)(2,1)S(1)}, bf16[4,288,512]{2,1,0:T(8,128)(2,1)S(1)}, u32[]{:S(2)}, u32[]{:S(2)}) collective-permute-start(bf16[4,288,512]{2,1,0:T(8,128)(2,1)S(1)} %get-tuple-element.56), channel_id=1, source_target_pairs={{0,12},{1,49},{2,14},{3,51},{4,0},{5,53},{6,2},{7,55},{8,4},{9,57}... | collective-permute-start | bytes 3538952 | tf_op jit(solution)/shard_map/ppermute | solution.py:44
  36.4 34.8 %collective-permute-start.10 = (bf16[4,288,512]{2,1,0:T(8,128)(2,1)S(1)}, bf16[4,288,512]{2,1,0:T(8,128)(2,1)S(1)}, u32[]{:S(2)}, u32[]{:S(2)}) collective-permute-start(bf16[4,288,512]{2,1,0:T(8,128)(2,1)S(1)} %get-tuple-element.55), channel_id=1, source_target_pairs={{0,8},{1,33},{2,10},{3,35},{4,12},{5,37},{6,14},{7,39},{8,0},{9,41... | collective-permute-start | bytes 3538952 | tf_op jit(solution)/shard_map/ppermute | solution.py:44
  48.7 35.9 %collective-permute-start.17 = (bf16[3,288,512]{2,1,0:T(8,128)(2,1)S(1)}, bf16[3,288,512]{2,1,0:T(8,128)(2,1)}, u32[]{:S(2)}, u32[]{:S(2)}) collective-permute-start(bf16[3,288,512]{2,1,0:T(8,128)(2,1)S(1)} %pad_maximum_fusion.1.rest_1_), channel_id=1, source_target_pairs={{0,194},{1,195},{2,192},{3,193},{4,198},{5,199},{6,196},{7,197},{8... | collective-permute-start | bytes 2654216 | tf_op jit(solution)/shard_map/ppermute | solution.py:44
  52.6 31.9 %collective-permute-start.18 = (bf16[3,288,512]{2,1,0:T(8,128)(2,1)S(1)}, bf16[3,288,512]{2,1,0:T(8,128)(2,1)}, u32[]{:S(2)}, u32[]{:S(2)}) collective-permute-start(bf16[3,288,512]{2,1,0:T(8,128)(2,1)S(1)} %pad_maximum_fusion.2.rest_2_), channel_id=1, source_target_pairs={{0,64},{1,65},{2,66},{3,67},{4,68},{5,69},{6,70},{7,71},{8,72},{9,... | collective-permute-start | bytes 2654216 | tf_op jit(solution)/shard_map/ppermute | solution.py:44
  72.9 5.9 %collective-permute-start.12 = (bf16[288,512]{1,0:T(8,128)(2,1)S(1)}, bf16[288,512]{1,0:T(8,128)(2,1)S(1)}, u32[]{:S(2)}, u32[]{:S(2)}) collective-permute-start(bf16[288,512]{1,0:T(8,128)(2,1)S(1)} %get-tuple-element.58), channel_id=1, source_target_pairs={{0,16},{1,5},{2,18},{3,7},{4,20},{5,9},{6,22},{7,11},{8,24},{9,13}... | collective-permute-start | bytes 884744 | tf_op jit(solution)/shard_map/ppermute | solution.py:44
  73.4 7.2 %collective-permute-start.13 = (bf16[288,512]{1,0:T(8,128)(2,1)S(1)}, bf16[288,512]{1,0:T(8,128)(2,1)S(1)}, u32[]{:S(2)}, u32[]{:S(2)}) collective-permute-start(bf16[288,512]{1,0:T(8,128)(2,1)S(1)} %get-tuple-element.59), channel_id=1, source_target_pairs={{0,32},{1,9},{2,34},{3,11},{4,36},{5,13},{6,38},{7,15},{8,40},{9,1... | collective-permute-start | bytes 884744 | tf_op jit(solution)/shard_map/ppermute | solution.py:44
  74.8 8.9 %collective-permute-start.14 = (bf16[288,512]{1,0:T(8,128)(2,1)S(1)}, bf16[288,512]{1,0:T(8,128)(2,1)S(1)}, u32[]{:S(2)}, u32[]{:S(2)}) collective-permute-start(bf16[288,512]{1,0:T(8,128)(2,1)S(1)} %get-tuple-element.60), channel_id=1, source_target_pairs={{0,48},{1,13},{2,50},{3,15},{4,52},{5,1},{6,54},{7,3},{8,56},{9,5}... | collective-permute-start | bytes 884744 | tf_op jit(solution)/shard_map/ppermute | solution.py:44
  84.5 8.3 %collective-permute-start.19 = (bf16[4,288,512]{2,1,0:T(8,128)(2,1)S(1)}, bf16[4,288,512]{2,1,0:T(8,128)(2,1)}, u32[]{:S(2)}, u32[]{:S(2)}) collective-permute-start(bf16[4,288,512]{2,1,0:T(8,128)(2,1)S(1)} %pad_maximum_fusion.rest_0_), channel_id=1, source_target_pairs={{0,1},{1,0},{2,3},{3,2},{4,5},{5,4},{6,7},{7,6},{8,9},{9,8},{10,11... | collective-permute-start | bytes 3538952 | tf_op jit(solution)/shard_map/ppermute | solution.py:44
  84.5 7.8 %collective-permute-start.20 = (bf16[3,288,512]{2,1,0:T(8,128)(2,1)S(1)}, bf16[3,288,512]{2,1,0:T(8,128)(2,1)}, u32[]{:S(2)}, u32[]{:S(2)}) collective-permute-start(bf16[3,288,512]{2,1,0:T(8,128)(2,1)S(1)} %pad_maximum_fusion.1.rest_1_), channel_id=1, source_target_pairs={{0,1},{1,0},{2,3},{3,2},{4,5},{5,4},{6,7},{7,6},{8,9},{9,8},{10,11... | collective-permute-start | bytes 2654216 | tf_op jit(solution)/shard_map/ppermute | solution.py:44
  85.0 7.5 %collective-permute-start.21 = (bf16[3,288,512]{2,1,0:T(8,128)(2,1)S(1)}, bf16[3,288,512]{2,1,0:T(8,128)(2,1)}, u32[]{:S(2)}, u32[]{:S(2)}) collective-permute-start(bf16[3,288,512]{2,1,0:T(8,128)(2,1)S(1)} %pad_maximum_fusion.2.rest_2_), channel_id=1, source_target_pairs={{0,1},{1,0},{2,3},{3,2},{4,5},{5,4},{6,7},{7,6},{8,9},{9,8},{10,11... | collective-permute-start | bytes 2654216 | tf_op jit(solution)/shard_map/ppermute | solution.py:44
  85.1 7.4 %collective-permute-start.22 = (bf16[3,288,512]{2,1,0:T(8,128)(2,1)}, bf16[3,288,512]{2,1,0:T(8,128)(2,1)}, u32[]{:S(2)}, u32[]{:S(2)}) collective-permute-start(bf16[3,288,512]{2,1,0:T(8,128)(2,1)} %collective-permute-done.17.rest_3_), channel_id=1, source_target_pairs={{0,1},{1,0},{2,3},{3,2},{4,5},{5,4},{6,7},{7,6},{8,9},{9,8},{10,11... | collective-permute-start | bytes 2654216 | tf_op jit(solution)/shard_map/ppermute | solution.py:44
  85.6 7.2 %collective-permute-start.23 = (bf16[3,288,512]{2,1,0:T(8,128)(2,1)}, bf16[3,288,512]{2,1,0:T(8,128)(2,1)}, u32[]{:S(2)}, u32[]{:S(2)}) collective-permute-start(bf16[3,288,512]{2,1,0:T(8,128)(2,1)} %collective-permute-done.18.rest_4_), channel_id=1, source_target_pairs={{0,1},{1,0},{2,3},{3,2},{4,5},{5,4},{6,7},{7,6},{8,9},{9,8},{10,11... | collective-permute-start | bytes 2654216 | tf_op jit(solution)/shard_map/ppermute | solution.py:44
  85.7 19.1 %all-to-all-start = ((bf16[16,72,128]{2,1,0:T(8,128)(2,1)}), bf16[16,72,128]{2,1,0:T(8,128)(2,1)S(1)}, u32[]{:S(2)}, u32[]{:S(2)}) async-start(bf16[16,72,128]{2,1,0:T(8,128)(2,1)} %shard_map.61), calls=%async_computation | async-start | bytes 589824 | tf_op jit(solution)/shard_map/all_to_all | solution.py:355
  104.8 9.2 %collective-permute-start.26 = (f32[2,72,128]{2,1,0:T(8,128)S(1)}, f32[2,72,128]{2,1,0:T(8,128)S(1)}, u32[]{:S(2)}, u32[]{:S(2)}) collective-permute-start(f32[2,72,128]{2,1,0:T(8,128)S(1)} %convert_reduce_fusion), channel_id=1, source_target_pairs={{0,64},{1,65},{2,66},{3,67},{4,68},{5,69},{6,70},{7,71},{8,72},{9,... | collective-permute-start | bytes 221192 | tf_op jit(solution)/shard_map/ppermute | solution.py:44
  106.0 8.0 %collective-permute-start.25 = (f32[2,72,128]{2,1,0:T(8,128)S(1)}, f32[2,72,128]{2,1,0:T(8,128)S(1)}, u32[]{:S(2)}, u32[]{:S(2)}) collective-permute-start(f32[2,72,128]{2,1,0:T(8,128)S(1)} %convert_reduce_fusion), channel_id=1, source_target_pairs={{0,128},{1,129},{2,130},{3,131},{4,132},{5,133},{6,134},{7,135},{8... | collective-permute-start | bytes 221192 | tf_op jit(solution)/shard_map/ppermute | solution.py:44
  107.2 4.9 %collective-permute-start.24 = (f32[2,72,128]{2,1,0:T(8,128)S(1)}, f32[2,72,128]{2,1,0:T(8,128)S(1)}, u32[]{:S(2)}, u32[]{:S(2)}) collective-permute-start(f32[2,72,128]{2,1,0:T(8,128)S(1)} %convert_reduce_fusion), channel_id=1, source_target_pairs={{0,192},{1,193},{2,194},{3,195},{4,196},{5,197},{6,198},{7,199},{8... | collective-permute-start | bytes 221192 | tf_op jit(solution)/shard_map/ppermute | solution.py:44

commit v4 on v3

--- a/solution.py
+++ b/solution.py
@@ -227,56 +227,65 @@
 
 
 def product_kernel(at_ref, x_ref, g_ref, *rest):
-    sides, (keys_ref, grad_ref, w, total, sem) = (rest[:5], rest[5:10]), rest[10:]
+    sides, (keys_ref, grad_ref, w, x, g, total, sem, x_sem, g_sem) = (rest[:5], rest[5:10]), rest[10:]
     step, core = pl.program_id(0), at_ref[2]
     x_at, y_at = jnp.where(core == 0, at_ref[0], at_ref[1]), jnp.where(core == 0, at_ref[1], at_ref[0])
-    turn = 2 * lax.rem(at_ref[3], 2)
-
-    def copy(source, y, x, side, i, m):
-        y, x = lax.rem(y_at + y, 4), lax.rem(x_at + x, 4)
-        rows = pl.ds(pl.multiple_of((4 * y + x) * BLK, BLK), BLK)
+    turn = 2 * (at_ref[3] & 1)
+
+    def quarter(i):
+        return pl.ds(pl.multiple_of(((y_at + turn + i) & 3) * ROWS, ROWS), ROWS)
+
+    def fetch(i):
+        return pltpu.make_async_copy(x_ref.at[:, quarter(i)], x.at[:, quarter(i)], x_sem.at[i])
+
+    def copy(source, dy, dx, side, i):
+        block = 4 * ((y_at + dy) & 3) + ((x_at + dx) & 3)
+        rows = pl.ds(pl.multiple_of(block * BLK, BLK), BLK)
         columns = slice(side * HALF, (side + 1) * HALF)
-        return pltpu.make_async_copy(source, w.at[rows, columns], sem.at[side, i, m])
+        return pltpu.make_async_copy(source, w.at[rows, columns], sem.at[side, i])
 
     def start(side, line, parts, i):
-        ahead = lax.rem(turn + i, 4)
+        ahead = (turn + i) & 3
         if side == 1:
-            copy(line.at[ahead], ahead, 0, side, i, 0).start()
+            copy(line.at[ahead], ahead, 0, side, i).start()
             for m in range(1, 4):
-                copy(parts[i].at[m - 1], ahead, m, side, i, m).start()
+                copy(parts[i].at[m - 1], ahead, m, side, i).start()
             return
 
         @pl.when(ahead == 0)
         def _():
             for m in range(4):
-                copy(line.at[m], 0, m, side, i, m).start()
+                copy(line.at[m], 0, m, side, i).start()
 
         @pl.when(ahead != 0)
         def _():
             for m in range(4):
-                copy(parts[m].at[jnp.maximum(ahead - 1, 0)], ahead, turn + m, side, i, m).start()
-
-    for i in range(4):
-        for own in range(2):
-
-            @pl.when((step == max(i - 1, 0)) & (core == own))
-            def _():
-                for side in range(2):
-                    mine = sides[0 if side == own else 1]
-                    start(side, mine[0], mine[1:], i)
+                copy(parts[m].at[jnp.maximum(ahead - 1, 0)], ahead, turn + m, side, i).start()
 
     @pl.when(step == 0)
     def _():
+        pltpu.make_async_copy(g_ref, g, g_sem).start()
+        for own in range(2):
+
+            @pl.when(core == own)
+            def _():
+                for i in range(4):
+                    fetch(i).start()
+                    for side in range(2):
+                        mine = sides[0 if side == own else 1]
+                        start(side, mine[0], mine[1:], i)
+
         total[...] = jnp.zeros_like(total)
-
+        pltpu.make_async_copy(g_ref, g, g_sem).wait()
+
+    fetch(step).wait()
+    rows = quarter(step)
     for side in range(2):
-        for m in range(4):
-            copy(sides[0][0].at[0], 0, 0, side, step, m).wait()
-
-    now = lax.rem(y_at + turn + step, 4)
-    part = w[pl.ds(pl.multiple_of(now * ROWS, ROWS), ROWS), :]
-    total[...] += jnp.dot(x_ref[...], part, preferred_element_type=jnp.float32)
-    grad = lax.dot_general(g_ref[...], part, (((1,), (1,)), ((), ())), preferred_element_type=jnp.float32)
+        part = w.at[rows, side * HALF : (side + 1) * HALF]
+        pltpu.make_async_copy(part, part, sem.at[side, step]).wait()
+    part = w[rows, :]
+    total[...] += jnp.dot(x[:, rows], part, preferred_element_type=jnp.float32)
+    grad = lax.dot_general(g[...], part, (((1,), (1,)), ((), ())), preferred_element_type=jnp.float32)
     grad_ref[...] = grad.astype(grad_ref.dtype)
 
     @pl.when(step == pl.num_programs(0) - 1)
@@ -295,13 +304,16 @@
         grid_spec=pltpu.PrefetchScalarGridSpec(
             num_scalar_prefetch=1,
             grid=(4,),
-            in_specs=[pl.BlockSpec((TOK, ROWS), across), pl.BlockSpec((TOK, KD), whole)]
-            + [pl.BlockSpec(memory_space=pl.ANY)] * 10,
+            in_specs=[pl.BlockSpec(memory_space=pl.ANY)] * 12,
             out_specs=[pl.BlockSpec((TOK, KD), whole), pl.BlockSpec((TOK, ROWS), across)],
             scratch_shapes=[
                 pltpu.VMEM((D, KD), jnp.bfloat16),
+                pltpu.VMEM((TOK, D), jnp.bfloat16),
+                pltpu.VMEM((TOK, KD), jnp.bfloat16),
                 pltpu.VMEM((TOK, KD), jnp.float32),
-                pltpu.SemaphoreType.DMA((2, 4, 4)),
+                pltpu.SemaphoreType.DMA((2, 4)),
+                pltpu.SemaphoreType.DMA((4,)),
+                pltpu.SemaphoreType.DMA,
             ],
         ),
         out_shape=[jax.ShapeDtypeStruct((TOK, KD), jnp.bfloat16), jax.ShapeDtypeStruct((TOK, D), jnp.bfloat16)],
@@ -348,8 +360,8 @@
 
     sums = sum_blocks(at, [out[0], got1, got2, got3])
     column = [sums[0]] + [send(sums[j], second_by(j)) for j in (1, 2, 3)]
+    column[1], line, parts = barrier((column[1], line, parts))
     units = unit_sums(column)
-    units, line, parts = barrier((units, line, parts))
     swapped = [send(p, other_core) for p in [line] + parts]
     keys, input_grad = products(at, normed, key_grad, [line] + parts, swapped)
     units = lax.all_to_all(units, ("zh", "zl", "c"), 0, 0, tiled=True)

time: 116 us -> 114 us (0.983)
  Pallas kernels: 22.6 us -> 21.2 us
    all_to_all x1, waiting for transfers between devices: 0.81 us -> 2.57 us  [local(): units = lax.all_to_all(units, ('zh', 'zl', 'c'), 0, 0, tiled=True)]
    pallas_call x1, Pallas kernels: 11.1 us -> 9.74 us  [products(): pl.pallas_call(product_kernel, grid_spec=pltpu.PrefetchScalarGridSpec(num...]
    ppermute x27, starting transfers between devices: 26.8 us -> 25.6 us  [send(): return lax.ppermute(value, AXES, pairs(move))]
  transfers between devices with their start and end apart: 28 -> 28, of which waited for: 14 -> 12; matrix products, arithmetic and copies ran while one was open for 3% -> 3% of each run, Pallas kernels for 20% -> 19%
where the time goes in v4:
time: 114 us; the launch traced here: 113 us
  waiting for transfers between devices  52.8 us (46%)
  starting transfers between devices  32.4 us (28%)
  Pallas kernels  21.2 us (19%)
  local copies, waits for them, and re-layouts  5.44 us (5%)
    ppermute x27, waiting for transfers between devices, send(): return lax.ppermute(value, AXES, pairs(move))  50.2 us
    ppermute x27, starting transfers between devices, send(): return lax.ppermute(value, AXES, pairs(move))  25.6 us
    pallas_call x1, Pallas kernels, products(): pl.pallas_call(product_kernel, grid_spec=pltpu.PrefetchScalarGridSpec(num...  9.74 us
    all_to_all x1, starting transfers between devices, local(): units = lax.all_to_all(units, ('zh', 'zl', 'c'), 0, 0, tiled=True)  6.81 us
    pallas_call x1, Pallas kernels, partial_blocks(): pl.pallas_call(partial_kernel, grid_spec=pltpu.PrefetchScalarGridSpec(num...  6.44 us
    dynamic_slice x2, local copies, waits for them, and re-layouts, half(): return lax.dynamic_slice_in_dim(a, which * HALF, HALF, axis=1)  2.63 us
    all_to_all x1, waiting for transfers between devices, local(): units = lax.all_to_all(units, ('zh', 'zl', 'c'), 0, 0, tiled=True)  2.57 us
    pallas_call x1, Pallas kernels, quantize(): pl.pallas_call(quantize_kernel, grid=(D // width,), in_specs=[pl.BlockSpe...  2.46 us
  transfers between devices with their start and end apart: 28, of which 12 were waited for; matrix products, arithmetic and copies ran while one was open for 3% of the time, Pallas kernels for 19%

profile of v4, /device:TPU:31, one launch (start us, length us, event | category | flops | bytes accessed | tf_op | source)
XLA Modules:
  0.0 113.4 jit_solution(12989091463032468115)
XLA Ops:
  0.6 0.8 collective-permute-start
  1.4 1.6 %constant_dynamic-slice_fusion.3 = (bf16[72,512]{1,0:T(8,128)(2,1)S(1)}, bf16[72,512]{1,0:T(8,128)(2,1)}) fusion(bf16[72,1024]{1,0:T(8,128)(2,1)} %param.4, s32[]{:T(128)S(6)} %select_n.54, s32[]{:T(128)S(6)} %select_n.55), kind=kLoop, calls=%fused_computation.20 | loop fusion | bytes 294920 | tf_op jit(solution)/shard_map/dynamic_slice | solution.py:331
  3.0 5.5 %collective-permute-start.3 = (bf16[72,512]{1,0:T(8,128)(2,1)}, bf16[72,512]{1,0:T(8,128)(2,1)S(1)}, u32[]{:S(2)}, u32[]{:S(2)}) collective-permute-start(bf16[72,512]{1,0:T(8,128)(2,1)} %get-tuple-element.82), channel_id=1, source_target_pairs={{0,195},{1,194},{2,193},{3,192},{4,199},{5,198},{6,197},{7,196},{8... | collective-permute-start | bytes 221192 | tf_op jit(solution)/shard_map/ppermute | solution.py:44
  8.9 1.1 constant_dynamic-slice_fusion
  10.5 1.7 %copy-done = bf16[256,4608]{1,0:T(8,128)(2,1)S(1)} copy-done((bf16[256,4608]{1,0:T(8,128)(2,1)S(1)}, bf16[256,4608]{1,0:T(8,128)(2,1)}, u32[]{:S(2)}) %copy-start) | copy-done | bytes 2359320
  12.1 2.5 %shard_map.58.mine_ref = bf16[4608,256]{1,0:T(8,128)(2,1)S(1)} custom-call(bf16[256,4608]{1,0:T(8,128)(2,1)S(1)} %copy-done), custom_call_target="tpu_custom_call" | custom-call | flops 1207959552 | bytes 4718592 | tf_op jit(solution)/shard_map/pallas_call | solution.py:111
  15.0 2.2 %collective-permute-start.6 = (bf16[288,512]{1,0:T(8,128)(2,1)S(1)}, bf16[288,512]{1,0:T(8,128)(2,1)S(1)}, u32[]{:S(2)}, u32[]{:S(2)}) collective-permute-start(bf16[288,512]{1,0:T(8,128)(2,1)S(1)} %bitcast.31), channel_id=1, source_target_pairs={{0,8},{1,33},{2,10},{3,35},{4,12},{5,37},{6,14},{7,39},{8,0},{9,41... | collective-permute-start | bytes 884744 | tf_op jit(solution)/shard_map/ppermute | solution.py:44
  17.2 6.4 %shard_map.59 = (bf16[4,288,512]{2,1,0:T(8,128)(2,1)S(1)}, bf16[4,288,512]{2,1,0:T(8,128)(2,1)S(1)}, bf16[4,288,512]{2,1,0:T(8,128)(2,1)S(1)}, bf16[4,288,512]{2,1,0:T(8,128)(2,1)S(1)}) custom-call(s32[4]{0:T(128)S(1)} %pad_add_fusion.at_ref, bf16[4608,256]{1,0:T(8,128)(2,1)S(1)} %shard_map.58.mine_ref, ...), custom_call_target="tpu_custom_call" | custom-call | flops 7247757312 | bytes 10485760 | tf_op jit(solution)/shard_map/pallas_call | solution.py:163
  23.7 1.9 %collective-permute-done.5 = bf16[288,512]{1,0:T(8,128)(2,1)S(1)} collective-permute-done((bf16[288,512]{1,0:T(8,128)(2,1)S(1)}, bf16[288,512]{1,0:T(8,128)(2,1)S(1)}, u32[]{:S(2)}, u32[]{:S(2)}) %collective-permute-start.5) | collective-permute-done | bytes 294944 | tf_op jit(solution)/shard_map/ppermute | solution.py:44
  25.7 1.1 collective-permute-start.9
  26.8 1.8 %collective-permute-start.14 = (bf16[2,288,512]{2,1,0:T(8,128)(2,1)S(1)}, bf16[2,288,512]{2,1,0:T(8,128)(2,1)S(1)}, u32[]{:S(2)}, u32[]{:S(2)}) collective-permute-start(bf16[2,288,512]{2,1,0:T(8,128)(2,1)S(1)} %maximum_select_fusion), channel_id=1, source_target_pairs={{0,16},{1,5},{2,18},{3,7},{4,20},{5,9},{6,22},{7,11},{8,24},{9,13}... | collective-permute-start | bytes 1769480 | tf_op jit(solution)/shard_map/ppermute | solution.py:44
  28.6 0.9 collective-permute-start.8
  30.1 6.3 %collective-permute-done.9 = bf16[2,288,512]{2,1,0:T(8,128)(2,1)S(1)} collective-permute-done((bf16[2,288,512]{2,1,0:T(8,128)(2,1)S(1)}, bf16[2,288,512]{2,1,0:T(8,128)(2,1)S(1)}, u32[]{:S(2)}, u32[]{:S(2)}) %collective-permute-start.9) | collective-permute-done | bytes 589856 | tf_op jit(solution)/shard_map/ppermute | solution.py:44
  36.4 1.2 %collective-permute-start.10 = (bf16[4,288,512]{2,1,0:T(8,128)(2,1)S(1)}, bf16[4,288,512]{2,1,0:T(8,128)(2,1)S(1)}, u32[]{:S(2)}, u32[]{:S(2)}) collective-permute-start(bf16[4,288,512]{2,1,0:T(8,128)(2,1)S(1)} %get-tuple-element.55), channel_id=1, source_target_pairs={{0,8},{1,33},{2,10},{3,35},{4,12},{5,37},{6,14},{7,39},{8,0},{9,41... | collective-permute-start | bytes 3538952 | tf_op jit(solution)/shard_map/ppermute | solution.py:44
  37.7 8.5 %collective-permute-done.14 = bf16[2,288,512]{2,1,0:T(8,128)(2,1)S(1)} collective-permute-done((bf16[2,288,512]{2,1,0:T(8,128)(2,1)S(1)}, bf16[2,288,512]{2,1,0:T(8,128)(2,1)S(1)}, u32[]{:S(2)}, u32[]{:S(2)}) %collective-permute-start.14) | collective-permute-done | bytes 589856 | tf_op jit(solution)/shard_map/ppermute | solution.py:44
  46.2 2.3 %collective-permute-done.13 = bf16[2,288,512]{2,1,0:T(8,128)(2,1)S(1)} collective-permute-done((bf16[2,288,512]{2,1,0:T(8,128)(2,1)S(1)}, bf16[2,288,512]{2,1,0:T(8,128)(2,1)S(1)}, u32[]{:S(2)}, u32[]{:S(2)}) %collective-permute-start.13) | collective-permute-done | bytes 589856 | tf_op jit(solution)/shard_map/ppermute | solution.py:44
  48.7 3.8 %collective-permute-start.15 = (bf16[3,288,512]{2,1,0:T(8,128)(2,1)S(1)}, bf16[3,288,512]{2,1,0:T(8,128)(2,1)}, u32[]{:S(2)}, u32[]{:S(2)}) collective-permute-start(bf16[3,288,512]{2,1,0:T(8,128)(2,1)S(1)} %pad_maximum_fusion.1.rest_1_), channel_id=1, source_target_pairs={{0,194},{1,195},{2,192},{3,193},{4,198},{5,199},{6,196},{7,197},{8... | collective-permute-start | bytes 2654216 | tf_op jit(solution)/shard_map/ppermute | solution.py:44
  52.7 3.0 %collective-permute-done.8.b = bf16[4,288,512]{2,1,0:T(8,128)(2,1)S(1)} collective-permute-done((bf16[4,288,512]{2,1,0:T(8,128)(2,1)S(1)}, bf16[4,288,512]{2,1,0:T(8,128)(2,1)S(1)}, u32[]{:S(2)}, u32[]{:S(2)}) %collective-permute-start.8) | collective-permute-done | bytes 1179680 | tf_op jit(solution)/shard_map/ppermute | solution.py:44
  55.7 15.5 %collective-permute-done.11.d = bf16[4,288,512]{2,1,0:T(8,128)(2,1)S(1)} collective-permute-done((bf16[4,288,512]{2,1,0:T(8,128)(2,1)S(1)}, bf16[4,288,512]{2,1,0:T(8,128)(2,1)S(1)}, u32[]{:S(2)}, u32[]{:S(2)}) %collective-permute-start.11) | collective-permute-done | bytes 1179680 | tf_op jit(solution)/shard_map/ppermute | solution.py:44
  71.2 1.7 %shard_map.60 = (f32[288,512]{1,0:T(8,128)S(1)}, bf16[288,512]{1,0:T(8,128)(2,1)S(1)}, bf16[288,512]{1,0:T(8,128)(2,1)S(1)}, bf16[288,512]{1,0:T(8,128)(2,1)S(1)}) custom-call(s32[4]{0:T(128)S(1)} %pad_add_fusion.at_ref, bf16[4,288,512]{2,1,0:T(8,128)(2,1)S(1)} %get-tuple-element.49.a, bf16[4,288,512]{2,1,0:T(8,128)(2,1)S(1)} %collective-permute-done.8.b, ...), custom_call_target="tpu_custom_call" | custom-call | bytes 6291456 | tf_op jit(solution)/shard_map/pallas_call | solution.py:193
  73.6 1.4 %collective-permute-start.17 = (bf16[288,512]{1,0:T(8,128)(2,1)S(1)}, bf16[288,512]{1,0:T(8,128)(2,1)S(1)}, u32[]{:S(2)}, u32[]{:S(2)}) collective-permute-start(bf16[288,512]{1,0:T(8,128)(2,1)S(1)} %get-tuple-element.61), channel_id=1, source_target_pairs={{0,32},{1,9},{2,34},{3,11},{4,36},{5,13},{6,38},{7,15},{8,40},{9,1... | collective-permute-start | bytes 884744 | tf_op jit(solution)/shard_map/ppermute | solution.py:44
  75.7 3.1 %collective-permute-done.12.b = bf16[288,512]{1,0:T(8,128)(2,1)S(1)} collective-permute-done((bf16[288,512]{1,0:T(8,128)(2,1)S(1)}, bf16[288,512]{1,0:T(8,128)(2,1)S(1)}, u32[]{:S(2)}, u32[]{:S(2)}) %collective-permute-start.12) | collective-permute-done | bytes 294944 | tf_op jit(solution)/shard_map/ppermute | solution.py:44
  79.4 1.5 %collective-permute-done.17.c = bf16[288,512]{1,0:T(8,128)(2,1)S(1)} collective-permute-done((bf16[288,512]{1,0:T(8,128)(2,1)S(1)}, bf16[288,512]{1,0:T(8,128)(2,1)S(1)}, u32[]{:S(2)}, u32[]{:S(2)}) %collective-permute-start.17) | collective-permute-done | bytes 294944 | tf_op jit(solution)/shard_map/ppermute | solution.py:44
  80.8 3.1 %collective-permute-done.18.d = bf16[288,512]{1,0:T(8,128)(2,1)S(1)} collective-permute-done((bf16[288,512]{1,0:T(8,128)(2,1)S(1)}, bf16[288,512]{1,0:T(8,128)(2,1)S(1)}, u32[]{:S(2)}, u32[]{:S(2)}) %collective-permute-start.18) | collective-permute-done | bytes 294944 | tf_op jit(solution)/shard_map/ppermute | solution.py:44
  83.9 0.9 shard_map.61
  84.8 6.8 %all-to-all-start = ((bf16[16,72,128]{2,1,0:T(8,128)(2,1)}), bf16[16,72,128]{2,1,0:T(8,128)(2,1)S(1)}, u32[]{:S(2)}, u32[]{:S(2)}) async-start(bf16[16,72,128]{2,1,0:T(8,128)(2,1)} %shard_map.61), calls=%async_computation | async-start | bytes 589824 | tf_op jit(solution)/shard_map/all_to_all | solution.py:367
  91.6 9.7 %shard_map.62 = (bf16[256,1024]{1,0:T(8,128)(2,1)}, bf16[256,4608]{1,0:T(8,128)(2,1)}) custom-call(s32[4]{0:T(128)S(1)} %pad_add_fusion.at_ref, bf16[256,4608]{1,0:T(8,128)(2,1)} %x_ref.3, bf16[256,1024]{1,0:T(8,128)(2,1)} %g_ref.1, bf16[4,288,512]{2,1,0:T(8,128)(2,1)S(1)} %pad_maximum_fusion.rest_0_, bf16[3,288,512]{2,1,0:T(8,128)(2,1)S(1)} %pad_maximum_fusion.1.rest_1_, ...), custom_call_target="tpu_custom_call" | custom-call | flops 4831838208 | bytes 14680064 | tf_op jit(solution)/shard_map/pallas_call | solution.py:302
  101.4 2.6 %all-to-all-done = bf16[16,72,128]{2,1,0:T(8,128)(2,1)S(1)} async-done(((bf16[16,72,128]{2,1,0:T(8,128)(2,1)}), bf16[16,72,128]{2,1,0:T(8,128)(2,1)S(1)}, u32[]{:S(2)}, u32[]{:S(2)}) %all-to-all-start) | async-done | bytes 294944 | tf_op jit(solution)/shard_map/all_to_all | solution.py:367
  104.1 1.1 %collective-permute-start.25 = (f32[2,72,128]{2,1,0:T(8,128)S(1)}, f32[2,72,128]{2,1,0:T(8,128)S(1)}, u32[]{:S(2)}, u32[]{:S(2)}) collective-permute-start(f32[2,72,128]{2,1,0:T(8,128)S(1)} %convert_reduce_fusion), channel_id=1, source_target_pairs={{0,128},{1,129},{2,130},{3,131},{4,132},{5,133},{6,134},{7,135},{8... | collective-permute-start | bytes 221192 | tf_op jit(solution)/shard_map/ppermute | solution.py:44
  105.2 2.1 %collective-permute-start.24 = (f32[2,72,128]{2,1,0:T(8,128)S(1)}, f32[2,72,128]{2,1,0:T(8,128)S(1)}, u32[]{:S(2)}, u32[]{:S(2)}) collective-permute-start(f32[2,72,128]{2,1,0:T(8,128)S(1)} %convert_reduce_fusion), channel_id=1, source_target_pairs={{0,192},{1,193},{2,194},{3,195},{4,196},{5,197},{6,198},{7,199},{8... | collective-permute-start | bytes 221192 | tf_op jit(solution)/shard_map/ppermute | solution.py:44
  107.3 4.4 %collective-permute-done.24 = f32[2,72,128]{2,1,0:T(8,128)S(1)} collective-permute-done((f32[2,72,128]{2,1,0:T(8,128)S(1)}, f32[2,72,128]{2,1,0:T(8,128)S(1)}, u32[]{:S(2)}, u32[]{:S(2)}) %collective-permute-start.24) | collective-permute-done | bytes 73760 | tf_op jit(solution)/shard_map/ppermute | solution.py:44
  112.6 0.8 reshape.20
  (56 shorter events, 5.2 us)
Async XLA Ops:
  0.6 14.3 %collective-permute-start = (bf16[256,4608]{1,0:T(8,128)(2,1)}, bf16[256,4608]{1,0:T(8,128)(2,1)S(1)}, u32[]{:S(2)}, u32[]{:S(2)}) collective-permute-start(bf16[256,4608]{1,0:T(8,128)(2,1)} %x_ref.3), channel_id=1, source_target_pairs={{0,1},{1,0},{2,3},{3,2},{4,5},{5,4},{6,7},{7,6},{8,9},{9,8},{10,11... | collective-permute-start | bytes 7077896 | tf_op jit(solution)/shard_map/ppermute | solution.py:44
  3.0 11.8 %collective-permute-start.3 = (bf16[72,512]{1,0:T(8,128)(2,1)}, bf16[72,512]{1,0:T(8,128)(2,1)S(1)}, u32[]{:S(2)}, u32[]{:S(2)}) collective-permute-start(bf16[72,512]{1,0:T(8,128)(2,1)} %get-tuple-element.82), channel_id=1, source_target_pairs={{0,195},{1,194},{2,193},{3,192},{4,199},{5,198},{6,197},{7,196},{8... | collective-permute-start | bytes 221192 | tf_op jit(solution)/shard_map/ppermute | solution.py:44
  8.4 6.3 %collective-permute-start.1 = (bf16[72,512]{1,0:T(8,128)(2,1)}, bf16[72,512]{1,0:T(8,128)(2,1)S(1)}, u32[]{:S(2)}, u32[]{:S(2)}) collective-permute-start(bf16[72,512]{1,0:T(8,128)(2,1)} %get-tuple-element.82), channel_id=1, source_target_pairs={{0,1},{1,0},{2,3},{3,2},{4,5},{5,4},{6,7},{7,6},{8,9},{9,8},{10,11... | collective-permute-start | bytes 221192 | tf_op jit(solution)/shard_map/ppermute | solution.py:44
  8.9 5.8 %collective-permute-start.2 = (bf16[72,512]{1,0:T(8,128)(2,1)S(1)}, bf16[72,512]{1,0:T(8,128)(2,1)S(1)}, u32[]{:S(2)}, u32[]{:S(2)}) collective-permute-start(bf16[72,512]{1,0:T(8,128)(2,1)S(1)} %get-tuple-element.81), channel_id=1, source_target_pairs={{0,194},{1,195},{2,192},{3,193},{4,198},{5,199},{6,196},{7,197},{8... | collective-permute-start | bytes 221192 | tf_op jit(solution)/shard_map/ppermute | solution.py:44
  10.0 7.2 %collective-permute-start.4 = (bf16[256,512]{1,0:T(8,128)(2,1)S(1)}, bf16[256,512]{1,0:T(8,128)(2,1)S(1)}, u32[]{:S(2)}, u32[]{:S(2)}) collective-permute-start(bf16[256,512]{1,0:T(8,128)(2,1)S(1)} %get-tuple-element.79), channel_id=1, source_target_pairs={{0,1},{1,0},{2,3},{3,2},{4,5},{5,4},{6,7},{7,6},{8,9},{9,8},{10,11... | collective-permute-start | bytes 786440 | tf_op jit(solution)/shard_map/ppermute | solution.py:44
  10.5 1.7 %copy-start = (bf16[256,4608]{1,0:T(8,128)(2,1)S(1)}, bf16[256,4608]{1,0:T(8,128)(2,1)}, u32[]{:S(2)}) copy-start(bf16[256,4608]{1,0:T(8,128)(2,1)} %x_ref.3) | copy-start | bytes 7077892
  14.9 8.8 %collective-permute-start.7 = (bf16[288,512]{1,0:T(8,128)(2,1)S(1)}, bf16[288,512]{1,0:T(8,128)(2,1)S(1)}, u32[]{:S(2)}, u32[]{:S(2)}) collective-permute-start(bf16[288,512]{1,0:T(8,128)(2,1)S(1)} %bitcast.30), channel_id=1, source_target_pairs={{0,4},{1,17},{2,6},{3,19},{4,8},{5,21},{6,10},{7,23},{8,12},{9,25}... | collective-permute-start | bytes 884744 | tf_op jit(solution)/shard_map/ppermute | solution.py:44
  15.0 8.7 %collective-permute-start.6 = (bf16[288,512]{1,0:T(8,128)(2,1)S(1)}, bf16[288,512]{1,0:T(8,128)(2,1)S(1)}, u32[]{:S(2)}, u32[]{:S(2)}) collective-permute-start(bf16[288,512]{1,0:T(8,128)(2,1)S(1)} %bitcast.31), channel_id=1, source_target_pairs={{0,8},{1,33},{2,10},{3,35},{4,12},{5,37},{6,14},{7,39},{8,0},{9,41... | collective-permute-start | bytes 884744 | tf_op jit(solution)/shard_map/ppermute | solution.py:44
  17.2 8.4 %collective-permute-start.5 = (bf16[288,512]{1,0:T(8,128)(2,1)S(1)}, bf16[288,512]{1,0:T(8,128)(2,1)S(1)}, u32[]{:S(2)}, u32[]{:S(2)}) collective-permute-start(bf16[288,512]{1,0:T(8,128)(2,1)S(1)} %bitcast.32), channel_id=1, source_target_pairs={{0,12},{1,49},{2,14},{3,51},{4,0},{5,53},{6,2},{7,55},{8,4},{9,57}... | collective-permute-start | bytes 884744 | tf_op jit(solution)/shard_map/ppermute | solution.py:44
  25.7 10.7 %collective-permute-start.9 = (bf16[2,288,512]{2,1,0:T(8,128)(2,1)S(1)}, bf16[2,288,512]{2,1,0:T(8,128)(2,1)S(1)}, u32[]{:S(2)}, u32[]{:S(2)}) collective-permute-start(bf16[2,288,512]{2,1,0:T(8,128)(2,1)S(1)} %maximum_select_fusion), channel_id=1, source_target_pairs={{0,32},{1,9},{2,34},{3,11},{4,36},{5,13},{6,38},{7,15},{8,40},{9,1... | collective-permute-start | bytes 1769480 | tf_op jit(solution)/shard_map/ppermute | solution.py:44
  26.8 19.4 %collective-permute-start.14 = (bf16[2,288,512]{2,1,0:T(8,128)(2,1)S(1)}, bf16[2,288,512]{2,1,0:T(8,128)(2,1)S(1)}, u32[]{:S(2)}, u32[]{:S(2)}) collective-permute-start(bf16[2,288,512]{2,1,0:T(8,128)(2,1)S(1)} %maximum_select_fusion), channel_id=1, source_target_pairs={{0,16},{1,5},{2,18},{3,7},{4,20},{5,9},{6,22},{7,11},{8,24},{9,13}... | collective-permute-start | bytes 1769480 | tf_op jit(solution)/shard_map/ppermute | solution.py:44
  28.6 19.9 %collective-permute-start.13 = (bf16[2,288,512]{2,1,0:T(8,128)(2,1)S(1)}, bf16[2,288,512]{2,1,0:T(8,128)(2,1)S(1)}, u32[]{:S(2)}, u32[]{:S(2)}) collective-permute-start(bf16[2,288,512]{2,1,0:T(8,128)(2,1)S(1)} %maximum_select_fusion), channel_id=1, source_target_pairs={{0,48},{1,13},{2,50},{3,15},{4,52},{5,1},{6,54},{7,3},{8,56},{9,5}... | collective-permute-start | bytes 1769480 | tf_op jit(solution)/shard_map/ppermute | solution.py:44
  28.6 27.1 %collective-permute-start.8 = (bf16[4,288,512]{2,1,0:T(8,128)(2,1)S(1)}, bf16[4,288,512]{2,1,0:T(8,128)(2,1)S(1)}, u32[]{:S(2)}, u32[]{:S(2)}) collective-permute-start(bf16[4,288,512]{2,1,0:T(8,128)(2,1)S(1)} %get-tuple-element.50), channel_id=1, source_target_pairs={{0,4},{1,17},{2,6},{3,19},{4,8},{5,21},{6,10},{7,23},{8,12},{9,25}... | collective-permute-start | bytes 3538952 | tf_op jit(solution)/shard_map/ppermute | solution.py:44
  29.5 41.6 %collective-permute-start.11 = (bf16[4,288,512]{2,1,0:T(8,128)(2,1)S(1)}, bf16[4,288,512]{2,1,0:T(8,128)(2,1)S(1)}, u32[]{:S(2)}, u32[]{:S(2)}) collective-permute-start(bf16[4,288,512]{2,1,0:T(8,128)(2,1)S(1)} %get-tuple-element.56), channel_id=1, source_target_pairs={{0,12},{1,49},{2,14},{3,51},{4,0},{5,53},{6,2},{7,55},{8,4},{9,57}... | collective-permute-start | bytes 3538952 | tf_op jit(solution)/shard_map/ppermute | solution.py:44
  36.4 34.8 %collective-permute-start.10 = (bf16[4,288,512]{2,1,0:T(8,128)(2,1)S(1)}, bf16[4,288,512]{2,1,0:T(8,128)(2,1)S(1)}, u32[]{:S(2)}, u32[]{:S(2)}) collective-permute-start(bf16[4,288,512]{2,1,0:T(8,128)(2,1)S(1)} %get-tuple-element.55), channel_id=1, source_target_pairs={{0,8},{1,33},{2,10},{3,35},{4,12},{5,37},{6,14},{7,39},{8,0},{9,41... | collective-permute-start | bytes 3538952 | tf_op jit(solution)/shard_map/ppermute | solution.py:44
  48.7 27.1 %collective-permute-start.15 = (bf16[3,288,512]{2,1,0:T(8,128)(2,1)S(1)}, bf16[3,288,512]{2,1,0:T(8,128)(2,1)}, u32[]{:S(2)}, u32[]{:S(2)}) collective-permute-start(bf16[3,288,512]{2,1,0:T(8,128)(2,1)S(1)} %pad_maximum_fusion.1.rest_1_), channel_id=1, source_target_pairs={{0,194},{1,195},{2,192},{3,193},{4,198},{5,199},{6,196},{7,197},{8... | collective-permute-start | bytes 2654216 | tf_op jit(solution)/shard_map/ppermute | solution.py:44
  52.6 23.1 %collective-permute-start.16 = (bf16[3,288,512]{2,1,0:T(8,128)(2,1)S(1)}, bf16[3,288,512]{2,1,0:T(8,128)(2,1)}, u32[]{:S(2)}, u32[]{:S(2)}) collective-permute-start(bf16[3,288,512]{2,1,0:T(8,128)(2,1)S(1)} %pad_maximum_fusion.2.rest_2_), channel_id=1, source_target_pairs={{0,64},{1,65},{2,66},{3,67},{4,68},{5,69},{6,70},{7,71},{8,72},{9,... | collective-permute-start | bytes 2654216 | tf_op jit(solution)/shard_map/ppermute | solution.py:44
  72.9 5.9 %collective-permute-start.12 = (bf16[288,512]{1,0:T(8,128)(2,1)S(1)}, bf16[288,512]{1,0:T(8,128)(2,1)S(1)}, u32[]{:S(2)}, u32[]{:S(2)}) collective-permute-start(bf16[288,512]{1,0:T(8,128)(2,1)S(1)} %get-tuple-element.58), channel_id=1, source_target_pairs={{0,16},{1,5},{2,18},{3,7},{4,20},{5,9},{6,22},{7,11},{8,24},{9,13}... | collective-permute-start | bytes 884744 | tf_op jit(solution)/shard_map/ppermute | solution.py:44
  73.6 7.3 %collective-permute-start.17 = (bf16[288,512]{1,0:T(8,128)(2,1)S(1)}, bf16[288,512]{1,0:T(8,128)(2,1)S(1)}, u32[]{:S(2)}, u32[]{:S(2)}) collective-permute-start(bf16[288,512]{1,0:T(8,128)(2,1)S(1)} %get-tuple-element.61), channel_id=1, source_target_pairs={{0,32},{1,9},{2,34},{3,11},{4,36},{5,13},{6,38},{7,15},{8,40},{9,1... | collective-permute-start | bytes 884744 | tf_op jit(solution)/shard_map/ppermute | solution.py:44
  75.0 8.9 %collective-permute-start.18 = (bf16[288,512]{1,0:T(8,128)(2,1)S(1)}, bf16[288,512]{1,0:T(8,128)(2,1)S(1)}, u32[]{:S(2)}, u32[]{:S(2)}) collective-permute-start(bf16[288,512]{1,0:T(8,128)(2,1)S(1)} %get-tuple-element.62), channel_id=1, source_target_pairs={{0,48},{1,13},{2,50},{3,15},{4,52},{5,1},{6,54},{7,3},{8,56},{9,5}... | collective-permute-start | bytes 884744 | tf_op jit(solution)/shard_map/ppermute | solution.py:44
  78.8 12.8 %collective-permute-start.19 = (bf16[4,288,512]{2,1,0:T(8,128)(2,1)S(1)}, bf16[4,288,512]{2,1,0:T(8,128)(2,1)}, u32[]{:S(2)}, u32[]{:S(2)}) collective-permute-start(bf16[4,288,512]{2,1,0:T(8,128)(2,1)S(1)} %pad_maximum_fusion.rest_0_), channel_id=1, source_target_pairs={{0,1},{1,0},{2,3},{3,2},{4,5},{5,4},{6,7},{7,6},{8,9},{9,8},{10,11... | collective-permute-start | bytes 3538952 | tf_op jit(solution)/shard_map/ppermute | solution.py:44
  78.9 12.7 %collective-permute-start.20 = (bf16[3,288,512]{2,1,0:T(8,128)(2,1)S(1)}, bf16[3,288,512]{2,1,0:T(8,128)(2,1)}, u32[]{:S(2)}, u32[]{:S(2)}) collective-permute-start(bf16[3,288,512]{2,1,0:T(8,128)(2,1)S(1)} %pad_maximum_fusion.1.rest_1_), channel_id=1, source_target_pairs={{0,1},{1,0},{2,3},{3,2},{4,5},{5,4},{6,7},{7,6},{8,9},{9,8},{10,11... | collective-permute-start | bytes 2654216 | tf_op jit(solution)/shard_map/ppermute | solution.py:44
  79.4 12.2 %collective-permute-start.21 = (bf16[3,288,512]{2,1,0:T(8,128)(2,1)S(1)}, bf16[3,288,512]{2,1,0:T(8,128)(2,1)}, u32[]{:S(2)}, u32[]{:S(2)}) collective-permute-start(bf16[3,288,512]{2,1,0:T(8,128)(2,1)S(1)} %pad_maximum_fusion.2.rest_2_), channel_id=1, source_target_pairs={{0,1},{1,0},{2,3},{3,2},{4,5},{5,4},{6,7},{7,6},{8,9},{9,8},{10,11... | collective-permute-start | bytes 2654216 | tf_op jit(solution)/shard_map/ppermute | solution.py:44
  80.8 10.8 %collective-permute-start.22 = (bf16[3,288,512]{2,1,0:T(8,128)(2,1)}, bf16[3,288,512]{2,1,0:T(8,128)(2,1)}, u32[]{:S(2)}, u32[]{:S(2)}) collective-permute-start(bf16[3,288,512]{2,1,0:T(8,128)(2,1)} %collective-permute-done.15.rest_3_), channel_id=1, source_target_pairs={{0,1},{1,0},{2,3},{3,2},{4,5},{5,4},{6,7},{7,6},{8,9},{9,8},{10,11... | collective-permute-start | bytes 2654216 | tf_op jit(solution)/shard_map/ppermute | solution.py:44
  83.9 7.7 %collective-permute-start.23 = (bf16[3,288,512]{2,1,0:T(8,128)(2,1)}, bf16[3,288,512]{2,1,0:T(8,128)(2,1)}, u32[]{:S(2)}, u32[]{:S(2)}) collective-permute-start(bf16[3,288,512]{2,1,0:T(8,128)(2,1)} %collective-permute-done.16.rest_4_), channel_id=1, source_target_pairs={{0,1},{1,0},{2,3},{3,2},{4,5},{5,4},{6,7},{7,6},{8,9},{9,8},{10,11... | collective-permute-start | bytes 2654216 | tf_op jit(solution)/shard_map/ppermute | solution.py:44
  84.8 19.2 %all-to-all-start = ((bf16[16,72,128]{2,1,0:T(8,128)(2,1)}), bf16[16,72,128]{2,1,0:T(8,128)(2,1)S(1)}, u32[]{:S(2)}, u32[]{:S(2)}) async-start(bf16[16,72,128]{2,1,0:T(8,128)(2,1)} %shard_map.61), calls=%async_computation | async-start | bytes 589824 | tf_op jit(solution)/shard_map/all_to_all | solution.py:367
  104.0 8.3 %collective-permute-start.26 = (f32[2,72,128]{2,1,0:T(8,128)S(1)}, f32[2,72,128]{2,1,0:T(8,128)S(1)}, u32[]{:S(2)}, u32[]{:S(2)}) collective-permute-start(f32[2,72,128]{2,1,0:T(8,128)S(1)} %convert_reduce_fusion), channel_id=1, source_target_pairs={{0,64},{1,65},{2,66},{3,67},{4,68},{5,69},{6,70},{7,71},{8,72},{9,... | collective-permute-start | bytes 221192 | tf_op jit(solution)/shard_map/ppermute | solution.py:44
  104.1 8.2 %collective-permute-start.25 = (f32[2,72,128]{2,1,0:T(8,128)S(1)}, f32[2,72,128]{2,1,0:T(8,128)S(1)}, u32[]{:S(2)}, u32[]{:S(2)}) collective-permute-start(f32[2,72,128]{2,1,0:T(8,128)S(1)} %convert_reduce_fusion), channel_id=1, source_target_pairs={{0,128},{1,129},{2,130},{3,131},{4,132},{5,133},{6,134},{7,135},{8... | collective-permute-start | bytes 221192 | tf_op jit(solution)/shard_map/ppermute | solution.py:44
  105.2 6.5 %collective-permute-start.24 = (f32[2,72,128]{2,1,0:T(8,128)S(1)}, f32[2,72,128]{2,1,0:T(8,128)S(1)}, u32[]{:S(2)}, u32[]{:S(2)}) collective-permute-start(f32[2,72,128]{2,1,0:T(8,128)S(1)} %convert_reduce_fusion), channel_id=1, source_target_pairs={{0,192},{1,193},{2,194},{3,195},{4,196},{5,197},{6,198},{7,199},{8... | collective-permute-start | bytes 221192 | tf_op jit(solution)/shard_map/ppermute | solution.py:44

commit v5 on v4

--- a/solution.py
+++ b/solution.py
@@ -359,8 +359,9 @@
     parts = [far_a, far_b, send(far_a, z_by(-1)), send(far_b, z_by(1))]
 
     sums = sum_blocks(at, [out[0], got1, got2, got3])
-    column = [sums[0]] + [send(sums[j], second_by(j)) for j in (1, 2, 3)]
-    column[1], line, parts = barrier((column[1], line, parts))
+    far_sum = send(sums[2], second_by(2))
+    far_sum, line, parts = barrier((far_sum, line, parts))
+    column = [sums[0], far_sum, send(sums[1], second_by(1)), send(sums[3], second_by(3))]
     units = unit_sums(column)
     swapped = [send(p, other_core) for p in [line] + parts]
     keys, input_grad = products(at, normed, key_grad, [line] + parts, swapped)

time: 114 us -> 114 us (level)
  waiting for transfers between devices: 52.8 us -> 51.5 us
    ppermute x27, waiting for transfers between devices: 50.2 us -> 48.9 us  [send(): return lax.ppermute(value, AXES, pairs(move))]
where the time goes in v5:
time: 114 us; the launch traced here: 113 us
  waiting for transfers between devices  51.5 us (45%)
  starting transfers between devices  33 us (29%)
  Pallas kernels  21.2 us (19%)
  local copies, waits for them, and re-layouts  5.44 us (5%)
    ppermute x27, waiting for transfers between devices, send(): return lax.ppermute(value, AXES, pairs(move))  48.9 us
    ppermute x27, starting transfers between devices, send(): return lax.ppermute(value, AXES, pairs(move))  26.2 us
    pallas_call x1, Pallas kernels, products(): pl.pallas_call(product_kernel, grid_spec=pltpu.PrefetchScalarGridSpec(num...  9.74 us
    all_to_all x1, starting transfers between devices, local(): units = lax.all_to_all(units, ('zh', 'zl', 'c'), 0, 0, tiled=True)  6.82 us
    pallas_call x1, Pallas kernels, partial_blocks(): pl.pallas_call(partial_kernel, grid_spec=pltpu.PrefetchScalarGridSpec(num...  6.44 us
    dynamic_slice x2, local copies, waits for them, and re-layouts, half(): return lax.dynamic_slice_in_dim(a, which * HALF, HALF, axis=1)  2.63 us
    all_to_all x1, waiting for transfers between devices, local(): units = lax.all_to_all(units, ('zh', 'zl', 'c'), 0, 0, tiled=True)  2.57 us
    pallas_call x1, Pallas kernels, quantize(): pl.pallas_call(quantize_kernel, grid=(D // width,), in_specs=[pl.BlockSpe...  2.46 us
  transfers between devices with their start and end apart: 28, of which 12 were waited for; matrix products, arithmetic and copies ran while one was open for 3% of the time, Pallas kernels for 19%

profile of v5, /device:TPU:31, one launch (start us, length us, event | category | flops | bytes accessed | tf_op | source)
XLA Modules:
  0.0 112.7 jit_solution(15855380078871968467)
XLA Ops:
  1.4 1.6 %constant_dynamic-slice_fusion.3 = (bf16[72,512]{1,0:T(8,128)(2,1)S(1)}, bf16[72,512]{1,0:T(8,128)(2,1)}) fusion(bf16[72,1024]{1,0:T(8,128)(2,1)} %param.4, s32[]{:T(128)S(6)} %select_n.54, s32[]{:T(128)S(6)} %select_n.55), kind=kLoop, calls=%fused_computation.20 | loop fusion | bytes 294920 | tf_op jit(solution)/shard_map/dynamic_slice | solution.py:331
  3.0 5.5 %collective-permute-start.3 = (bf16[72,512]{1,0:T(8,128)(2,1)}, bf16[72,512]{1,0:T(8,128)(2,1)S(1)}, u32[]{:S(2)}, u32[]{:S(2)}) collective-permute-start(bf16[72,512]{1,0:T(8,128)(2,1)} %get-tuple-element.82), channel_id=1, source_target_pairs={{0,195},{1,194},{2,193},{3,192},{4,199},{5,198},{6,197},{7,196},{8... | collective-permute-start | bytes 221192 | tf_op jit(solution)/shard_map/ppermute | solution.py:44
  8.9 1.1 constant_dynamic-slice_fusion
  10.5 1.7 %copy-done = bf16[256,4608]{1,0:T(8,128)(2,1)S(1)} copy-done((bf16[256,4608]{1,0:T(8,128)(2,1)S(1)}, bf16[256,4608]{1,0:T(8,128)(2,1)}, u32[]{:S(2)}) %copy-start) | copy-done | bytes 2359320
  12.1 2.5 %shard_map.58.mine_ref = bf16[4608,256]{1,0:T(8,128)(2,1)S(1)} custom-call(bf16[256,4608]{1,0:T(8,128)(2,1)S(1)} %copy-done), custom_call_target="tpu_custom_call" | custom-call | flops 1207959552 | bytes 4718592 | tf_op jit(solution)/shard_map/pallas_call | solution.py:111
  15.0 2.2 %collective-permute-start.6 = (bf16[288,512]{1,0:T(8,128)(2,1)S(1)}, bf16[288,512]{1,0:T(8,128)(2,1)S(1)}, u32[]{:S(2)}, u32[]{:S(2)}) collective-permute-start(bf16[288,512]{1,0:T(8,128)(2,1)S(1)} %bitcast.31), channel_id=1, source_target_pairs={{0,8},{1,33},{2,10},{3,35},{4,12},{5,37},{6,14},{7,39},{8,0},{9,41... | collective-permute-start | bytes 884744 | tf_op jit(solution)/shard_map/ppermute | solution.py:44
  17.2 6.4 %shard_map.59 = (bf16[4,288,512]{2,1,0:T(8,128)(2,1)S(1)}, bf16[4,288,512]{2,1,0:T(8,128)(2,1)S(1)}, bf16[4,288,512]{2,1,0:T(8,128)(2,1)S(1)}, bf16[4,288,512]{2,1,0:T(8,128)(2,1)S(1)}) custom-call(s32[4]{0:T(128)S(1)} %pad_add_fusion.at_ref, bf16[4608,256]{1,0:T(8,128)(2,1)S(1)} %shard_map.58.mine_ref, ...), custom_call_target="tpu_custom_call" | custom-call | flops 7247757312 | bytes 10485760 | tf_op jit(solution)/shard_map/pallas_call | solution.py:163
  23.7 1.9 %collective-permute-done.5 = bf16[288,512]{1,0:T(8,128)(2,1)S(1)} collective-permute-done((bf16[288,512]{1,0:T(8,128)(2,1)S(1)}, bf16[288,512]{1,0:T(8,128)(2,1)S(1)}, u32[]{:S(2)}, u32[]{:S(2)}) %collective-permute-start.5) | collective-permute-done | bytes 294944 | tf_op jit(solution)/shard_map/ppermute | solution.py:44
  25.7 1.1 collective-permute-start.9
  26.8 1.8 %collective-permute-start.14 = (bf16[2,288,512]{2,1,0:T(8,128)(2,1)S(1)}, bf16[2,288,512]{2,1,0:T(8,128)(2,1)S(1)}, u32[]{:S(2)}, u32[]{:S(2)}) collective-permute-start(bf16[2,288,512]{2,1,0:T(8,128)(2,1)S(1)} %maximum_select_fusion), channel_id=1, source_target_pairs={{0,16},{1,5},{2,18},{3,7},{4,20},{5,9},{6,22},{7,11},{8,24},{9,13}... | collective-permute-start | bytes 1769480 | tf_op jit(solution)/shard_map/ppermute | solution.py:44
  28.6 0.9 collective-permute-start.8
  30.1 6.3 %collective-permute-done.9 = bf16[2,288,512]{2,1,0:T(8,128)(2,1)S(1)} collective-permute-done((bf16[2,288,512]{2,1,0:T(8,128)(2,1)S(1)}, bf16[2,288,512]{2,1,0:T(8,128)(2,1)S(1)}, u32[]{:S(2)}, u32[]{:S(2)}) %collective-permute-start.9) | collective-permute-done | bytes 589856 | tf_op jit(solution)/shard_map/ppermute | solution.py:44
  36.4 1.2 %collective-permute-start.10 = (bf16[4,288,512]{2,1,0:T(8,128)(2,1)S(1)}, bf16[4,288,512]{2,1,0:T(8,128)(2,1)S(1)}, u32[]{:S(2)}, u32[]{:S(2)}) collective-permute-start(bf16[4,288,512]{2,1,0:T(8,128)(2,1)S(1)} %get-tuple-element.55), channel_id=1, source_target_pairs={{0,8},{1,33},{2,10},{3,35},{4,12},{5,37},{6,14},{7,39},{8,0},{9,41... | collective-permute-start | bytes 3538952 | tf_op jit(solution)/shard_map/ppermute | solution.py:44
  37.7 8.5 %collective-permute-done.14 = bf16[2,288,512]{2,1,0:T(8,128)(2,1)S(1)} collective-permute-done((bf16[2,288,512]{2,1,0:T(8,128)(2,1)S(1)}, bf16[2,288,512]{2,1,0:T(8,128)(2,1)S(1)}, u32[]{:S(2)}, u32[]{:S(2)}) %collective-permute-start.14) | collective-permute-done | bytes 589856 | tf_op jit(solution)/shard_map/ppermute | solution.py:44
  46.2 2.3 %collective-permute-done.13 = bf16[2,288,512]{2,1,0:T(8,128)(2,1)S(1)} collective-permute-done((bf16[2,288,512]{2,1,0:T(8,128)(2,1)S(1)}, bf16[2,288,512]{2,1,0:T(8,128)(2,1)S(1)}, u32[]{:S(2)}, u32[]{:S(2)}) %collective-permute-start.13) | collective-permute-done | bytes 589856 | tf_op jit(solution)/shard_map/ppermute | solution.py:44
  48.7 3.8 %collective-permute-start.15 = (bf16[3,288,512]{2,1,0:T(8,128)(2,1)S(1)}, bf16[3,288,512]{2,1,0:T(8,128)(2,1)}, u32[]{:S(2)}, u32[]{:S(2)}) collective-permute-start(bf16[3,288,512]{2,1,0:T(8,128)(2,1)S(1)} %pad_maximum_fusion.1.rest_1_), channel_id=1, source_target_pairs={{0,194},{1,195},{2,192},{3,193},{4,198},{5,199},{6,196},{7,197},{8... | collective-permute-start | bytes 2654216 | tf_op jit(solution)/shard_map/ppermute | solution.py:44
  52.7 3.0 %collective-permute-done.8.b = bf16[4,288,512]{2,1,0:T(8,128)(2,1)S(1)} collective-permute-done((bf16[4,288,512]{2,1,0:T(8,128)(2,1)S(1)}, bf16[4,288,512]{2,1,0:T(8,128)(2,1)S(1)}, u32[]{:S(2)}, u32[]{:S(2)}) %collective-permute-start.8) | collective-permute-done | bytes 1179680 | tf_op jit(solution)/shard_map/ppermute | solution.py:44
  55.7 15.5 %collective-permute-done.11.d = bf16[4,288,512]{2,1,0:T(8,128)(2,1)S(1)} collective-permute-done((bf16[4,288,512]{2,1,0:T(8,128)(2,1)S(1)}, bf16[4,288,512]{2,1,0:T(8,128)(2,1)S(1)}, u32[]{:S(2)}, u32[]{:S(2)}) %collective-permute-start.11) | collective-permute-done | bytes 1179680 | tf_op jit(solution)/shard_map/ppermute | solution.py:44
  71.2 1.7 %shard_map.60 = (f32[288,512]{1,0:T(8,128)S(1)}, bf16[288,512]{1,0:T(8,128)(2,1)S(1)}, bf16[288,512]{1,0:T(8,128)(2,1)S(1)}, bf16[288,512]{1,0:T(8,128)(2,1)S(1)}) custom-call(s32[4]{0:T(128)S(1)} %pad_add_fusion.at_ref, bf16[4,288,512]{2,1,0:T(8,128)(2,1)S(1)} %get-tuple-element.49.a, bf16[4,288,512]{2,1,0:T(8,128)(2,1)S(1)} %collective-permute-done.8.b, ...), custom_call_target="tpu_custom_call" | custom-call | bytes 6291456 | tf_op jit(solution)/shard_map/pallas_call | solution.py:193
  72.9 1.7 %collective-permute-start.12 = (bf16[288,512]{1,0:T(8,128)(2,1)S(1)}, bf16[288,512]{1,0:T(8,128)(2,1)S(1)}, u32[]{:S(2)}, u32[]{:S(2)}) collective-permute-start(bf16[288,512]{1,0:T(8,128)(2,1)S(1)} %get-tuple-element.58), channel_id=1, source_target_pairs={{0,32},{1,9},{2,34},{3,11},{4,36},{5,13},{6,38},{7,15},{8,40},{9,1... | collective-permute-start | bytes 884744 | tf_op jit(solution)/shard_map/ppermute | solution.py:44
  74.8 0.8 collective-permute-start.17
  76.3 3.8 %collective-permute-done.12.b = bf16[288,512]{1,0:T(8,128)(2,1)S(1)} collective-permute-done((bf16[288,512]{1,0:T(8,128)(2,1)S(1)}, bf16[288,512]{1,0:T(8,128)(2,1)S(1)}, u32[]{:S(2)}, u32[]{:S(2)}) %collective-permute-start.12) | collective-permute-done | bytes 294944 | tf_op jit(solution)/shard_map/ppermute | solution.py:44
  80.7 0.9 collective-permute-done.17.c
  81.6 1.6 %collective-permute-done.18.d = bf16[288,512]{1,0:T(8,128)(2,1)S(1)} collective-permute-done((bf16[288,512]{1,0:T(8,128)(2,1)S(1)}, bf16[288,512]{1,0:T(8,128)(2,1)S(1)}, u32[]{:S(2)}, u32[]{:S(2)}) %collective-permute-start.18) | collective-permute-done | bytes 294944 | tf_op jit(solution)/shard_map/ppermute | solution.py:44
  83.2 0.9 shard_map.61
  84.1 6.8 %all-to-all-start = ((bf16[16,72,128]{2,1,0:T(8,128)(2,1)}), bf16[16,72,128]{2,1,0:T(8,128)(2,1)S(1)}, u32[]{:S(2)}, u32[]{:S(2)}) async-start(bf16[16,72,128]{2,1,0:T(8,128)(2,1)} %shard_map.61), calls=%async_computation | async-start | bytes 589824 | tf_op jit(solution)/shard_map/all_to_all | solution.py:368
  91.0 9.7 %shard_map.62 = (bf16[256,1024]{1,0:T(8,128)(2,1)}, bf16[256,4608]{1,0:T(8,128)(2,1)}) custom-call(s32[4]{0:T(128)S(1)} %pad_add_fusion.at_ref, bf16[256,4608]{1,0:T(8,128)(2,1)} %x_ref.3, bf16[256,1024]{1,0:T(8,128)(2,1)} %g_ref.1, bf16[4,288,512]{2,1,0:T(8,128)(2,1)S(1)} %pad_maximum_fusion.rest_0_, bf16[3,288,512]{2,1,0:T(8,128)(2,1)S(1)} %pad_maximum_fusion.1.rest_1_, ...), custom_call_target="tpu_custom_call" | custom-call | flops 4831838208 | bytes 14680064 | tf_op jit(solution)/shard_map/pallas_call | solution.py:302
  100.7 2.6 %all-to-all-done = bf16[16,72,128]{2,1,0:T(8,128)(2,1)S(1)} async-done(((bf16[16,72,128]{2,1,0:T(8,128)(2,1)}), bf16[16,72,128]{2,1,0:T(8,128)(2,1)S(1)}, u32[]{:S(2)}, u32[]{:S(2)}) %all-to-all-start) | async-done | bytes 294944 | tf_op jit(solution)/shard_map/all_to_all | solution.py:368
  103.4 1.1 %collective-permute-start.25 = (f32[2,72,128]{2,1,0:T(8,128)S(1)}, f32[2,72,128]{2,1,0:T(8,128)S(1)}, u32[]{:S(2)}, u32[]{:S(2)}) collective-permute-start(f32[2,72,128]{2,1,0:T(8,128)S(1)} %convert_reduce_fusion), channel_id=1, source_target_pairs={{0,128},{1,129},{2,130},{3,131},{4,132},{5,133},{6,134},{7,135},{8... | collective-permute-start | bytes 221192 | tf_op jit(solution)/shard_map/ppermute | solution.py:44
  104.6 2.1 %collective-permute-start.24 = (f32[2,72,128]{2,1,0:T(8,128)S(1)}, f32[2,72,128]{2,1,0:T(8,128)S(1)}, u32[]{:S(2)}, u32[]{:S(2)}) collective-permute-start(f32[2,72,128]{2,1,0:T(8,128)S(1)} %convert_reduce_fusion), channel_id=1, source_target_pairs={{0,192},{1,193},{2,194},{3,195},{4,196},{5,197},{6,198},{7,199},{8... | collective-permute-start | bytes 221192 | tf_op jit(solution)/shard_map/ppermute | solution.py:44
  106.7 4.4 %collective-permute-done.24 = f32[2,72,128]{2,1,0:T(8,128)S(1)} collective-permute-done((f32[2,72,128]{2,1,0:T(8,128)S(1)}, f32[2,72,128]{2,1,0:T(8,128)S(1)}, u32[]{:S(2)}, u32[]{:S(2)}) %collective-permute-start.24) | collective-permute-done | bytes 73760 | tf_op jit(solution)/shard_map/ppermute | solution.py:44
  111.9 0.8 reshape.20
  (56 shorter events, 5.4 us)
Async XLA Ops:
  0.6 14.3 %collective-permute-start = (bf16[256,4608]{1,0:T(8,128)(2,1)}, bf16[256,4608]{1,0:T(8,128)(2,1)S(1)}, u32[]{:S(2)}, u32[]{:S(2)}) collective-permute-start(bf16[256,4608]{1,0:T(8,128)(2,1)} %x_ref.3), channel_id=1, source_target_pairs={{0,1},{1,0},{2,3},{3,2},{4,5},{5,4},{6,7},{7,6},{8,9},{9,8},{10,11... | collective-permute-start | bytes 7077896 | tf_op jit(solution)/shard_map/ppermute | solution.py:44
  3.0 11.8 %collective-permute-start.3 = (bf16[72,512]{1,0:T(8,128)(2,1)}, bf16[72,512]{1,0:T(8,128)(2,1)S(1)}, u32[]{:S(2)}, u32[]{:S(2)}) collective-permute-start(bf16[72,512]{1,0:T(8,128)(2,1)} %get-tuple-element.82), channel_id=1, source_target_pairs={{0,195},{1,194},{2,193},{3,192},{4,199},{5,198},{6,197},{7,196},{8... | collective-permute-start | bytes 221192 | tf_op jit(solution)/shard_map/ppermute | solution.py:44
  8.4 6.3 %collective-permute-start.1 = (bf16[72,512]{1,0:T(8,128)(2,1)}, bf16[72,512]{1,0:T(8,128)(2,1)S(1)}, u32[]{:S(2)}, u32[]{:S(2)}) collective-permute-start(bf16[72,512]{1,0:T(8,128)(2,1)} %get-tuple-element.82), channel_id=1, source_target_pairs={{0,1},{1,0},{2,3},{3,2},{4,5},{5,4},{6,7},{7,6},{8,9},{9,8},{10,11... | collective-permute-start | bytes 221192 | tf_op jit(solution)/shard_map/ppermute | solution.py:44
  8.9 5.8 %collective-permute-start.2 = (bf16[72,512]{1,0:T(8,128)(2,1)S(1)}, bf16[72,512]{1,0:T(8,128)(2,1)S(1)}, u32[]{:S(2)}, u32[]{:S(2)}) collective-permute-start(bf16[72,512]{1,0:T(8,128)(2,1)S(1)} %get-tuple-element.81), channel_id=1, source_target_pairs={{0,194},{1,195},{2,192},{3,193},{4,198},{5,199},{6,196},{7,197},{8... | collective-permute-start | bytes 221192 | tf_op jit(solution)/shard_map/ppermute | solution.py:44
  10.0 7.2 %collective-permute-start.4 = (bf16[256,512]{1,0:T(8,128)(2,1)S(1)}, bf16[256,512]{1,0:T(8,128)(2,1)S(1)}, u32[]{:S(2)}, u32[]{:S(2)}) collective-permute-start(bf16[256,512]{1,0:T(8,128)(2,1)S(1)} %get-tuple-element.79), channel_id=1, source_target_pairs={{0,1},{1,0},{2,3},{3,2},{4,5},{5,4},{6,7},{7,6},{8,9},{9,8},{10,11... | collective-permute-start | bytes 786440 | tf_op jit(solution)/shard_map/ppermute | solution.py:44
  10.5 1.7 %copy-start = (bf16[256,4608]{1,0:T(8,128)(2,1)S(1)}, bf16[256,4608]{1,0:T(8,128)(2,1)}, u32[]{:S(2)}) copy-start(bf16[256,4608]{1,0:T(8,128)(2,1)} %x_ref.3) | copy-start | bytes 7077892
  14.9 8.8 %collective-permute-start.7 = (bf16[288,512]{1,0:T(8,128)(2,1)S(1)}, bf16[288,512]{1,0:T(8,128)(2,1)S(1)}, u32[]{:S(2)}, u32[]{:S(2)}) collective-permute-start(bf16[288,512]{1,0:T(8,128)(2,1)S(1)} %bitcast.30), channel_id=1, source_target_pairs={{0,4},{1,17},{2,6},{3,19},{4,8},{5,21},{6,10},{7,23},{8,12},{9,25}... | collective-permute-start | bytes 884744 | tf_op jit(solution)/shard_map/ppermute | solution.py:44
  15.0 8.7 %collective-permute-start.6 = (bf16[288,512]{1,0:T(8,128)(2,1)S(1)}, bf16[288,512]{1,0:T(8,128)(2,1)S(1)}, u32[]{:S(2)}, u32[]{:S(2)}) collective-permute-start(bf16[288,512]{1,0:T(8,128)(2,1)S(1)} %bitcast.31), channel_id=1, source_target_pairs={{0,8},{1,33},{2,10},{3,35},{4,12},{5,37},{6,14},{7,39},{8,0},{9,41... | collective-permute-start | bytes 884744 | tf_op jit(solution)/shard_map/ppermute | solution.py:44
  17.2 8.4 %collective-permute-start.5 = (bf16[288,512]{1,0:T(8,128)(2,1)S(1)}, bf16[288,512]{1,0:T(8,128)(2,1)S(1)}, u32[]{:S(2)}, u32[]{:S(2)}) collective-permute-start(bf16[288,512]{1,0:T(8,128)(2,1)S(1)} %bitcast.32), channel_id=1, source_target_pairs={{0,12},{1,49},{2,14},{3,51},{4,0},{5,53},{6,2},{7,55},{8,4},{9,57}... | collective-permute-start | bytes 884744 | tf_op jit(solution)/shard_map/ppermute | solution.py:44
  25.7 10.7 %collective-permute-start.9 = (bf16[2,288,512]{2,1,0:T(8,128)(2,1)S(1)}, bf16[2,288,512]{2,1,0:T(8,128)(2,1)S(1)}, u32[]{:S(2)}, u32[]{:S(2)}) collective-permute-start(bf16[2,288,512]{2,1,0:T(8,128)(2,1)S(1)} %maximum_select_fusion), channel_id=1, source_target_pairs={{0,32},{1,9},{2,34},{3,11},{4,36},{5,13},{6,38},{7,15},{8,40},{9,1... | collective-permute-start | bytes 1769480 | tf_op jit(solution)/shard_map/ppermute | solution.py:44
  26.8 19.4 %collective-permute-start.14 = (bf16[2,288,512]{2,1,0:T(8,128)(2,1)S(1)}, bf16[2,288,512]{2,1,0:T(8,128)(2,1)S(1)}, u32[]{:S(2)}, u32[]{:S(2)}) collective-permute-start(bf16[2,288,512]{2,1,0:T(8,128)(2,1)S(1)} %maximum_select_fusion), channel_id=1, source_target_pairs={{0,16},{1,5},{2,18},{3,7},{4,20},{5,9},{6,22},{7,11},{8,24},{9,13}... | collective-permute-start | bytes 1769480 | tf_op jit(solution)/shard_map/ppermute | solution.py:44
  28.6 19.9 %collective-permute-start.13 = (bf16[2,288,512]{2,1,0:T(8,128)(2,1)S(1)}, bf16[2,288,512]{2,1,0:T(8,128)(2,1)S(1)}, u32[]{:S(2)}, u32[]{:S(2)}) collective-permute-start(bf16[2,288,512]{2,1,0:T(8,128)(2,1)S(1)} %maximum_select_fusion), channel_id=1, source_target_pairs={{0,48},{1,13},{2,50},{3,15},{4,52},{5,1},{6,54},{7,3},{8,56},{9,5}... | collective-permute-start | bytes 1769480 | tf_op jit(solution)/shard_map/ppermute | solution.py:44
  28.6 27.1 %collective-permute-start.8 = (bf16[4,288,512]{2,1,0:T(8,128)(2,1)S(1)}, bf16[4,288,512]{2,1,0:T(8,128)(2,1)S(1)}, u32[]{:S(2)}, u32[]{:S(2)}) collective-permute-start(bf16[4,288,512]{2,1,0:T(8,128)(2,1)S(1)} %get-tuple-element.50), channel_id=1, source_target_pairs={{0,4},{1,17},{2,6},{3,19},{4,8},{5,21},{6,10},{7,23},{8,12},{9,25}... | collective-permute-start | bytes 3538952 | tf_op jit(solution)/shard_map/ppermute | solution.py:44
  29.5 41.6 %collective-permute-start.11 = (bf16[4,288,512]{2,1,0:T(8,128)(2,1)S(1)}, bf16[4,288,512]{2,1,0:T(8,128)(2,1)S(1)}, u32[]{:S(2)}, u32[]{:S(2)}) collective-permute-start(bf16[4,288,512]{2,1,0:T(8,128)(2,1)S(1)} %get-tuple-element.56), channel_id=1, source_target_pairs={{0,12},{1,49},{2,14},{3,51},{4,0},{5,53},{6,2},{7,55},{8,4},{9,57}... | collective-permute-start | bytes 3538952 | tf_op jit(solution)/shard_map/ppermute | solution.py:44
  36.4 34.8 %collective-permute-start.10 = (bf16[4,288,512]{2,1,0:T(8,128)(2,1)S(1)}, bf16[4,288,512]{2,1,0:T(8,128)(2,1)S(1)}, u32[]{:S(2)}, u32[]{:S(2)}) collective-permute-start(bf16[4,288,512]{2,1,0:T(8,128)(2,1)S(1)} %get-tuple-element.55), channel_id=1, source_target_pairs={{0,8},{1,33},{2,10},{3,35},{4,12},{5,37},{6,14},{7,39},{8,0},{9,41... | collective-permute-start | bytes 3538952 | tf_op jit(solution)/shard_map/ppermute | solution.py:44
  48.7 27.7 %collective-permute-start.15 = (bf16[3,288,512]{2,1,0:T(8,128)(2,1)S(1)}, bf16[3,288,512]{2,1,0:T(8,128)(2,1)}, u32[]{:S(2)}, u32[]{:S(2)}) collective-permute-start(bf16[3,288,512]{2,1,0:T(8,128)(2,1)S(1)} %pad_maximum_fusion.1.rest_1_), channel_id=1, source_target_pairs={{0,194},{1,195},{2,192},{3,193},{4,198},{5,199},{6,196},{7,197},{8... | collective-permute-start | bytes 2654216 | tf_op jit(solution)/shard_map/ppermute | solution.py:44
  52.6 23.7 %collective-permute-start.16 = (bf16[3,288,512]{2,1,0:T(8,128)(2,1)S(1)}, bf16[3,288,512]{2,1,0:T(8,128)(2,1)}, u32[]{:S(2)}, u32[]{:S(2)}) collective-permute-start(bf16[3,288,512]{2,1,0:T(8,128)(2,1)S(1)} %pad_maximum_fusion.2.rest_2_), channel_id=1, source_target_pairs={{0,64},{1,65},{2,66},{3,67},{4,68},{5,69},{6,70},{7,71},{8,72},{9,... | collective-permute-start | bytes 2654216 | tf_op jit(solution)/shard_map/ppermute | solution.py:44
  72.9 7.3 %collective-permute-start.12 = (bf16[288,512]{1,0:T(8,128)(2,1)S(1)}, bf16[288,512]{1,0:T(8,128)(2,1)S(1)}, u32[]{:S(2)}, u32[]{:S(2)}) collective-permute-start(bf16[288,512]{1,0:T(8,128)(2,1)S(1)} %get-tuple-element.58), channel_id=1, source_target_pairs={{0,32},{1,9},{2,34},{3,11},{4,36},{5,13},{6,38},{7,15},{8,40},{9,1... | collective-permute-start | bytes 884744 | tf_op jit(solution)/shard_map/ppermute | solution.py:44
  74.8 6.8 %collective-permute-start.17 = (bf16[288,512]{1,0:T(8,128)(2,1)S(1)}, bf16[288,512]{1,0:T(8,128)(2,1)S(1)}, u32[]{:S(2)}, u32[]{:S(2)}) collective-permute-start(bf16[288,512]{1,0:T(8,128)(2,1)S(1)} %get-tuple-element.61), channel_id=1, source_target_pairs={{0,16},{1,5},{2,18},{3,7},{4,20},{5,9},{6,22},{7,11},{8,24},{9,13}... | collective-permute-start | bytes 884744 | tf_op jit(solution)/shard_map/ppermute | solution.py:44
  75.6 7.6 %collective-permute-start.18 = (bf16[288,512]{1,0:T(8,128)(2,1)S(1)}, bf16[288,512]{1,0:T(8,128)(2,1)S(1)}, u32[]{:S(2)}, u32[]{:S(2)}) collective-permute-start(bf16[288,512]{1,0:T(8,128)(2,1)S(1)} %get-tuple-element.62), channel_id=1, source_target_pairs={{0,48},{1,13},{2,50},{3,15},{4,52},{5,1},{6,54},{7,3},{8,56},{9,5}... | collective-permute-start | bytes 884744 | tf_op jit(solution)/shard_map/ppermute | solution.py:44
  80.2 10.8 %collective-permute-start.19 = (bf16[4,288,512]{2,1,0:T(8,128)(2,1)S(1)}, bf16[4,288,512]{2,1,0:T(8,128)(2,1)}, u32[]{:S(2)}, u32[]{:S(2)}) collective-permute-start(bf16[4,288,512]{2,1,0:T(8,128)(2,1)S(1)} %pad_maximum_fusion.rest_0_), channel_id=1, source_target_pairs={{0,1},{1,0},{2,3},{3,2},{4,5},{5,4},{6,7},{7,6},{8,9},{9,8},{10,11... | collective-permute-start | bytes 3538952 | tf_op jit(solution)/shard_map/ppermute | solution.py:44
  80.2 10.8 %collective-permute-start.20 = (bf16[3,288,512]{2,1,0:T(8,128)(2,1)S(1)}, bf16[3,288,512]{2,1,0:T(8,128)(2,1)}, u32[]{:S(2)}, u32[]{:S(2)}) collective-permute-start(bf16[3,288,512]{2,1,0:T(8,128)(2,1)S(1)} %pad_maximum_fusion.1.rest_1_), channel_id=1, source_target_pairs={{0,1},{1,0},{2,3},{3,2},{4,5},{5,4},{6,7},{7,6},{8,9},{9,8},{10,11... | collective-permute-start | bytes 2654216 | tf_op jit(solution)/shard_map/ppermute | solution.py:44
  80.7 10.3 %collective-permute-start.21 = (bf16[3,288,512]{2,1,0:T(8,128)(2,1)S(1)}, bf16[3,288,512]{2,1,0:T(8,128)(2,1)}, u32[]{:S(2)}, u32[]{:S(2)}) collective-permute-start(bf16[3,288,512]{2,1,0:T(8,128)(2,1)S(1)} %pad_maximum_fusion.2.rest_2_), channel_id=1, source_target_pairs={{0,1},{1,0},{2,3},{3,2},{4,5},{5,4},{6,7},{7,6},{8,9},{9,8},{10,11... | collective-permute-start | bytes 2654216 | tf_op jit(solution)/shard_map/ppermute | solution.py:44
  81.6 9.4 %collective-permute-start.22 = (bf16[3,288,512]{2,1,0:T(8,128)(2,1)}, bf16[3,288,512]{2,1,0:T(8,128)(2,1)}, u32[]{:S(2)}, u32[]{:S(2)}) collective-permute-start(bf16[3,288,512]{2,1,0:T(8,128)(2,1)} %collective-permute-done.15.rest_3_), channel_id=1, source_target_pairs={{0,1},{1,0},{2,3},{3,2},{4,5},{5,4},{6,7},{7,6},{8,9},{9,8},{10,11... | collective-permute-start | bytes 2654216 | tf_op jit(solution)/shard_map/ppermute | solution.py:44
  83.2 7.7 %collective-permute-start.23 = (bf16[3,288,512]{2,1,0:T(8,128)(2,1)}, bf16[3,288,512]{2,1,0:T(8,128)(2,1)}, u32[]{:S(2)}, u32[]{:S(2)}) collective-permute-start(bf16[3,288,512]{2,1,0:T(8,128)(2,1)} %collective-permute-done.16.rest_4_), channel_id=1, source_target_pairs={{0,1},{1,0},{2,3},{3,2},{4,5},{5,4},{6,7},{7,6},{8,9},{9,8},{10,11... | collective-permute-start | bytes 2654216 | tf_op jit(solution)/shard_map/ppermute | solution.py:44
  84.1 19.2 %all-to-all-start = ((bf16[16,72,128]{2,1,0:T(8,128)(2,1)}), bf16[16,72,128]{2,1,0:T(8,128)(2,1)S(1)}, u32[]{:S(2)}, u32[]{:S(2)}) async-start(bf16[16,72,128]{2,1,0:T(8,128)(2,1)} %shard_map.61), calls=%async_computation | async-start | bytes 589824 | tf_op jit(solution)/shard_map/all_to_all | solution.py:368
  103.3 8.3 %collective-permute-start.26 = (f32[2,72,128]{2,1,0:T(8,128)S(1)}, f32[2,72,128]{2,1,0:T(8,128)S(1)}, u32[]{:S(2)}, u32[]{:S(2)}) collective-permute-start(f32[2,72,128]{2,1,0:T(8,128)S(1)} %convert_reduce_fusion), channel_id=1, source_target_pairs={{0,64},{1,65},{2,66},{3,67},{4,68},{5,69},{6,70},{7,71},{8,72},{9,... | collective-permute-start | bytes 221192 | tf_op jit(solution)/shard_map/ppermute | solution.py:44
  103.4 8.2 %collective-permute-start.25 = (f32[2,72,128]{2,1,0:T(8,128)S(1)}, f32[2,72,128]{2,1,0:T(8,128)S(1)}, u32[]{:S(2)}, u32[]{:S(2)}) collective-permute-start(f32[2,72,128]{2,1,0:T(8,128)S(1)} %convert_reduce_fusion), channel_id=1, source_target_pairs={{0,128},{1,129},{2,130},{3,131},{4,132},{5,133},{6,134},{7,135},{8... | collective-permute-start | bytes 221192 | tf_op jit(solution)/shard_map/ppermute | solution.py:44
  104.6 6.5 %collective-permute-start.24 = (f32[2,72,128]{2,1,0:T(8,128)S(1)}, f32[2,72,128]{2,1,0:T(8,128)S(1)}, u32[]{:S(2)}, u32[]{:S(2)}) collective-permute-start(f32[2,72,128]{2,1,0:T(8,128)S(1)} %convert_reduce_fusion), channel_id=1, source_target_pairs={{0,192},{1,193},{2,194},{3,195},{4,196},{5,197},{6,198},{7,199},{8... | collective-permute-start | bytes 221192 | tf_op jit(solution)/shard_map/ppermute | solution.py:44
